TPU v7x, 256 devices: a whole 4x4x8 slice. The times are simulated.
256 devices in a mesh: space: 128 (over y, x, z), chan: 2 (over core).
Axes of the slice: x: 4, y: 4, z: 8, core: 2. Of those that a mesh axis runs over, the one named last changes fastest.
Arguments:
- feats: bfloat16 [1024, 64, 512], P('space', 'chan'), may hold values from -6 to 6
- live_count: int32 [128], P('space'), may hold values from 1 to 8, 640 in all
- neighbours: int32 [1024, 26], P('space'), may hold values from 0 to 1024, as said below
- parent: int32 [1024], P('space'), may hold values from 0 to 1023, as said below
- fine_weight: bfloat16 [27, 64, 64], P(None, 'chan'), may hold values from -0.15625 to 0.15625
- coarse_weight: bfloat16 [27, 128, 64], P(None, 'chan'), may hold values from -0.15625 to 0.15625
- project_weight: bfloat16 [64, 128], P(None, 'chan'), may hold values from -0.5 to 0.5
- cotangent: bfloat16 [1024, 64, 512], P('space', 'chan'), may hold values from -6 to 6
Outputs:
- out_feats: bfloat16 [1024, 64, 512], P('space', 'chan')
- grad_feats: bfloat16 [1024, 64, 512], P('space', 'chan')
- fine_weight_grad: float32 [27, 64, 64], P(None, 'chan')
- coarse_weight_grad: float32 [27, 128, 64], P(None, 'chan')
- project_weight_grad: float32 [64, 128], P(None, 'chan')
Inputs may be any that keep to these rules, and one draw needn't show every extreme that they name: `live_count`: some index of space has all 8 slots occupied. Entry [b, t] is the brick beside brick b in direction t, or 1024 where there is none. A brick's neighbours belong to its own index of space or to the indices just before and after it. The lists are symmetric: if entry [b, t] is b2 < 1024, entry [b2, 25 - t] is b. Every value occurs once; coarse brick j belongs to index j // 1 of space. A brick's parent lies on its own index of space or on the index just before or after it. Between two neighbouring indices, as many bricks of the lower have parents on the upper as the reverse, from 1 to 1; some pair of neighbouring indices has exactly 1.
All inputs are finite; a program needn't handle non-finite values. No bound on the sum of `live_count` on one device may be relied on, other than what follows from the above.
Results may differ from a plain program's by a relative error of at most 0.012.
Values may be sent and summed in bfloat16 or wider, within the bound.
A program may use at most 320 MiB of HBM per device.

v0:
```python
import math

import jax
import jax.numpy as jnp
import numpy as np
from jax import lax
from jax.experimental import pallas as pl
from jax.experimental.pallas import tpu as pltpu
from jax.sharding import PartitionSpec as P


def extended(block, sides, width):
    for axis, dim in sides:
        count = lax.axis_size(axis)
        forward = [(i, i + 1) for i in range(count - 1)]
        backward = [(target, source) for source, target in forward]
        low = lax.ppermute(
            lax.slice_in_dim(block, block.shape[dim] - width, None, axis=dim), axis, forward
        )
        high = lax.ppermute(lax.slice_in_dim(block, 0, width, axis=dim), axis, backward)
        block = jnp.concatenate([low, block, high], axis=dim)
    return block


def lean_list():
    leans = []
    for lean_x in (-1, 0, 1):
        for lean_y in (-1, 0, 1):
            for lean_z in (-1, 0, 1):
                leans.append((lean_x, lean_y, lean_z))
    return leans


def pool_table():
    voxel = np.arange(512)
    octant_voxel = 16 * (voxel // 128) + 4 * (voxel // 16 % 4) + voxel % 8 // 2
    return (octant_voxel[:, None] == np.arange(64)[None, :]).astype(np.float32)


def octant_table():
    voxel = np.arange(512)
    coord_x = voxel // 64
    coord_y = voxel // 8 % 8
    coord_z = voxel % 8
    octant = 4 * (coord_x // 4) + 2 * (coord_y // 4) + coord_z // 4
    inner = 16 * (coord_x % 4) + 4 * (coord_y % 4) + coord_z % 4
    table = np.zeros((8, 64, 512), np.float32)
    table[octant, inner, voxel] = 1.0
    return table


def flip_weight(weight):
    return jnp.transpose(weight[::-1], (0, 2, 1))


def pool_sum(field_in):
    table = jnp.asarray(pool_table()).astype(jnp.bfloat16)
    return jnp.einsum("bcv,vu->bcu", field_in, table, preferred_element_type=jnp.float32)


def enlarge(octants):
    table = jnp.asarray(pool_table()).astype(jnp.bfloat16)
    return jnp.einsum("bcu,vu->bcv", octants, table, preferred_element_type=jnp.float32)


def place_octants(octants):
    amount, channels = (octants.shape[0] // 8, octants.shape[1])
    grouped = octants.reshape(amount, 8, channels, 64)
    table = jnp.asarray(octant_table()).astype(jnp.bfloat16)
    return jnp.einsum("jocu,ouv->jcv", grouped, table, preferred_element_type=jnp.float32).astype(
        jnp.bfloat16
    )


def split_octants(coarse):
    amount, channels = (coarse.shape[0], coarse.shape[1])
    table = jnp.asarray(octant_table()).astype(jnp.bfloat16)
    parts = jnp.einsum("jcv,ouv->jocu", coarse, table, preferred_element_type=jnp.float32).astype(
        jnp.bfloat16
    )
    return parts.reshape(amount * 8, channels, 64)


def select_rows(picker, values):
    return jnp.dot(picker, values, preferred_element_type=jnp.float32).astype(jnp.bfloat16)


def route_places(slot_list, dev_index, moving, bricks):
    direction = slot_list // bricks - dev_index
    to_left = (direction == -1).astype(jnp.int32)
    to_right = (direction == 1).astype(jnp.int32)
    left_rank = jnp.cumsum(to_left) - to_left
    right_rank = jnp.cumsum(to_right) - to_right
    return jnp.where(
        to_left == 1, left_rank, jnp.where(to_right == 1, moving + right_rank, 2 * moving)
    ).astype(jnp.int32)


def both_sides(widened, moving):
    return jnp.concatenate([widened[:moving], widened[3 * moving :]], axis=0)


def gather_back(local_part, send_pick, returned):
    total = local_part.astype(jnp.float32) + jnp.dot(
        send_pick.T, returned, preferred_element_type=jnp.float32
    )
    return total.astype(jnp.bfloat16)


SPANS = {-1: (slice(0, 1), slice(7, 8)), 0: (slice(1, 9), slice(0, 8)), 1: (slice(9, 10), slice(0, 1))}
KZ_ORDER = np.array([1, 0, 2])


def brick_kernel(with_conv, with_grad, masked, *refs):
    refs = list(refs)
    near_ref, live_ref, table_ref = refs[:3]
    del refs[:3]
    weight_ref = refs.pop(0) if with_conv else None
    grad_ref = refs.pop(0) if with_grad else None
    out_ref = refs.pop(0) if with_conv else None
    total_ref = refs.pop(0) if with_grad else None
    padded, columns = refs
    brick = pl.program_id(0)
    for index, (lean_x, lean_y, lean_z) in enumerate(lean_list()):
        slot = near_ref[brick, index]
        to_x, from_x = SPANS[lean_x]
        to_y, from_y = SPANS[lean_y]
        padded[lean_z + 1, to_x, to_y] = table_ref[slot, from_x, from_y]
    shape = (10, 8, 8, 128)
    place_z = lax.broadcasted_iota(jnp.int32, shape, 2)
    low_half = lax.broadcasted_iota(jnp.int32, shape, 3) < 64
    for tap_y in range(3):
        below = padded[0, :, tap_y : tap_y + 8]
        level = padded[1, :, tap_y : tap_y + 8]
        above = padded[2, :, tap_y : tap_y + 8]
        minus = pltpu.roll(jnp.where(place_z == 7, below, level), 1, 2)
        plus = pltpu.roll(jnp.where(place_z == 0, above, level), 7, 2)
        first = jnp.where(low_half, level, minus).reshape(640, 128)
        second = jnp.where(low_half, plus, 0.0).reshape(640, 128)
        start = 256 * tap_y
        columns[:, start : start + 128] = first.astype(jnp.bfloat16)
        columns[:, start + 128 : start + 256] = second.astype(jnp.bfloat16)
    if with_conv:
        total = None
        for tap_x in range(3):
            part = lax.dot_general(
                weight_ref[tap_x],
                columns[64 * tap_x : 64 * tap_x + 512, :],
                (((1,), (1,)), ((), ())),
                preferred_element_type=jnp.float32,
            )
            total = part if total is None else total + part
        if masked:
            total = jnp.where(brick < live_ref[0], total, 0.0)
        out_ref[0] = total.astype(out_ref.dtype)
    if with_grad:

        @pl.when(brick == 0)
        def clear():
            total_ref[...] = jnp.zeros_like(total_ref)

        for tap_x in range(3):
            total_ref[tap_x] += jnp.dot(
                grad_ref[0],
                columns[64 * tap_x : 64 * tap_x + 512, :],
                preferred_element_type=jnp.float32,
            )


def brick_pass(field_in, near, live_count, weight, grad_rows, out_dtype, masked):
    amount = near.shape[0]
    slots, channels = field_in.shape[:2]
    rows = weight.shape[1] if weight is not None else grad_rows.shape[1]
    table = jnp.transpose(field_in, (0, 2, 1)).astype(jnp.float32)
    table = jnp.concatenate([table, table], axis=2)
    table = jnp.concatenate([table, jnp.zeros((1, 512, 128), jnp.float32)], axis=0)
    table = table.reshape(slots + 1, 8, 8, 8, 128)
    operands = [near, live_count, table]
    in_specs = [
        pl.BlockSpec(memory_space=pltpu.SMEM),
        pl.BlockSpec(memory_space=pltpu.SMEM),
        pl.BlockSpec((slots + 1, 8, 8, 8, 128), lambda b: (0, 0, 0, 0, 0)),
    ]
    outs, out_specs = [], []
    if weight is not None:
        operands.append(weight_blocks(weight))
        in_specs.append(pl.BlockSpec((3, rows, 768), lambda b: (0, 0, 0)))
        outs.append(jax.ShapeDtypeStruct((amount, rows, 512), out_dtype))
        out_specs.append(pl.BlockSpec((1, rows, 512), lambda b: (b, 0, 0)))
    if grad_rows is not None:
        operands.append(grad_rows)
        in_specs.append(pl.BlockSpec((1, rows, 512), lambda b: (b, 0, 0)))
        outs.append(jax.ShapeDtypeStruct((3, rows, 768), jnp.float32))
        out_specs.append(pl.BlockSpec((3, rows, 768), lambda b: (0, 0, 0)))
    products = (weight is not None) + (grad_rows is not None)
    return pl.pallas_call(
        lambda *refs: brick_kernel(weight is not None, grad_rows is not None, masked, *refs),
        grid=(amount,),
        in_specs=in_specs,
        out_specs=out_specs,
        out_shape=outs,
        scratch_shapes=[
            pltpu.VMEM((3, 10, 10, 8, 128), jnp.float32),
            pltpu.VMEM((640, 768), jnp.bfloat16),
        ],
        compiler_params=pltpu.CompilerParams(vmem_limit_bytes=48 * 1024 * 1024),
        cost_estimate=pl.CostEstimate(
            flops=amount * products * 2 * rows * 2304 * 512,
            bytes_accessed=(slots + 1) * 512 * 128 * 4,
            transcendentals=0,
        ),
    )(*operands)


def weight_blocks(weight):
    rows, channels = weight.shape[1:]
    taps = weight.reshape(9, 3, rows, channels)[:, KZ_ORDER]
    taps = jnp.concatenate([taps, jnp.zeros_like(taps[:, :1])], axis=1)
    taps = taps.reshape(3, 3, 4, rows, channels)
    return jnp.transpose(taps, (0, 3, 1, 2, 4)).reshape(3, rows, 768)


def grad_taps(total):
    rows = total.shape[1]
    taps = total.reshape(3, rows, 3, 4, 64)
    taps = jnp.transpose(taps, (0, 2, 3, 1, 4)).reshape(9, 4, rows, 64)[:, KZ_ORDER]
    return taps.reshape(27, rows, 64)


def around(block):
    count = lax.axis_size("space")
    forward = [(i, i + 1) for i in range(count - 1)]
    backward = [(i + 1, i) for i in range(count - 1)]
    low = lax.ppermute(block, "space", forward)
    high = lax.ppermute(block, "space", backward)
    return jnp.concatenate([low, block, high], axis=0)


def sum_over_space(parts):
    sizes = [math.prod(part.shape) for part in parts]
    count = lax.axis_size("space")
    me = lax.axis_index("space")
    flat = jnp.concatenate([part.reshape(-1) for part in parts])
    unit = 1024 * count
    length = -(-sum(sizes) // unit) * unit
    flat = jnp.pad(flat, (0, length - sum(sizes))).reshape(-1, 128)
    strides = [1 << bit for bit in range(count.bit_length() - 1)][::-1]
    for stride in strides:
        upper = me // stride % 2 == 1
        half = flat.shape[0] // 2
        low, high = flat[:half], flat[half:]
        pairs = [(i, i ^ stride) for i in range(count)]
        arrived = lax.ppermute(jnp.where(upper, low, high), "space", pairs)
        flat = jnp.where(upper, high, low) + arrived
    for stride in strides[::-1]:
        upper = me // stride % 2 == 1
        pairs = [(i, i ^ stride) for i in range(count)]
        arrived = lax.ppermute(flat, "space", pairs)
        flat = jnp.where(
            upper, jnp.concatenate([arrived, flat]), jnp.concatenate([flat, arrived])
        )
    flat = flat.reshape(-1)
    totals, start = [], 0
    for part, size in zip(parts, sizes):
        totals.append(flat[start : start + size].reshape(part.shape))
        start += size
    return totals


def per_device(
    feats, live_count, neighbours, parent, fine_weight, coarse_weight, project_weight, cotangent
):
    bricks = feats.shape[0]
    half_channels = feats.shape[1]
    devices = lax.axis_size("space")
    own_index = lax.axis_index("space")
    moving = max(1, bricks // 8)
    coarse_bricks = bricks // 8
    live_mask = (jnp.arange(bricks, dtype=jnp.int32) < live_count[0]).astype(jnp.float32)[
        :, None, None
    ]
    near_parent = extended(parent, (("space", 0),), bricks)
    left_list = near_parent[:bricks]
    right_list = near_parent[2 * bricks :]
    send_place = route_places(parent, own_index, moving, bricks)
    left_place = route_places(left_list, own_index - 1, moving, bricks)
    right_place = route_places(right_list, own_index + 1, moving, bricks)
    local_ok = parent // bricks == own_index
    left_ok = (own_index > 0) & (left_place >= moving) & (left_place < 2 * moving)
    right_ok = (own_index < devices - 1) & (right_place < moving)
    dest_rows = jnp.concatenate([parent % bricks, left_list % bricks, right_list % bricks])
    source_cols = jnp.concatenate(
        [
            jnp.arange(bricks, dtype=jnp.int32),
            bricks + left_place - moving,
            bricks + moving + right_place,
        ]
    )
    valid = jnp.concatenate([local_ok, left_ok, right_ok])
    dest_rows = jnp.where(valid, dest_rows, 0)
    source_cols = jnp.where(valid, source_cols, 0)
    receive_pick = (
        jnp.zeros((bricks, bricks + 2 * moving), jnp.float32)
        .at[dest_rows, source_cols]
        .add(valid.astype(jnp.float32))
        .astype(jnp.bfloat16)
    )
    send_pick = (jnp.arange(2 * moving, dtype=jnp.int32)[:, None] == send_place[None, :]).astype(
        jnp.bfloat16
    )
    pooled = (pool_sum(feats) * 0.125 * live_mask).astype(jnp.bfloat16).reshape(bricks, -1)
    outgoing = select_rows(send_pick, pooled)
    widened = extended(outgoing, (("space", 0),), moving)
    arrived = select_rows(
        receive_pick, jnp.concatenate([pooled, both_sides(widened, moving)], axis=0)
    )
    coarse_half = place_octants(arrived.reshape(bricks, half_channels, 64))
    coarse_in = lax.all_gather(coarse_half, "chan", axis=1, tiled=True)
    lone = jnp.asarray(
        np.array([[0 if lean == (0, 0, 0) else coarse_bricks for lean in lean_list()]] * 1)
    ).astype(jnp.int32)
    lone = jnp.where(
        lone == coarse_bricks, lone, jnp.arange(coarse_bricks, dtype=jnp.int32)[:, None]
    )
    preactivation = brick_pass(
        coarse_in, lone, live_count, coarse_weight, None, jnp.float32, False
    )[0]
    hidden = jax.nn.silu(preactivation).astype(jnp.bfloat16)
    out_terms = jnp.einsum(
        "cj,bjv->bcv", project_weight, hidden, preferred_element_type=jnp.float32
    )
    coarse_out = lax.psum_scatter(out_terms, "chan", scatter_dimension=1, tiled=True).astype(
        jnp.bfloat16
    )
    back_source = select_rows(receive_pick.T, split_octants(coarse_out).reshape(bricks, -1))
    widened_back = extended(back_source[bricks:], (("space", 0),), moving)
    up_octants = gather_back(
        back_source[:bricks], send_pick, both_sides(widened_back, moving)
    ).reshape(bricks, half_channels, 64)
    mixed_feats = ((feats.astype(jnp.float32) + enlarge(up_octants)) * live_mask).astype(
        jnp.bfloat16
    )
    last_brick = devices * bricks
    near_local = jnp.where(
        neighbours >= last_brick, 3 * bricks, neighbours - (own_index - 1) * bricks
    ).astype(jnp.int32)
    slots = jnp.arange(bricks, dtype=jnp.int32)[:, None] + bricks
    near = jnp.concatenate([near_local[:, :13], slots, near_local[:, 13:]], axis=1)
    grad_rows = (cotangent.astype(jnp.float32) * live_mask).astype(jnp.bfloat16)
    grad_table = lax.all_gather(around(grad_rows), "chan", axis=1, tiled=True)
    whole_weight = lax.all_gather(fine_weight, "chan", axis=1, tiled=True)
    own_weight = lax.dynamic_slice_in_dim(
        whole_weight, lax.axis_index("chan") * half_channels, half_channels, 2
    )
    back_feats = brick_pass(
        grad_table, near, live_count, flip_weight(own_weight), None, jnp.bfloat16, True
    )[0]
    feat_table = lax.all_gather(around(mixed_feats), "chan", axis=1, tiled=True)
    out_feats, fine_total = brick_pass(
        feat_table, near, live_count, fine_weight, grad_rows, jnp.bfloat16, True
    )
    up_grad = pool_sum(back_feats).astype(jnp.bfloat16).reshape(bricks, -1)
    outgoing_grad = select_rows(send_pick, up_grad)
    widened_grad = extended(outgoing_grad, (("space", 0),), moving)
    arrived_grad = select_rows(
        receive_pick, jnp.concatenate([up_grad, both_sides(widened_grad, moving)], axis=0)
    )
    coarse_grad_half = place_octants(arrived_grad.reshape(bricks, half_channels, 64))
    coarse_grad = lax.all_gather(coarse_grad_half, "chan", axis=1, tiled=True)
    project_matrix = jnp.einsum(
        "bcv,bjv->cj", coarse_grad, hidden, preferred_element_type=jnp.float32
    )
    hidden_grad = jnp.einsum(
        "cj,bcv->bjv", project_weight, coarse_grad, preferred_element_type=jnp.float32
    )
    sigmoid_pre = jax.nn.sigmoid(preactivation)
    pre_grad = (hidden_grad * sigmoid_pre * (1.0 + preactivation * (1.0 - sigmoid_pre))).astype(
        jnp.bfloat16
    )
    coarse_total = brick_pass(
        coarse_in, lone, live_count, None, pre_grad, None, False
    )[0]
    coarse_terms = brick_pass(
        pre_grad, lone, live_count, flip_weight(coarse_weight), None, jnp.float32, False
    )[0]
    coarse_back = lax.psum_scatter(
        coarse_terms.astype(jnp.bfloat16), "chan", scatter_dimension=1, tiled=True
    )
    down_source = select_rows(receive_pick.T, split_octants(coarse_back).reshape(bricks, -1))
    widened_down = extended(down_source[bricks:], (("space", 0),), moving)
    down_grad = gather_back(
        down_source[:bricks], send_pick, both_sides(widened_down, moving)
    ).reshape(bricks, half_channels, 64)
    grad_feats = (back_feats.astype(jnp.float32) + live_mask * enlarge(down_grad) * 0.125).astype(
        jnp.bfloat16
    )
    fine_sum, coarse_sum, project_total = sum_over_space(
        (grad_taps(fine_total), grad_taps(coarse_total), project_matrix)
    )
    fine_scale = 1.0 / math.sqrt(512.0 * bricks * devices)
    coarse_scale = 1.0 / math.sqrt(512.0 * coarse_bricks * devices)
    fine_weight_grad = fine_sum * fine_scale
    coarse_weight_grad = coarse_sum * coarse_scale
    project_weight_grad = project_total * coarse_scale
    return (out_feats, grad_feats, fine_weight_grad, coarse_weight_grad, project_weight_grad)


def solution(mesh):
    placed = (
        P("space", "chan", None),
        P("space"),
        P("space", None),
        P("space"),
        P(None, "chan", None),
        P(None, "chan", None),
        P(None, "chan"),
        P("space", "chan", None),
    )
    return jax.shard_map(
        per_device,
        mesh=mesh,
        in_specs=placed,
        out_specs=(
            P("space", "chan", None),
            P("space", "chan", None),
            P(None, "chan", None),
            P(None, "chan", None),
            P(None, "chan"),
        ),
        check_vma=False,
    )
```

profile of v0, /device:TPU:8, one launch (start us, length us, event | category | flops | bytes accessed | tf_op | source)
XLA Modules:
  0.0 287.5 jit_solution(6890010541288733925)
XLA Ops:
  7.2 4.0 %collective-permute-start = (s32[8]{0:T(128)}, s32[8]{0:T(128)S(1)}, u32[]{:S(2)}, u32[]{:S(2)}) collective-permute-start(s32[8]{0:T(128)} %param.27), channel_id=1, source_target_pairs={{0,2},{2,4},{4,6},{6,8},{8,10},{10,12},{12,14},{14,16},{16,18},{18... | collective-permute-start | bytes 104 | tf_op jit(solution)/shard_map/ppermute | solution.py:17
  11.2 7.9 %collective-permute-start.1 = (s32[8]{0:T(128)}, s32[8]{0:T(128)S(1)}, u32[]{:S(2)}, u32[]{:S(2)}) collective-permute-start(s32[8]{0:T(128)} %param.27), channel_id=1, source_target_pairs={{2,0},{4,2},{6,4},{8,6},{10,8},{12,10},{14,12},{16,14},{18,16},{20... | collective-permute-start | bytes 104 | tf_op jit(solution)/shard_map/ppermute | solution.py:20
  22.8 8.1 %collective-permute-start.9 = (bf16[8,32,512]{2,1,0:T(8,128)(2,1)S(1)}, bf16[8,32,512]{2,1,0:T(8,128)(2,1)}, u32[]{:S(2)}, u32[]{:S(2)}) collective-permute-start(bf16[8,32,512]{2,1,0:T(8,128)(2,1)S(1)} %multiply_convert_fusion.refs_4_), channel_id=1, source_target_pairs={{2,0},{4,2},{6,4},{8,6},{10,8},{12,10},{14,12},{16,14},{18,16},{20... | collective-permute-start | bytes 786440 | tf_op jit(solution)/shard_map/ppermute | solution.py:235
  39.5 8.1 %collective-permute-start.3 = (bf16[1,2048]{1,0:T(2,128)(2,1)S(1)}, bf16[1,2048]{1,0:T(2,128)(2,1)S(1)}, u32[]{:S(2)}, u32[]{:S(2)}) collective-permute-start(bf16[1,2048]{1,0:T(2,128)(2,1)S(1)} %get-tuple-element.26), channel_id=1, source_target_pairs={{2,0},{4,2},{6,4},{8,6},{10,8},{12,10},{14,12},{16,14},{18,16},{20... | collective-permute-start | bytes 12296 | tf_op jit(solution)/shard_map/ppermute | solution.py:20
  59.9 6.9 %reduce-scatter.3.cloned.1.call-done = f32[1,32,512]{2,1,0:T(8,128)} async-done(((f32[1,64,512]{2,1,0:T(8,128)}), f32[1,32,512]{2,1,0:T(8,128)}) %reduce-scatter.3.cloned.1.call-update) | async-done | bytes 65552 | tf_op jit(solution)/shard_map/reduce_scatter | solution.py:332
  68.3 3.4 %collective-permute-start.4 = (bf16[1,2048]{1,0:T(2,128)(2,1)S(1)}, bf16[1,2048]{1,0:T(2,128)(2,1)S(1)}, u32[]{:S(2)}, u32[]{:S(2)}) collective-permute-start(bf16[1,2048]{1,0:T(2,128)(2,1)S(1)} %get-tuple-element.21), channel_id=1, source_target_pairs={{0,2},{2,4},{4,6},{6,8},{8,10},{10,12},{12,14},{14,16},{16,18},{18... | collective-permute-start | bytes 12296 | tf_op jit(solution)/shard_map/ppermute | solution.py:17
  71.8 6.6 %collective-permute-start.5 = (bf16[1,2048]{1,0:T(2,128)(2,1)S(1)}, bf16[1,2048]{1,0:T(2,128)(2,1)S(1)}, u32[]{:S(2)}, u32[]{:S(2)}) collective-permute-start(bf16[1,2048]{1,0:T(2,128)(2,1)S(1)} %get-tuple-element.22), channel_id=1, source_target_pairs={{2,0},{4,2},{6,4},{8,6},{10,8},{12,10},{14,12},{16,14},{18,16},{20... | collective-permute-start | bytes 12296 | tf_op jit(solution)/shard_map/ppermute | solution.py:20
  82.2 8.4 %collective-permute-start.7 = (bf16[8,32,512]{2,1,0:T(8,128)(2,1)S(1)}, bf16[8,32,512]{2,1,0:T(8,128)(2,1)}, u32[]{:S(2)}, u32[]{:S(2)}) collective-permute-start(bf16[8,32,512]{2,1,0:T(8,128)(2,1)S(1)} %fusion.14), channel_id=1, source_target_pairs={{2,0},{4,2},{6,4},{8,6},{10,8},{12,10},{14,12},{16,14},{18,16},{20... | collective-permute-start | bytes 786440 | tf_op jit(solution)/shard_map/ppermute | solution.py:235
  97.3 5.6 %fusion.7 = f32[25,512,128]{1,2,0:T(8,128)} fusion(bf16[24,512,64]{1,2,0:T(8,128)(2,1)} %bitcast.211), kind=kLoop, calls=%fused_computation.15 | loop fusion | flops 11468800 | bytes 8126464 | tf_op jit(solution)/shard_map/reshape | solution.py:177
  102.9 8.2 %copy.51 = f32[25,512,128]{2,1,0:T(8,128)} copy(f32[25,512,128]{1,2,0:T(8,128)} %fusion.7) | data formatting | bytes 13107200 | tf_op jit(solution)/shard_map/reshape | solution.py:177
  111.1 9.9 %shard_map.265 = bf16[8,32,512]{2,1,0:T(8,128)(2,1)S(1)} custom-call(s32[8,27]{1,0:T(8,128)S(1)} %pad_add_fusion.refs_0_, s32[1]{0:T(128)} %copy.68.refs_1_, f32[25,8,8,8,128]{4,3,2,1,0:T(8,128)} %bitcast.199, bf16[3,32,768]{2,1,0:T(8,128)(2,1)S(1)} %reshape.542.refs_3_), custom_call_target="tpu_custom_call" | custom-call | flops 603979776 | bytes 6553600 | tf_op jit(solution)/shard_map/pallas_call | solution.py:196
  123.5 8.8 %collective-permute-start.11 = (bf16[1,2048]{1,0:T(2,128)(2,1)S(1)}, bf16[1,2048]{1,0:T(2,128)(2,1)S(1)}, u32[]{:S(2)}, u32[]{:S(2)}) collective-permute-start(bf16[1,2048]{1,0:T(2,128)(2,1)S(1)} %get-tuple-element.24), channel_id=1, source_target_pairs={{2,0},{4,2},{6,4},{8,6},{10,8},{12,10},{14,12},{16,14},{18,16},{20... | collective-permute-start | bytes 12296 | tf_op jit(solution)/shard_map/ppermute | solution.py:20
  143.7 5.7 %fusion.5 = f32[25,512,128]{1,2,0:T(8,128)} fusion(bf16[24,512,64]{1,2,0:T(8,128)(2,1)} %bitcast.210), kind=kLoop, calls=%fused_computation.13 | loop fusion | flops 11468800 | bytes 8126464 | tf_op jit(solution)/shard_map/reshape | solution.py:177
  149.4 8.2 %copy.48 = f32[25,512,128]{2,1,0:T(8,128)} copy(f32[25,512,128]{1,2,0:T(8,128)} %fusion.5) | data formatting | bytes 13107200 | tf_op jit(solution)/shard_map/reshape | solution.py:177
  157.6 14.1 %shard_map.264 = (bf16[8,32,512]{2,1,0:T(8,128)(2,1)}, f32[3,32,768]{2,1,0:T(8,128)S(1)}) custom-call(s32[8,27]{1,0:T(8,128)S(1)} %pad_add_fusion.refs_0_, s32[1]{0:T(128)} %copy.68.refs_1_, f32[25,8,8,8,128]{4,3,2,1,0:T(8,128)} %bitcast.198, bf16[3,32,768]{2,1,0:T(8,128)(2,1)S(1)} %reshape.537.refs_3_, bf16[8,32,512]{2,1,0:T(8,128)(2,1)S(1)} %multiply_convert_fusion.refs_4_), custom_call_target="tpu_custom_call" | custom-call | flops 1207959552 | bytes 6553600 | tf_op jit(solution)/shard_map/pallas_call | solution.py:196
  172.8 2.2 collective-permute-start.14
  175.0 13.4 %collective-permute-done.14 = f32[1024,128]{1,0:T(8,128)S(1)} collective-permute-done((f32[1024,128]{1,0:T(8,128)S(1)}, f32[1024,128]{1,0:T(8,128)S(1)}, u32[]{:S(2)}, u32[]{:S(2)}) %collective-permute-start.14) | collective-permute-done | bytes 524320 | tf_op jit(solution)/shard_map/ppermute | solution.py:253
  188.9 7.2 %collective-permute-done.15 = f32[512,128]{1,0:T(8,128)S(1)} collective-permute-done((f32[512,128]{1,0:T(8,128)S(1)}, f32[512,128]{1,0:T(8,128)S(1)}, u32[]{:S(2)}, u32[]{:S(2)}) %collective-permute-start.15) | collective-permute-done | bytes 262176 | tf_op jit(solution)/shard_map/ppermute | solution.py:253
  196.3 7.1 %collective-permute-done.16 = f32[256,128]{1,0:T(8,128)S(1)} collective-permute-done((f32[256,128]{1,0:T(8,128)S(1)}, f32[256,128]{1,0:T(8,128)S(1)}, u32[]{:S(2)}, u32[]{:S(2)}) %collective-permute-start.16) | collective-permute-done | bytes 131104 | tf_op jit(solution)/shard_map/ppermute | solution.py:253
  203.6 4.2 %collective-permute-done.17 = f32[128,128]{1,0:T(8,128)S(1)} collective-permute-done((f32[128,128]{1,0:T(8,128)S(1)}, f32[128,128]{1,0:T(8,128)S(1)}, u32[]{:S(2)}, u32[]{:S(2)}) %collective-permute-start.17) | collective-permute-done | bytes 65568 | tf_op jit(solution)/shard_map/ppermute | solution.py:253
  208.0 7.8 %collective-permute-done.18 = f32[64,128]{1,0:T(8,128)S(1)} collective-permute-done((f32[64,128]{1,0:T(8,128)S(1)}, f32[64,128]{1,0:T(8,128)S(1)}, u32[]{:S(2)}, u32[]{:S(2)}) %collective-permute-start.18) | collective-permute-done | bytes 32800 | tf_op jit(solution)/shard_map/ppermute | solution.py:253
  215.9 4.6 %collective-permute-done.19 = f32[32,128]{1,0:T(8,128)S(1)} collective-permute-done((f32[32,128]{1,0:T(8,128)S(1)}, f32[32,128]{1,0:T(8,128)S(1)}, u32[]{:S(2)}, u32[]{:S(2)}) %collective-permute-start.19) | collective-permute-done | bytes 16416 | tf_op jit(solution)/shard_map/ppermute | solution.py:253
  220.6 3.6 %collective-permute-done.20 = f32[16,128]{1,0:T(8,128)S(1)} collective-permute-done((f32[16,128]{1,0:T(8,128)S(1)}, f32[16,128]{1,0:T(8,128)S(1)}, u32[]{:S(2)}, u32[]{:S(2)}) %collective-permute-start.20) | collective-permute-done | bytes 8224 | tf_op jit(solution)/shard_map/ppermute | solution.py:253
  224.2 3.6 %collective-permute-done.21 = f32[16,128]{1,0:T(8,128)S(1)} collective-permute-done((f32[16,128]{1,0:T(8,128)S(1)}, f32[16,128]{1,0:T(8,128)S(1)}, u32[]{:S(2)}, u32[]{:S(2)}) %collective-permute-start.21) | collective-permute-done | bytes 8224 | tf_op jit(solution)/shard_map/ppermute | solution.py:258
  227.9 4.6 %collective-permute-done.22 = f32[32,128]{1,0:T(8,128)S(1)} collective-permute-done((f32[32,128]{1,0:T(8,128)S(1)}, f32[32,128]{1,0:T(8,128)S(1)}, u32[]{:S(2)}, u32[]{:S(2)}) %collective-permute-start.22) | collective-permute-done | bytes 16416 | tf_op jit(solution)/shard_map/ppermute | solution.py:258
  233.3 7.0 %collective-permute-done.23 = f32[64,128]{1,0:T(8,128)S(1)} collective-permute-done((f32[64,128]{1,0:T(8,128)S(1)}, f32[64,128]{1,0:T(8,128)S(1)}, u32[]{:S(2)}, u32[]{:S(2)}) %collective-permute-start.23) | collective-permute-done | bytes 32800 | tf_op jit(solution)/shard_map/ppermute | solution.py:258
  242.4 2.3 collective-permute-done.24
  247.4 4.1 %collective-permute-done.25 = f32[256,128]{1,0:T(8,128)S(1)} collective-permute-done((f32[256,128]{1,0:T(8,128)S(1)}, f32[256,128]{1,0:T(8,128)S(1)}, u32[]{:S(2)}, u32[]{:S(2)}) %collective-permute-start.25) | collective-permute-done | bytes 131104 | tf_op jit(solution)/shard_map/ppermute | solution.py:258
  252.3 8.5 %reduce-scatter.5.cloned.1.call-done = bf16[1,32,512]{2,1,0:T(8,128)(2,1)} async-done(((bf16[1,64,512]{2,1,0:T(8,128)(2,1)}), bf16[1,32,512]{2,1,0:T(8,128)(2,1)}) %reduce-scatter.5.cloned.1.call-update) | async-done | bytes 32784 | tf_op jit(solution)/shard_map/reduce_scatter | solution.py:386
  262.3 2.2 collective-permute-start.27
  264.5 3.5 %collective-permute-start.12 = (bf16[1,2048]{1,0:T(2,128)(2,1)S(1)}, bf16[1,2048]{1,0:T(2,128)(2,1)S(1)}, u32[]{:S(2)}, u32[]{:S(2)}) collective-permute-start(bf16[1,2048]{1,0:T(2,128)(2,1)S(1)} %get-tuple-element.19), channel_id=1, source_target_pairs={{0,2},{2,4},{4,6},{6,8},{8,10},{10,12},{12,14},{14,16},{16,18},{18... | collective-permute-start | bytes 12296 | tf_op jit(solution)/shard_map/ppermute | solution.py:17
  268.0 6.7 %collective-permute-start.13 = (bf16[1,2048]{1,0:T(2,128)(2,1)S(1)}, bf16[1,2048]{1,0:T(2,128)(2,1)S(1)}, u32[]{:S(2)}, u32[]{:S(2)}) collective-permute-start(bf16[1,2048]{1,0:T(2,128)(2,1)S(1)} %get-tuple-element.20), channel_id=1, source_target_pairs={{2,0},{4,2},{6,4},{8,6},{10,8},{12,10},{14,12},{16,14},{18,16},{20... | collective-permute-start | bytes 12296 | tf_op jit(solution)/shard_map/ppermute | solution.py:20
  (193 shorter events, 65.4 us)
Async XLA Ops:
  7.2 59.6 %reduce-scatter.3.cloned.1.call-start = ((), (), s32[]{:S(2)}) async-start(), calls=%async_computation.2 | async-start | bytes 196608 | tf_op jit(solution)/shard_map/reduce_scatter | solution.py:332
  7.2 32.2 %collective-permute-start = (s32[8]{0:T(128)}, s32[8]{0:T(128)S(1)}, u32[]{:S(2)}, u32[]{:S(2)}) collective-permute-start(s32[8]{0:T(128)} %param.27), channel_id=1, source_target_pairs={{0,2},{2,4},{4,6},{6,8},{8,10},{10,12},{12,14},{14,16},{16,18},{18... | collective-permute-start | bytes 104 | tf_op jit(solution)/shard_map/ppermute | solution.py:17
  11.2 36.8 %collective-permute-start.1 = (s32[8]{0:T(128)}, s32[8]{0:T(128)S(1)}, u32[]{:S(2)}, u32[]{:S(2)}) collective-permute-start(s32[8]{0:T(128)} %param.27), channel_id=1, source_target_pairs={{2,0},{4,2},{6,4},{8,6},{10,8},{12,10},{14,12},{16,14},{18,16},{20... | collective-permute-start | bytes 104 | tf_op jit(solution)/shard_map/ppermute | solution.py:20
  20.9 37.0 %collective-permute-start.8 = (bf16[8,32,512]{2,1,0:T(8,128)(2,1)S(1)}, bf16[8,32,512]{2,1,0:T(8,128)(2,1)S(1)}, u32[]{:S(2)}, u32[]{:S(2)}) collective-permute-start(bf16[8,32,512]{2,1,0:T(8,128)(2,1)S(1)} %multiply_convert_fusion.refs_4_), channel_id=1, source_target_pairs={{0,2},{2,4},{4,6},{6,8},{8,10},{10,12},{12,14},{14,16},{16,18},{18... | collective-permute-start | bytes 786440 | tf_op jit(solution)/shard_map/ppermute | solution.py:234
  22.8 35.1 %collective-permute-start.9 = (bf16[8,32,512]{2,1,0:T(8,128)(2,1)S(1)}, bf16[8,32,512]{2,1,0:T(8,128)(2,1)}, u32[]{:S(2)}, u32[]{:S(2)}) collective-permute-start(bf16[8,32,512]{2,1,0:T(8,128)(2,1)S(1)} %multiply_convert_fusion.refs_4_), channel_id=1, source_target_pairs={{2,0},{4,2},{6,4},{8,6},{10,8},{12,10},{14,12},{16,14},{18,16},{20... | collective-permute-start | bytes 786440 | tf_op jit(solution)/shard_map/ppermute | solution.py:235
  33.5 17.2 %collective-permute-start.2 = (bf16[1,2048]{1,0:T(2,128)(2,1)S(1)}, bf16[1,2048]{1,0:T(2,128)(2,1)S(1)}, u32[]{:S(2)}, u32[]{:S(2)}) collective-permute-start(bf16[1,2048]{1,0:T(2,128)(2,1)S(1)} %get-tuple-element.25), channel_id=1, source_target_pairs={{0,2},{2,4},{4,6},{6,8},{8,10},{10,12},{12,14},{14,16},{16,18},{18... | collective-permute-start | bytes 12296 | tf_op jit(solution)/shard_map/ppermute | solution.py:17
  39.5 11.2 %collective-permute-start.3 = (bf16[1,2048]{1,0:T(2,128)(2,1)S(1)}, bf16[1,2048]{1,0:T(2,128)(2,1)S(1)}, u32[]{:S(2)}, u32[]{:S(2)}) collective-permute-start(bf16[1,2048]{1,0:T(2,128)(2,1)S(1)} %get-tuple-element.26), channel_id=1, source_target_pairs={{2,0},{4,2},{6,4},{8,6},{10,8},{12,10},{14,12},{16,14},{18,16},{20... | collective-permute-start | bytes 12296 | tf_op jit(solution)/shard_map/ppermute | solution.py:20
  55.7 41.7 %all-gather.7.cloned.1.call-start = ((), (), s32[]{:S(2)}) async-start(), calls=%async_computation.4 | async-start | bytes 2359296 | tf_op jit(solution)/shard_map/all_gather | solution.py:350
  59.8 83.8 %all-gather.5.cloned.1.call-start = ((), (), s32[]{:S(2)}) async-start(), calls=%async_computation.3 | async-start | bytes 2359296 | tf_op jit(solution)/shard_map/all_gather | solution.py:358
  68.3 10.3 %collective-permute-start.4 = (bf16[1,2048]{1,0:T(2,128)(2,1)S(1)}, bf16[1,2048]{1,0:T(2,128)(2,1)S(1)}, u32[]{:S(2)}, u32[]{:S(2)}) collective-permute-start(bf16[1,2048]{1,0:T(2,128)(2,1)S(1)} %get-tuple-element.21), channel_id=1, source_target_pairs={{0,2},{2,4},{4,6},{6,8},{8,10},{10,12},{12,14},{14,16},{16,18},{18... | collective-permute-start | bytes 12296 | tf_op jit(solution)/shard_map/ppermute | solution.py:17
  71.8 8.0 %collective-permute-start.5 = (bf16[1,2048]{1,0:T(2,128)(2,1)S(1)}, bf16[1,2048]{1,0:T(2,128)(2,1)S(1)}, u32[]{:S(2)}, u32[]{:S(2)}) collective-permute-start(bf16[1,2048]{1,0:T(2,128)(2,1)S(1)} %get-tuple-element.22), channel_id=1, source_target_pairs={{2,0},{4,2},{6,4},{8,6},{10,8},{12,10},{14,12},{16,14},{18,16},{20... | collective-permute-start | bytes 12296 | tf_op jit(solution)/shard_map/ppermute | solution.py:20
  80.3 13.8 %collective-permute-start.6 = (bf16[8,32,512]{2,1,0:T(8,128)(2,1)S(1)}, bf16[8,32,512]{2,1,0:T(8,128)(2,1)}, u32[]{:S(2)}, u32[]{:S(2)}) collective-permute-start(bf16[8,32,512]{2,1,0:T(8,128)(2,1)S(1)} %fusion.14), channel_id=1, source_target_pairs={{0,2},{2,4},{4,6},{6,8},{8,10},{10,12},{12,14},{14,16},{16,18},{18... | collective-permute-start | bytes 786440 | tf_op jit(solution)/shard_map/ppermute | solution.py:234
  82.2 13.0 %collective-permute-start.7 = (bf16[8,32,512]{2,1,0:T(8,128)(2,1)S(1)}, bf16[8,32,512]{2,1,0:T(8,128)(2,1)}, u32[]{:S(2)}, u32[]{:S(2)}) collective-permute-start(bf16[8,32,512]{2,1,0:T(8,128)(2,1)S(1)} %fusion.14), channel_id=1, source_target_pairs={{2,0},{4,2},{6,4},{8,6},{10,8},{12,10},{14,12},{16,14},{18,16},{20... | collective-permute-start | bytes 786440 | tf_op jit(solution)/shard_map/ppermute | solution.py:235
  97.3 163.6 %reduce-scatter.5.cloned.1.call-start = ((), (), s32[]{:S(2)}) async-start(), calls=%async_computation.5 | async-start | bytes 98304 | tf_op jit(solution)/shard_map/reduce_scatter | solution.py:386
  121.5 11.8 %collective-permute-start.10 = (bf16[1,2048]{1,0:T(2,128)(2,1)S(1)}, bf16[1,2048]{1,0:T(2,128)(2,1)S(1)}, u32[]{:S(2)}, u32[]{:S(2)}) collective-permute-start(bf16[1,2048]{1,0:T(2,128)(2,1)S(1)} %get-tuple-element.23), channel_id=1, source_target_pairs={{0,2},{2,4},{4,6},{6,8},{8,10},{10,12},{12,14},{14,16},{16,18},{18... | collective-permute-start | bytes 12296 | tf_op jit(solution)/shard_map/ppermute | solution.py:17
  123.5 10.1 %collective-permute-start.11 = (bf16[1,2048]{1,0:T(2,128)(2,1)S(1)}, bf16[1,2048]{1,0:T(2,128)(2,1)S(1)}, u32[]{:S(2)}, u32[]{:S(2)}) collective-permute-start(bf16[1,2048]{1,0:T(2,128)(2,1)S(1)} %get-tuple-element.24), channel_id=1, source_target_pairs={{2,0},{4,2},{6,4},{8,6},{10,8},{12,10},{14,12},{16,14},{18,16},{20... | collective-permute-start | bytes 12296 | tf_op jit(solution)/shard_map/ppermute | solution.py:20
  172.8 15.6 %collective-permute-start.14 = (f32[1024,128]{1,0:T(8,128)S(1)}, f32[1024,128]{1,0:T(8,128)S(1)}, u32[]{:S(2)}, u32[]{:S(2)}) collective-permute-start(f32[1024,128]{1,0:T(8,128)S(1)} %select_bitcast_fusion), channel_id=1, source_target_pairs={{0,128},{2,130},{4,132},{6,134},{8,136},{10,138},{12,140},{14,142}... | collective-permute-start | bytes 1572872 | tf_op jit(solution)/shard_map/ppermute | solution.py:253
  188.5 7.6 %collective-permute-start.15 = (f32[512,128]{1,0:T(8,128)S(1)}, f32[512,128]{1,0:T(8,128)S(1)}, u32[]{:S(2)}, u32[]{:S(2)}) collective-permute-start(f32[512,128]{1,0:T(8,128)S(1)} %slice_select_fusion), channel_id=1, source_target_pairs={{0,64},{2,66},{4,68},{6,70},{8,72},{10,74},{12,76},{14,78},{16,80}... | collective-permute-start | bytes 786440 | tf_op jit(solution)/shard_map/ppermute | solution.py:253
  196.2 7.2 %collective-permute-start.16 = (f32[256,128]{1,0:T(8,128)S(1)}, f32[256,128]{1,0:T(8,128)S(1)}, u32[]{:S(2)}, u32[]{:S(2)}) collective-permute-start(f32[256,128]{1,0:T(8,128)S(1)} %slice_select_fusion.1), channel_id=1, source_target_pairs={{0,32},{2,34},{4,36},{6,38},{8,40},{10,42},{12,44},{14,46},{16,48}... | collective-permute-start | bytes 393224 | tf_op jit(solution)/shard_map/ppermute | solution.py:253
  203.4 4.4 %collective-permute-start.17 = (f32[128,128]{1,0:T(8,128)S(1)}, f32[128,128]{1,0:T(8,128)S(1)}, u32[]{:S(2)}, u32[]{:S(2)}) collective-permute-start(f32[128,128]{1,0:T(8,128)S(1)} %slice_select_fusion.2), channel_id=1, source_target_pairs={{0,16},{2,18},{4,20},{6,22},{8,24},{10,26},{12,28},{14,30},{16,0},... | collective-permute-start | bytes 196616 | tf_op jit(solution)/shard_map/ppermute | solution.py:253
  207.8 7.9 %collective-permute-start.18 = (f32[64,128]{1,0:T(8,128)S(1)}, f32[64,128]{1,0:T(8,128)S(1)}, u32[]{:S(2)}, u32[]{:S(2)}) collective-permute-start(f32[64,128]{1,0:T(8,128)S(1)} %slice_select_fusion.3), channel_id=1, source_target_pairs={{0,8},{2,10},{4,12},{6,14},{8,0},{10,2},{12,4},{14,6},{16,24},{18,... | collective-permute-start | bytes 98312 | tf_op jit(solution)/shard_map/ppermute | solution.py:253
  215.8 4.7 %collective-permute-start.19 = (f32[32,128]{1,0:T(8,128)S(1)}, f32[32,128]{1,0:T(8,128)S(1)}, u32[]{:S(2)}, u32[]{:S(2)}) collective-permute-start(f32[32,128]{1,0:T(8,128)S(1)} %slice_select_fusion.4), channel_id=1, source_target_pairs={{0,4},{2,6},{4,0},{6,2},{8,12},{10,14},{12,8},{14,10},{16,20},{18,... | collective-permute-start | bytes 49160 | tf_op jit(solution)/shard_map/ppermute | solution.py:253
  220.5 3.7 %collective-permute-start.20 = (f32[16,128]{1,0:T(8,128)S(1)}, f32[16,128]{1,0:T(8,128)S(1)}, u32[]{:S(2)}, u32[]{:S(2)}) collective-permute-start(f32[16,128]{1,0:T(8,128)S(1)} %slice_select_fusion.5), channel_id=1, source_target_pairs={{0,2},{2,0},{4,6},{6,4},{8,10},{10,8},{12,14},{14,12},{16,18},{18,... | collective-permute-start | bytes 24584 | tf_op jit(solution)/shard_map/ppermute | solution.py:253
  224.2 3.7 %collective-permute-start.21 = (f32[16,128]{1,0:T(8,128)S(1)}, f32[16,128]{1,0:T(8,128)S(1)}, u32[]{:S(2)}, u32[]{:S(2)}) collective-permute-start(f32[16,128]{1,0:T(8,128)S(1)} %select_add_fusion.5), channel_id=1, source_target_pairs={{0,2},{2,0},{4,6},{6,4},{8,10},{10,8},{12,14},{14,12},{16,18},{18,... | collective-permute-start | bytes 24584 | tf_op jit(solution)/shard_map/ppermute | solution.py:258
  227.9 4.6 %collective-permute-start.22 = (f32[32,128]{1,0:T(8,128)S(1)}, f32[32,128]{1,0:T(8,128)S(1)}, u32[]{:S(2)}, u32[]{:S(2)}) collective-permute-start(f32[32,128]{1,0:T(8,128)S(1)} %maximum_select_fusion.6), channel_id=1, source_target_pairs={{0,4},{2,6},{4,0},{6,2},{8,12},{10,14},{12,8},{14,10},{16,20},{18,... | collective-permute-start | bytes 49160 | tf_op jit(solution)/shard_map/ppermute | solution.py:258
  232.5 7.8 %collective-permute-start.23 = (f32[64,128]{1,0:T(8,128)S(1)}, f32[64,128]{1,0:T(8,128)S(1)}, u32[]{:S(2)}, u32[]{:S(2)}) collective-permute-start(f32[64,128]{1,0:T(8,128)S(1)} %maximum_select_fusion.5), channel_id=1, source_target_pairs={{0,8},{2,10},{4,12},{6,14},{8,0},{10,2},{12,4},{14,6},{16,24},{18,... | collective-permute-start | bytes 98312 | tf_op jit(solution)/shard_map/ppermute | solution.py:258
  240.4 4.4 %collective-permute-start.24 = (f32[128,128]{1,0:T(8,128)S(1)}, f32[128,128]{1,0:T(8,128)S(1)}, u32[]{:S(2)}, u32[]{:S(2)}) collective-permute-start(f32[128,128]{1,0:T(8,128)S(1)} %maximum_select_fusion.4), channel_id=1, source_target_pairs={{0,16},{2,18},{4,20},{6,22},{8,24},{10,26},{12,28},{14,30},{16,0},... | collective-permute-start | bytes 196616 | tf_op jit(solution)/shard_map/ppermute | solution.py:258
  244.7 6.8 %collective-permute-start.25 = (f32[256,128]{1,0:T(8,128)S(1)}, f32[256,128]{1,0:T(8,128)S(1)}, u32[]{:S(2)}, u32[]{:S(2)}) collective-permute-start(f32[256,128]{1,0:T(8,128)S(1)} %maximum_select_fusion.3), channel_id=1, source_target_pairs={{0,32},{2,34},{4,36},{6,38},{8,40},{10,42},{12,44},{14,46},{16,48}... | collective-permute-start | bytes 393224 | tf_op jit(solution)/shard_map/ppermute | solution.py:258
  251.5 10.7 %collective-permute-start.26 = (f32[512,128]{1,0:T(8,128)S(1)}, f32[512,128]{1,0:T(8,128)S(1)}, u32[]{:S(2)}, u32[]{:S(2)}) collective-permute-start(f32[512,128]{1,0:T(8,128)S(1)} %maximum_select_fusion.2), channel_id=1, source_target_pairs={{0,64},{2,66},{4,68},{6,70},{8,72},{10,74},{12,76},{14,78},{16,80}... | collective-permute-start | bytes 786440 | tf_op jit(solution)/shard_map/ppermute | solution.py:258
  262.3 15.7 %collective-permute-start.27 = (f32[1024,128]{1,0:T(8,128)S(1)}, f32[1024,128]{1,0:T(8,128)S(1)}, u32[]{:S(2)}, u32[]{:S(2)}) collective-permute-start(f32[1024,128]{1,0:T(8,128)S(1)} %maximum_select_fusion.1), channel_id=1, source_target_pairs={{0,128},{2,130},{4,132},{6,134},{8,136},{10,138},{12,140},{14,142}... | collective-permute-start | bytes 1572872 | tf_op jit(solution)/shard_map/ppermute | solution.py:258
  264.5 10.2 %collective-permute-start.12 = (bf16[1,2048]{1,0:T(2,128)(2,1)S(1)}, bf16[1,2048]{1,0:T(2,128)(2,1)S(1)}, u32[]{:S(2)}, u32[]{:S(2)}) collective-permute-start(bf16[1,2048]{1,0:T(2,128)(2,1)S(1)} %get-tuple-element.19), channel_id=1, source_target_pairs={{0,2},{2,4},{4,6},{6,8},{8,10},{10,12},{12,14},{14,16},{16,18},{18... | collective-permute-start | bytes 12296 | tf_op jit(solution)/shard_map/ppermute | solution.py:17
  268.0 8.0 %collective-permute-start.13 = (bf16[1,2048]{1,0:T(2,128)(2,1)S(1)}, bf16[1,2048]{1,0:T(2,128)(2,1)S(1)}, u32[]{:S(2)}, u32[]{:S(2)}) collective-permute-start(bf16[1,2048]{1,0:T(2,128)(2,1)S(1)} %get-tuple-element.20), channel_id=1, source_target_pairs={{2,0},{4,2},{6,4},{8,6},{10,8},{12,10},{14,12},{16,14},{18,16},{20... | collective-permute-start | bytes 12296 | tf_op jit(solution)/shard_map/ppermute | solution.py:20
  (8 other events, 276.5 us)
Sparse Core Ops, SparseCore 0:
  55.8 10.9 reduce-scatter.2
  69.1 16.4 all-gather.6
  97.4 14.8 all-gather.4
  247.5 13.2 reduce-scatter.4
where the time goes:
time: 290 us; the launch traced here: 288 us
  waiting for transfers between devices  91.8 us (32%)
  starting transfers between devices  80.7 us (28%)
  local copies, waits for them, and re-layouts  34.7 us (12%)
  Pallas kernels  28 us (10%)
  other arithmetic  23 us (8%)
  between operations  15.5 us (5%)
  matrix products  7.81 us (3%)
  blocking collectives  6.01 us (2%)
    ppermute x7, waiting for transfers between devices, sum_over_space(): arrived = lax.ppermute(jnp.where(upper, low, high), 'space', pairs)  47.9 us
    ppermute x5, starting transfers between devices, extended(): lax.ppermute(lax.slice_in_dim(block, 0, width, axis=dim), axis, backward)  38.1 us
    pallas_call x5, Pallas kernels, brick_pass(): pl.pallas_call(lambda *refs: brick_kernel(weight is not None, grad_rows i...  28 us
    ppermute x7, waiting for transfers between devices, sum_over_space(): arrived = lax.ppermute(flat, 'space', pairs)  22.5 us
    reshape x4, local copies, waits for them, and re-layouts, brick_pass(): table = table.reshape(slots + 1, 8, 8, 8, 128)  16.8 us
    ppermute x2, starting transfers between devices, around(): high = lax.ppermute(block, 'space', backward)  16.6 us
    ppermute x5, starting transfers between devices, extended(): lax.ppermute(lax.slice_in_dim(block, block.shape[dim] - width, None, axis...  14.7 us
    reshape x4, other arithmetic, brick_pass(): table = table.reshape(slots + 1, 8, 8, 8, 128)  11.4 us
  transfers between devices with their start and end apart: 32, of which 20 were waited for; matrix products, arithmetic and copies ran while one was open for 16% of the time, Pallas kernels for 5%

commit v1 on v0

v1 whole, which is shorter than its diff:
```python
import math

import jax
import jax.numpy as jnp
import numpy as np
from jax import lax
from jax.experimental import pallas as pl
from jax.experimental.pallas import tpu as pltpu
from jax.sharding import PartitionSpec as P


def lean_list():
    leans = []
    for lean_x in (-1, 0, 1):
        for lean_y in (-1, 0, 1):
            for lean_z in (-1, 0, 1):
                leans.append((lean_x, lean_y, lean_z))
    return leans


def pool_table():
    voxel = np.arange(512)
    octant_voxel = 16 * (voxel // 128) + 4 * (voxel // 16 % 4) + voxel % 8 // 2
    return (octant_voxel[:, None] == np.arange(64)[None, :]).astype(np.float32)


def octant_table():
    voxel = np.arange(512)
    coord_x = voxel // 64
    coord_y = voxel // 8 % 8
    coord_z = voxel % 8
    octant = 4 * (coord_x // 4) + 2 * (coord_y // 4) + coord_z // 4
    inner = 16 * (coord_x % 4) + 4 * (coord_y % 4) + coord_z % 4
    table = np.zeros((8, 64, 512), np.float32)
    table[octant, inner, voxel] = 1.0
    return table


def flip_weight(weight):
    return jnp.transpose(weight[::-1], (0, 2, 1))


def pool_sum(field_in):
    table = jnp.asarray(pool_table()).astype(jnp.bfloat16)
    return jnp.einsum("bcv,vu->bcu", field_in, table, preferred_element_type=jnp.float32)


def enlarge(octants):
    table = jnp.asarray(pool_table()).astype(jnp.bfloat16)
    return jnp.einsum("bcu,vu->bcv", octants, table, preferred_element_type=jnp.float32)


def place_octants(octants):
    amount, channels = (octants.shape[0] // 8, octants.shape[1])
    grouped = octants.reshape(amount, 8, channels, 64)
    table = jnp.asarray(octant_table()).astype(jnp.bfloat16)
    return jnp.einsum("jocu,ouv->jcv", grouped, table, preferred_element_type=jnp.float32).astype(
        jnp.bfloat16
    )


def split_octants(coarse):
    amount, channels = (coarse.shape[0], coarse.shape[1])
    table = jnp.asarray(octant_table()).astype(jnp.bfloat16)
    parts = jnp.einsum("jcv,ouv->jocu", coarse, table, preferred_element_type=jnp.float32).astype(
        jnp.bfloat16
    )
    return parts.reshape(amount * 8, channels, 64)


def select_rows(picker, values):
    return jnp.dot(picker, values, preferred_element_type=jnp.float32).astype(jnp.bfloat16)


def route_places(slot_list, dev_index, moving, bricks):
    direction = slot_list // bricks - dev_index
    to_left = (direction == -1).astype(jnp.int32)
    to_right = (direction == 1).astype(jnp.int32)
    left_rank = jnp.cumsum(to_left) - to_left
    right_rank = jnp.cumsum(to_right) - to_right
    return jnp.where(
        to_left == 1, left_rank, jnp.where(to_right == 1, moving + right_rank, 2 * moving)
    ).astype(jnp.int32)


def from_sides(rows, moving):
    count = lax.axis_size("space")
    low = lax.ppermute(rows[moving:], "space", [(i, i + 1) for i in range(count - 1)])
    high = lax.ppermute(rows[:moving], "space", [(i + 1, i) for i in range(count - 1)])
    return jnp.concatenate([low, high], axis=0)


def lone_bricks(amount):
    centre = jnp.arange(27, dtype=jnp.int32)[None, :] == 13
    return jnp.where(centre, jnp.arange(amount, dtype=jnp.int32)[:, None], amount)


def gather_back(local_part, send_pick, returned):
    total = local_part.astype(jnp.float32) + jnp.dot(
        send_pick.T, returned, preferred_element_type=jnp.float32
    )
    return total.astype(jnp.bfloat16)


SPANS = {-1: (slice(0, 1), slice(7, 8)), 0: (slice(1, 9), slice(0, 8)), 1: (slice(9, 10), slice(0, 1))}
KZ_ORDER = np.array([1, 0, 2])


def brick_kernel(with_conv, with_grad, masked, *refs):
    refs = list(refs)
    near_ref, live_ref, field_ref = refs[:3]
    del refs[:3]
    weight_ref = refs.pop(0) if with_conv else None
    grad_ref = refs.pop(0) if with_grad else None
    out_ref = refs.pop(0) if with_conv else None
    total_ref = refs.pop(0) if with_grad else None
    table, padded, columns = refs
    brick = pl.program_id(0)

    @pl.when(brick == 0)
    def fill():
        slots = field_ref.shape[0]

        def turn(slot, carry):
            field = field_ref[slot].astype(jnp.float32)
            turned = jnp.concatenate([field, field], axis=0).T
            table[slot] = turned.reshape(8, 8, 8, 128)
            return carry

        lax.fori_loop(0, slots, turn, 0)
        table[slots] = jnp.zeros((8, 8, 8, 128), jnp.float32)

    for index, (lean_x, lean_y, lean_z) in enumerate(lean_list()):
        slot = near_ref[brick, index]
        to_x, from_x = SPANS[lean_x]
        to_y, from_y = SPANS[lean_y]
        padded[lean_z + 1, to_x, to_y] = table[slot, from_x, from_y]
    shape = (10, 8, 8, 128)
    place_z = lax.broadcasted_iota(jnp.int32, shape, 2)
    low_half = lax.broadcasted_iota(jnp.int32, shape, 3) < 64
    for tap_y in range(3):
        below = padded[0, :, tap_y : tap_y + 8]
        level = padded[1, :, tap_y : tap_y + 8]
        above = padded[2, :, tap_y : tap_y + 8]
        minus = pltpu.roll(jnp.where(place_z == 7, below, level), 1, 2)
        plus = pltpu.roll(jnp.where(place_z == 0, above, level), 7, 2)
        first = jnp.where(low_half, level, minus).reshape(640, 128)
        second = jnp.where(low_half, plus, 0.0).reshape(640, 128)
        start = 256 * tap_y
        columns[:, start : start + 128] = first.astype(jnp.bfloat16)
        columns[:, start + 128 : start + 256] = second.astype(jnp.bfloat16)
    if with_conv:
        total = None
        for tap_x in range(3):
            part = lax.dot_general(
                weight_ref[0, tap_x],
                columns[64 * tap_x : 64 * tap_x + 512, :],
                (((1,), (1,)), ((), ())),
                preferred_element_type=jnp.float32,
            )
            total = part if total is None else total + part
        if masked:
            total = jnp.where(brick < live_ref[0], total, 0.0)
        out_ref[0] = total.astype(out_ref.dtype)
    if with_grad:

        @pl.when(brick == 0)
        def clear():
            total_ref[...] = jnp.zeros_like(total_ref)

        for tap_x in range(3):
            total_ref[tap_x] += jnp.dot(
                grad_ref[0],
                columns[64 * tap_x : 64 * tap_x + 512, :],
                preferred_element_type=jnp.float32,
            )


def brick_pass(field_in, near, live_count, weight, grad_rows, out_dtype, masked):
    amount = near.shape[0]
    slots = field_in.shape[0]
    rows = weight.shape[2] if weight is not None else grad_rows.shape[1]
    operands = [near, live_count, field_in]
    in_specs = [
        pl.BlockSpec(memory_space=pltpu.SMEM),
        pl.BlockSpec(memory_space=pltpu.SMEM),
        pl.BlockSpec((slots, 64, 512), lambda b: (0, 0, 0)),
    ]
    outs, out_specs = [], []
    if weight is not None:
        parts = weight.shape[0]
        operands.append(jnp.stack([weight_blocks(part) for part in weight]))
        in_specs.append(pl.BlockSpec((1, 3, rows, 768), lambda b: (b % parts, 0, 0, 0)))
        outs.append(jax.ShapeDtypeStruct((amount, rows, 512), out_dtype))
        out_specs.append(pl.BlockSpec((1, rows, 512), lambda b: (b, 0, 0)))
    if grad_rows is not None:
        operands.append(grad_rows)
        in_specs.append(pl.BlockSpec((1, rows, 512), lambda b: (b, 0, 0)))
        outs.append(jax.ShapeDtypeStruct((3, rows, 768), jnp.float32))
        out_specs.append(pl.BlockSpec((3, rows, 768), lambda b: (0, 0, 0)))
    products = (weight is not None) + (grad_rows is not None)
    return pl.pallas_call(
        lambda *refs: brick_kernel(weight is not None, grad_rows is not None, masked, *refs),
        grid=(amount,),
        in_specs=in_specs,
        out_specs=out_specs,
        out_shape=outs,
        scratch_shapes=[
            pltpu.VMEM((slots + 1, 8, 8, 8, 128), jnp.float32),
            pltpu.VMEM((3, 10, 10, 8, 128), jnp.float32),
            pltpu.VMEM((640, 768), jnp.bfloat16),
        ],
        compiler_params=pltpu.CompilerParams(vmem_limit_bytes=48 * 1024 * 1024),
        cost_estimate=pl.CostEstimate(
            flops=amount * products * 2 * rows * 2304 * 512,
            bytes_accessed=slots * 64 * 512 * 2,
            transcendentals=0,
        ),
    )(*operands)


def weight_blocks(weight):
    rows, channels = weight.shape[1:]
    taps = weight.reshape(9, 3, rows, channels)[:, KZ_ORDER]
    taps = jnp.concatenate([taps, jnp.zeros_like(taps[:, :1])], axis=1)
    taps = taps.reshape(3, 3, 4, rows, channels)
    return jnp.transpose(taps, (0, 3, 1, 2, 4)).reshape(3, rows, 768)


def grad_taps(total):
    rows = total.shape[1]
    taps = total.reshape(3, rows, 3, 4, 64)
    taps = jnp.transpose(taps, (0, 2, 3, 1, 4)).reshape(9, 4, rows, 64)[:, KZ_ORDER]
    return taps.reshape(27, rows, 64)


def around(block):
    count = lax.axis_size("space")
    forward = [(i, i + 1) for i in range(count - 1)]
    backward = [(i + 1, i) for i in range(count - 1)]
    low = lax.ppermute(block, "space", forward)
    high = lax.ppermute(block, "space", backward)
    return jnp.concatenate([low, block, high], axis=0)


def torus_sizes(count):
    return (4, 4, 8) if count == 128 else (1, 1, count)


def sum_kernel(sizes, data, total, part_first, part_second, part_last, own_first, own_second,
               whole_last, *sems):
    size_y, size_x, size_z = sizes
    me, core = lax.axis_index("space"), lax.axis_index("chan")
    at_z = me % size_z
    at_x = me // size_z % size_x
    at_y = me // (size_z * size_x)

    def along(axis, step):
        if axis == "x":
            return (at_y * size_x + (at_x + step) % size_x) * size_z + at_z
        if axis == "y":
            return ((at_y + step) % size_y * size_x + at_x) * size_z + at_z
        return (at_y * size_x + at_x) * size_z + (at_z + step) % size_z

    steps = {"x": size_x, "y": size_y, "z": size_z}
    place = {"x": at_x, "y": at_y, "z": at_z}
    orders = (("x", "y"), ("y", "x"))
    barrier = pltpu.get_barrier_semaphore()
    for axis in steps:
        for step in range(1, steps[axis]):
            pl.semaphore_signal(
                barrier,
                inc=1,
                device_id=(along(axis, step), core),
                device_id_type=pl.DeviceIdType.MESH,
            )
    pl.semaphore_wait(barrier, sum(steps.values()) - 3)
    started = []

    def send(source, target, phase, slot, axis, step):
        copy = pltpu.make_async_remote_copy(
            src_ref=source,
            dst_ref=target,
            send_sem=sems[2 * phase].at[slot],
            recv_sem=sems[2 * phase + 1].at[slot],
            device_id=(along(axis, step), core),
            device_id_type=pl.DeviceIdType.MESH,
        )
        copy.start()
        started.append(copy)
        return copy

    first = [(half, orders[half][0], orders[half][1]) for half in range(2)]
    copies = [[], []]
    for half, axis, _ in first:
        for step in range(1, steps[axis]):
            other = (place[axis] + step) % steps[axis]
            slot = half * (steps[axis] - 1) + step - 1
            copies[half].append(
                send(data.at[half, other], part_first.at[slot], 0, slot, axis, step)
            )
    seconds = [[], []]
    for half, axis, axis_two in first:
        value = data[half, place[axis]]
        for step in range(1, steps[axis]):
            copies[half][step - 1].wait_recv()
            value = value + part_first[half * (steps[axis] - 1) + step - 1]
        own_first[half] = value
        for step in range(1, steps[axis_two]):
            other = (place[axis_two] + step) % steps[axis_two]
            slot = half * (steps[axis_two] - 1) + step - 1
            seconds[half].append(
                send(own_first.at[half, other], part_second.at[slot], 1, slot, axis_two, step)
            )
    for half, _, axis in first:
        value = own_first[half, place[axis]]
        for step in range(1, steps[axis]):
            seconds[half][step - 1].wait_recv()
            value = value + part_second[half * (steps[axis] - 1) + step - 1]
        for level in range(size_z):
            own_second[level, half] = value[level]
    lasts = []
    for step in range(1, size_z):
        other = (at_z + step) % size_z
        lasts.append(
            send(own_second.at[other], part_last.at[step - 1], 2, step - 1, "z", step)
        )
    value = own_second[at_z]
    for step in range(1, size_z):
        lasts[step - 1].wait_recv()
        value = value + part_last[step - 1]
    whole_last[at_z] = value
    lasts = []
    for step in range(1, size_z):
        lasts.append(
            send(whole_last.at[at_z], whole_last.at[at_z], 3, step - 1, "z", step)
        )
    for copy in lasts:
        copy.wait_recv()
    seconds = [[], []]
    for half, axis, axis_two in first:
        for level in range(size_z):
            total[half, place[axis], place[axis_two], level] = whole_last[level, half]
        for step in range(1, steps[axis_two]):
            slot = half * (steps[axis_two] - 1) + step - 1
            spot = total.at[half, place[axis], place[axis_two]]
            seconds[half].append(send(spot, spot, 4, slot, axis_two, step))
    copies = []
    for half, axis, axis_two in first:
        for copy in seconds[half]:
            copy.wait_recv()
        spot = total.at[half, place[axis]]
        for step in range(1, steps[axis]):
            slot = half * (steps[axis] - 1) + step - 1
            copies.append(send(spot, spot, 5, slot, axis, step))
    for copy in copies:
        copy.wait_recv()
    for copy in started:
        copy.wait_send()


def sum_tiles(tiles):
    count = lax.axis_size("space")
    sizes = torus_sizes(count)
    side, size_z = sizes[1], sizes[2]
    piece = tiles.shape[0] // (2 * count)
    shape = (2, side, side, size_z, piece, 8, 128)
    peers = max(1, 2 * (side - 1))
    sems = []
    for number in (peers, peers, size_z - 1, size_z - 1, peers, peers):
        sems += [pltpu.SemaphoreType.DMA((number,)), pltpu.SemaphoreType.DMA((number,))]
    summed = pl.pallas_call(
        lambda *refs: sum_kernel(sizes, *refs),
        in_specs=[pl.BlockSpec(memory_space=pltpu.VMEM)],
        out_specs=pl.BlockSpec(memory_space=pltpu.VMEM),
        out_shape=jax.ShapeDtypeStruct(shape, jnp.float32),
        scratch_shapes=[
            pltpu.VMEM((peers,) + shape[2:], jnp.float32),
            pltpu.VMEM((peers,) + shape[3:], jnp.float32),
            pltpu.VMEM((size_z - 1, 2) + shape[4:], jnp.float32),
            pltpu.VMEM((2,) + shape[2:], jnp.float32),
            pltpu.VMEM((size_z, 2) + shape[4:], jnp.float32),
            pltpu.VMEM((size_z, 2) + shape[4:], jnp.float32),
        ]
        + sems,
        compiler_params=pltpu.CompilerParams(
            collective_id=1, has_side_effects=True, vmem_limit_bytes=32 * 1024 * 1024
        ),
        cost_estimate=pl.CostEstimate(
            flops=tiles.size * 4, bytes_accessed=tiles.size * 32, transcendentals=0
        ),
    )(tiles.reshape(shape))
    return summed.reshape(tiles.shape)


def sum_over_space(fine, coarse, project):
    wide = jnp.concatenate([fine.reshape(-1, 768), coarse.reshape(-1, 768)], axis=0)
    tiles = jnp.transpose(wide.reshape(-1, 8, 6, 128), (0, 2, 1, 3)).reshape(-1, 8, 128)
    small = project.reshape(-1, 8, 128)
    count = lax.axis_size("space")
    used = tiles.shape[0] + small.shape[0]
    spare = -used % (2 * count)
    tiles = jnp.concatenate([tiles, small, jnp.zeros((spare, 8, 128), jnp.float32)], axis=0)
    tiles = sum_tiles(tiles)
    wide_tiles = wide.shape[0] // 8 * 6
    wide = jnp.transpose(tiles[:wide_tiles].reshape(-1, 6, 8, 128), (0, 2, 1, 3)).reshape(-1, 768)
    fine_rows = 3 * fine.shape[1]
    return (
        wide[:fine_rows].reshape(fine.shape),
        wide[fine_rows:].reshape(coarse.shape),
        tiles[wide_tiles:used].reshape(project.shape),
    )


def per_device(
    feats, live_count, neighbours, parent, fine_weight, coarse_weight, project_weight, cotangent
):
    bricks = feats.shape[0]
    half_channels = feats.shape[1]
    devices = lax.axis_size("space")
    own_index = lax.axis_index("space")
    moving = max(1, bricks // 8)
    coarse_bricks = bricks // 8
    live_mask = (jnp.arange(bricks, dtype=jnp.int32) < live_count[0]).astype(jnp.float32)[
        :, None, None
    ]
    core = lax.axis_index("chan")
    whole_coarse = lax.all_gather(coarse_weight, "chan", axis=1, tiled=True)
    whole_project = lax.all_gather(project_weight, "chan", axis=1, tiled=True)
    whole_fine = lax.all_gather(fine_weight, "chan", axis=1, tiled=True)
    send_place = route_places(parent, own_index, moving, bricks)
    send_pick = (jnp.arange(2 * moving, dtype=jnp.int32)[:, None] == send_place[None, :]).astype(
        jnp.bfloat16
    )
    pooled = (pool_sum(feats) * 0.125 * live_mask).astype(jnp.bfloat16).reshape(bricks, -1)
    slot_rows = jnp.broadcast_to(
        (parent % bricks + 1).astype(jnp.bfloat16)[:, None], (bricks, 128)
    )
    outgoing = select_rows(send_pick, jnp.concatenate([pooled, slot_rows], axis=1))
    incoming = from_sides(outgoing, moving)
    incoming_slots = incoming[:, -1].astype(jnp.int32) - 1
    local_slots = jnp.where(parent // bricks == own_index, parent % bricks, -1)
    all_slots = jnp.concatenate([local_slots, incoming_slots])
    receive_pick = (jnp.arange(bricks, dtype=jnp.int32)[:, None] == all_slots[None, :]).astype(
        jnp.bfloat16
    )
    arrived = select_rows(receive_pick, jnp.concatenate([pooled, incoming[:, :-128]], axis=0))
    coarse_half = place_octants(arrived.reshape(bricks, half_channels, 64))
    coarse_in = lax.all_gather(coarse_half, "chan", axis=1, tiled=True)
    lone = lone_bricks(coarse_bricks)
    preactivation = brick_pass(
        coarse_in, lone, live_count, whole_coarse[None], None, jnp.float32, False
    )[0]
    hidden = jax.nn.silu(preactivation).astype(jnp.bfloat16)
    own_project = lax.dynamic_slice_in_dim(
        whole_project, core * half_channels, half_channels, 0
    )
    coarse_out = jnp.einsum(
        "cj,bjv->bcv", own_project, hidden, preferred_element_type=jnp.float32
    ).astype(jnp.bfloat16)
    back_source = select_rows(receive_pick.T, split_octants(coarse_out).reshape(bricks, -1))
    up_octants = gather_back(
        back_source[:bricks], send_pick, from_sides(back_source[bricks:], moving)
    ).reshape(bricks, half_channels, 64)
    mixed_feats = ((feats.astype(jnp.float32) + enlarge(up_octants)) * live_mask).astype(
        jnp.bfloat16
    )
    last_brick = devices * bricks
    near_local = jnp.where(
        neighbours >= last_brick, 3 * bricks, neighbours - (own_index - 1) * bricks
    ).astype(jnp.int32)
    slots = jnp.arange(bricks, dtype=jnp.int32)[:, None] + bricks
    near = jnp.concatenate([near_local[:, :13], slots, near_local[:, 13:]], axis=1)
    grad_rows = (cotangent.astype(jnp.float32) * live_mask).astype(jnp.bfloat16)
    grad_table = lax.all_gather(around(grad_rows), "chan", axis=1, tiled=True)
    own_weight = lax.dynamic_slice_in_dim(whole_fine, core * half_channels, half_channels, 2)
    back_feats = brick_pass(
        grad_table, near, live_count, flip_weight(own_weight)[None], None, jnp.bfloat16, True
    )[0]
    feat_table = lax.all_gather(around(mixed_feats), "chan", axis=1, tiled=True)
    out_feats, fine_total = brick_pass(
        feat_table, near, live_count, fine_weight[None], grad_rows, jnp.bfloat16, True
    )
    up_grad = pool_sum(back_feats).astype(jnp.bfloat16).reshape(bricks, -1)
    outgoing_grad = select_rows(send_pick, up_grad)
    arrived_grad = select_rows(
        receive_pick, jnp.concatenate([up_grad, from_sides(outgoing_grad, moving)], axis=0)
    )
    coarse_grad_half = place_octants(arrived_grad.reshape(bricks, half_channels, 64))
    coarse_grad = lax.all_gather(coarse_grad_half, "chan", axis=1, tiled=True)
    hidden_half = hidden.shape[1] // 2
    own_hidden = lax.dynamic_slice_in_dim(hidden, core * hidden_half, hidden_half, 1)
    project_matrix = jnp.einsum(
        "bcv,bjv->cj", coarse_grad, own_hidden, preferred_element_type=jnp.float32
    )
    hidden_grad = jnp.einsum(
        "cj,bcv->bjv", whole_project, coarse_grad, preferred_element_type=jnp.float32
    )
    sigmoid_pre = jax.nn.sigmoid(preactivation)
    pre_grad = (hidden_grad * sigmoid_pre * (1.0 + preactivation * (1.0 - sigmoid_pre))).astype(
        jnp.bfloat16
    )
    own_pre_grad = lax.dynamic_slice_in_dim(pre_grad, core * hidden_half, hidden_half, 1)
    coarse_total = brick_pass(
        coarse_in, lone, live_count, None, own_pre_grad, None, False
    )[0]
    own_coarse = flip_weight(
        lax.dynamic_slice_in_dim(whole_coarse, core * half_channels, half_channels, 2)
    )
    coarse_terms = brick_pass(
        pre_grad.reshape(2 * coarse_bricks, hidden_half, 512),
        lone_bricks(2 * coarse_bricks),
        live_count,
        jnp.stack([own_coarse[:, :, :hidden_half], own_coarse[:, :, hidden_half:]]),
        None,
        jnp.float32,
        False,
    )[0]
    coarse_back = (
        coarse_terms.reshape(coarse_bricks, 2, half_channels, 512).sum(1).astype(jnp.bfloat16)
    )
    down_source = select_rows(receive_pick.T, split_octants(coarse_back).reshape(bricks, -1))
    down_grad = gather_back(
        down_source[:bricks], send_pick, from_sides(down_source[bricks:], moving)
    ).reshape(bricks, half_channels, 64)
    grad_feats = (back_feats.astype(jnp.float32) + live_mask * enlarge(down_grad) * 0.125).astype(
        jnp.bfloat16
    )
    fine_sum, coarse_sum, project_total = sum_over_space(
        fine_total, coarse_total, project_matrix
    )
    fine_sum, coarse_sum = grad_taps(fine_sum), grad_taps(coarse_sum)
    fine_scale = 1.0 / math.sqrt(512.0 * bricks * devices)
    coarse_scale = 1.0 / math.sqrt(512.0 * coarse_bricks * devices)
    fine_weight_grad = fine_sum * fine_scale
    coarse_weight_grad = coarse_sum * coarse_scale
    project_weight_grad = project_total * coarse_scale
    return (out_feats, grad_feats, fine_weight_grad, coarse_weight_grad, project_weight_grad)


def solution(mesh):
    placed = (
        P("space", "chan", None),
        P("space"),
        P("space", None),
        P("space"),
        P(None, "chan", None),
        P(None, "chan", None),
        P(None, "chan"),
        P("space", "chan", None),
    )
    return jax.shard_map(
        per_device,
        mesh=mesh,
        in_specs=placed,
        out_specs=(
            P("space", "chan", None),
            P("space", "chan", None),
            P(None, "chan", None),
            P(None, "chan", None),
            P(None, "chan"),
        ),
        check_vma=False,
    )
```

time: 290 us -> 188 us (0.65)
  waiting for transfers between devices: 91.8 us -> 0.4 us
  Pallas kernels: 28 us -> 67.9 us
  starting transfers between devices: 80.7 us -> 61.4 us
  local copies, waits for them, and re-layouts: 34.7 us -> 18 us
  other arithmetic: 23 us -> 6.68 us
  blocking collectives: 6.01 us -> 10.1 us
    ppermute x24 -> x8, waiting for transfers between devices: 73.2 us -> 0.34 us  [the longest x4 0.33 us: from_sides(): lax.ppermute(rows[:moving], 'space', [(i + 1, i) for i in range(count - 1)])]
    pallas_call x0 -> x1, Pallas kernels: none -> 38.2 us  [sum_tiles(): pl.pallas_call(lambda *refs: sum_kernel(sizes, *refs), in_specs=[pl.Block...]
    reshape x15 -> x3, local copies, waits for them, and re-layouts: 21.6 us -> 0.33 us  [the longest x1 0.13 us: per_device(): down_grad = gather_back(down_source[:bricks], send_pick, from_sides(down_...]
    ppermute x24 -> x8, starting transfers between devices: 60.1 us -> 40.7 us  [the longest x4 33 us: from_sides(): lax.ppermute(rows[:moving], 'space', [(i + 1, i) for i in range(count - 1)])]
    reduce_scatter x2 -> x0, waiting for transfers between devices: 15.4 us -> none  [the longest x1 8.5 us: per_device(): lax.psum_scatter(coarse_terms.astype(jnp.bfloat16), 'chan', scatter_dimen...]
    reshape x4 -> x0, other arithmetic: 11.4 us -> none  [brick_pass(): table = table.reshape(slots + 1, 8, 8, 8, 128)]
    all_gather x1 -> x3, blocking collectives: 2.11 us -> 6.38 us  [the longest x1 2.43 us: per_device(): whole_coarse = lax.all_gather(coarse_weight, 'chan', axis=1, tiled=True)]
    unnamed x16 -> x40, local copies, waits for them, and re-layouts: 0.05 us -> 3.51 us
  transfers between devices with their start and end apart: 32 -> 14, of which waited for: 20 -> 1; matrix products, arithmetic and copies ran while one was open for 16% -> 10% of each run, Pallas kernels for 5% -> 8%
where the time goes in v1:
time: 188 us; the launch traced here: 186 us
  Pallas kernels  67.9 us (36%)
  starting transfers between devices  61.4 us (33%)
  local copies, waits for them, and re-layouts  18 us (10%)
  between operations  15.7 us (8%)
  blocking collectives  10.1 us (5%)
  other arithmetic  6.68 us (4%)
  matrix products  6.22 us (3%)
    pallas_call x1, Pallas kernels, sum_tiles(): pl.pallas_call(lambda *refs: sum_kernel(sizes, *refs), in_specs=[pl.Block...  38.2 us
    ppermute x4, starting transfers between devices, from_sides(): lax.ppermute(rows[:moving], 'space', [(i + 1, i) for i in range(count - 1)])  33 us
    pallas_call x5, Pallas kernels, brick_pass(): pl.pallas_call(lambda *refs: brick_kernel(weight is not None, grad_rows i...  29.7 us
    ppermute x2, starting transfers between devices, around(): high = lax.ppermute(block, 'space', backward)  16.8 us
    ppermute x4, starting transfers between devices, from_sides(): lax.ppermute(rows[moving:], 'space', [(i, i + 1) for i in range(count - 1)])  7.67 us
    ppermute x2, starting transfers between devices, around(): low = lax.ppermute(block, 'space', forward)  3.84 us
  transfers between devices with their start and end apart: 14, of which 1 were waited for; matrix products, arithmetic and copies ran while one was open for 10% of the time, Pallas kernels for 8%

profile of v1, /device:TPU:8, one launch (start us, length us, event | category | flops | bytes accessed | tf_op | source)
XLA Modules:
  0.0 186.4 jit_solution(11636432309444092610)
XLA Ops:
  8.0 1.1 multiply_convert_fusion.refs_4_
  9.1 9.8 %collective-permute-start.7 = (bf16[8,32,512]{2,1,0:T(8,128)(2,1)S(1)}, bf16[8,32,512]{2,1,0:T(8,128)(2,1)}, u32[]{:S(2)}, u32[]{:S(2)}) collective-permute-start(bf16[8,32,512]{2,1,0:T(8,128)(2,1)S(1)} %multiply_convert_fusion.refs_4_), channel_id=1, source_target_pairs={{2,0},{4,2},{6,4},{8,6},{10,8},{12,10},{14,12},{16,14},{18,16},{20... | collective-permute-start | bytes 786440 | tf_op jit(solution)/shard_map/ppermute | solution.py:242
  18.9 1.9 %collective-permute-start.6 = (bf16[8,32,512]{2,1,0:T(8,128)(2,1)S(1)}, bf16[8,32,512]{2,1,0:T(8,128)(2,1)}, u32[]{:S(2)}, u32[]{:S(2)}) collective-permute-start(bf16[8,32,512]{2,1,0:T(8,128)(2,1)S(1)} %multiply_convert_fusion.refs_4_), channel_id=1, source_target_pairs={{0,2},{2,4},{4,6},{6,8},{8,10},{10,12},{12,14},{14,16},{16,18},{18... | collective-permute-start | bytes 786440 | tf_op jit(solution)/shard_map/ppermute | solution.py:241
  21.9 1.2 fusion.11
  24.6 1.9 %collective-permute-start = (bf16[1,2176]{1,0:T(2,128)(2,1)}, bf16[1,2176]{1,0:T(2,128)(2,1)S(1)}, u32[]{:S(2)}, u32[]{:S(2)}) collective-permute-start(bf16[1,2176]{1,0:T(2,128)(2,1)} %get-tuple-element.18), channel_id=1, source_target_pairs={{0,2},{2,4},{4,6},{6,8},{8,10},{10,12},{12,14},{14,16},{16,18},{18... | collective-permute-start | bytes 13064 | tf_op jit(solution)/shard_map/ppermute | solution.py:88
  26.5 8.1 %collective-permute-start.1 = (bf16[1,2176]{1,0:T(2,128)(2,1)S(1)}, bf16[1,2176]{1,0:T(2,128)(2,1)S(1)}, u32[]{:S(2)}, u32[]{:S(2)}) collective-permute-start(bf16[1,2176]{1,0:T(2,128)(2,1)S(1)} %get-tuple-element.19), channel_id=1, source_target_pairs={{2,0},{4,2},{6,4},{8,6},{10,8},{12,10},{14,12},{16,14},{18,16},{20... | collective-permute-start | bytes 13064 | tf_op jit(solution)/shard_map/ppermute | solution.py:89
  35.5 2.1 %all_gather.26 = bf16[27,64,64]{2,1,0:T(8,128)(2,1)S(1)} all-gather(bf16[27,32,64]{2,1,0:T(8,128)(2,1)S(1)} %copy-done.5), channel_id=1, replica_groups=mesh['space'=128,'chan'=2] {'chan'}, dimensions={1}, use_global_device_ids=true | all-gather | bytes 331776 | tf_op jit(solution)/shard_map/all_gather | solution.py:430
  37.7 2.4 %all_gather.22 = bf16[27,128,64]{2,1,0:T(8,128)(2,1)S(1)} all-gather(bf16[27,64,64]{2,1,0:T(8,128)(2,1)S(1)} %copy-done.8), channel_id=1, replica_groups=mesh['space'=128,'chan'=2] {'chan'}, dimensions={1}, use_global_device_ids=true | all-gather | bytes 663552 | tf_op jit(solution)/shard_map/all_gather | solution.py:428
  44.8 1.8 all_gather.23
  47.4 1.9 all-gather
  49.2 1.6 shard_map.263
  50.9 2.0 %pad_maximum_fusion.2 = bf16[24,32,512]{2,1,0:T(8,128)(2,1)} fusion(bf16[8,32,512]{2,1,0:T(8,128)(2,1)} %collective-permute-done.7, bf16[8,32,512]{2,1,0:T(8,128)(2,1)S(1)} %multiply_convert_fusion.refs_4_, bf16[8,32,512]{2,1,0:T(8,128)(2,1)} %collective-permute-done.6), kind=kLoop, calls=%fused_computation.45 | loop fusion | flops 786432 | bytes 1572864 | tf_op jit(solution)/shard_map/concatenate | solution.py:243
  54.0 1.9 %collective-permute-start.2 = (bf16[1,2048]{1,0:T(2,128)(2,1)S(1)}, bf16[1,2048]{1,0:T(2,128)(2,1)S(1)}, u32[]{:S(2)}, u32[]{:S(2)}) collective-permute-start(bf16[1,2048]{1,0:T(2,128)(2,1)S(1)} %get-tuple-element.16), channel_id=1, source_target_pairs={{0,2},{2,4},{4,6},{6,8},{8,10},{10,12},{12,14},{14,16},{16,18},{18... | collective-permute-start | bytes 12296 | tf_op jit(solution)/shard_map/ppermute | solution.py:88
  55.9 8.1 %collective-permute-start.3 = (bf16[1,2048]{1,0:T(2,128)(2,1)S(1)}, bf16[1,2048]{1,0:T(2,128)(2,1)}, u32[]{:S(2)}, u32[]{:S(2)}) collective-permute-start(bf16[1,2048]{1,0:T(2,128)(2,1)S(1)} %get-tuple-element.17), channel_id=1, source_target_pairs={{2,0},{4,2},{6,4},{8,6},{10,8},{12,10},{14,12},{16,14},{18,16},{20... | collective-permute-start | bytes 12296 | tf_op jit(solution)/shard_map/ppermute | solution.py:89
  66.9 0.9 fusion
  68.2 7.0 %collective-permute-start.5 = (bf16[8,32,512]{2,1,0:T(8,128)(2,1)S(1)}, bf16[8,32,512]{2,1,0:T(8,128)(2,1)S(1)}, u32[]{:S(2)}, u32[]{:S(2)}) collective-permute-start(bf16[8,32,512]{2,1,0:T(8,128)(2,1)S(1)} %fusion.4), channel_id=1, source_target_pairs={{2,0},{4,2},{6,4},{8,6},{10,8},{12,10},{14,12},{16,14},{18,16},{20... | collective-permute-start | bytes 786440 | tf_op jit(solution)/shard_map/ppermute | solution.py:242
  75.2 1.9 %collective-permute-start.4 = (bf16[8,32,512]{2,1,0:T(8,128)(2,1)S(1)}, bf16[8,32,512]{2,1,0:T(8,128)(2,1)S(1)}, u32[]{:S(2)}, u32[]{:S(2)}) collective-permute-start(bf16[8,32,512]{2,1,0:T(8,128)(2,1)S(1)} %fusion.4), channel_id=1, source_target_pairs={{0,2},{2,4},{4,6},{6,8},{8,10},{10,12},{12,14},{14,16},{16,18},{18... | collective-permute-start | bytes 786440 | tf_op jit(solution)/shard_map/ppermute | solution.py:241
  77.2 1.4 copy-done.1
  78.6 10.1 %shard_map.265 = bf16[8,32,512]{2,1,0:T(8,128)(2,1)S(1)} custom-call(s32[8,27]{1,0:T(8,128)S(1)} %pad_add_fusion.refs_0_, s32[1]{0:T(128)} %copy.82.refs_1_, bf16[24,64,512]{2,1,0:T(8,128)(2,1)S(1)} %copy-done.1, bf16[1,3,32,768]{3,2,1,0:T(8,128)(2,1)S(1)} %stack_reshape.17.refs_3_), custom_call_target="tpu_custom_call" | custom-call | flops 603979776 | bytes 1572864 | tf_op jit(solution)/shard_map/pallas_call | solution.py:202
  89.1 1.9 %collective-permute-start.8 = (bf16[1,2048]{1,0:T(2,128)(2,1)S(1)}, bf16[1,2048]{1,0:T(2,128)(2,1)S(1)}, u32[]{:S(2)}, u32[]{:S(2)}) collective-permute-start(bf16[1,2048]{1,0:T(2,128)(2,1)S(1)} %get-tuple-element.20), channel_id=1, source_target_pairs={{0,2},{2,4},{4,6},{6,8},{8,10},{10,12},{12,14},{14,16},{16,18},{18... | collective-permute-start | bytes 12296 | tf_op jit(solution)/shard_map/ppermute | solution.py:88
  91.1 8.1 %collective-permute-start.9 = (bf16[1,2048]{1,0:T(2,128)(2,1)S(1)}, bf16[1,2048]{1,0:T(2,128)(2,1)S(1)}, u32[]{:S(2)}, u32[]{:S(2)}) collective-permute-start(bf16[1,2048]{1,0:T(2,128)(2,1)S(1)} %get-tuple-element.21), channel_id=1, source_target_pairs={{2,0},{4,2},{6,4},{8,6},{10,8},{12,10},{14,12},{16,14},{18,16},{20... | collective-permute-start | bytes 12296 | tf_op jit(solution)/shard_map/ppermute | solution.py:89
  99.2 1.0 pad_maximum_fusion.1
  101.1 1.9 all-gather.1
  103.1 2.5 %shard_map.266 = f32[2,32,512]{2,1,0:T(8,128)S(1)} custom-call(s32[2,27]{1,0:T(2,128)S(1)} %iota_select_fusion.refs_0_, s32[1]{0:T(128)} %copy.82.refs_1_, bf16[2,64,512]{2,1,0:T(8,128)(2,1)S(1)} %bitcast.156, bf16[2,3,32,768]{3,2,1,0:T(8,128)(2,1)S(1)} %pad_maximum_fusion.3.refs_3_), custom_call_target="tpu_custom_call" | custom-call | flops 150994944 | bytes 131072 | tf_op jit(solution)/shard_map/pallas_call | solution.py:202
  106.4 1.9 %collective-permute-start.10 = (bf16[1,2048]{1,0:T(2,128)(2,1)S(1)}, bf16[1,2048]{1,0:T(2,128)(2,1)S(1)}, u32[]{:S(2)}, u32[]{:S(2)}) collective-permute-start(bf16[1,2048]{1,0:T(2,128)(2,1)S(1)} %get-tuple-element.14), channel_id=1, source_target_pairs={{0,2},{2,4},{4,6},{6,8},{8,10},{10,12},{12,14},{14,16},{16,18},{18... | collective-permute-start | bytes 12296 | tf_op jit(solution)/shard_map/ppermute | solution.py:88
  108.3 8.6 %collective-permute-start.11 = (bf16[1,2048]{1,0:T(2,128)(2,1)S(1)}, bf16[1,2048]{1,0:T(2,128)(2,1)S(1)}, u32[]{:S(2)}, u32[]{:S(2)}) collective-permute-start(bf16[1,2048]{1,0:T(2,128)(2,1)S(1)} %get-tuple-element.15), channel_id=1, source_target_pairs={{2,0},{4,2},{6,4},{8,6},{10,8},{12,10},{14,12},{16,14},{18,16},{20... | collective-permute-start | bytes 12296 | tf_op jit(solution)/shard_map/ppermute | solution.py:89
  117.1 1.3 shard_map.267
  118.8 0.9 add_convert_fusion
  119.7 1.4 copy-done
  121.1 14.3 %shard_map.264 = (bf16[8,32,512]{2,1,0:T(8,128)(2,1)}, f32[3,32,768]{2,1,0:T(8,128)S(1)}) custom-call(s32[8,27]{1,0:T(8,128)S(1)} %pad_add_fusion.refs_0_, s32[1]{0:T(128)} %copy.82.refs_1_, bf16[24,64,512]{2,1,0:T(8,128)(2,1)S(1)} %copy-done, bf16[1,3,32,768]{3,2,1,0:T(8,128)(2,1)S(1)} %stack_reshape.16.refs_3_, ...), custom_call_target="tpu_custom_call" | custom-call | flops 1207959552 | bytes 1572864 | tf_op jit(solution)/shard_map/pallas_call | solution.py:202
  135.8 38.2 %shard_map.268 = f32[2,4,4,8,1,8,128]{6,5,4,3,2,1,0:T(8,128)S(1)} custom-call(f32[2,4,4,8,1,8,128]{6,5,4,3,2,1,0:T(8,128)S(1)} %bitcast.149), custom_call_target="tpu_custom_call" | custom-call | flops 1048576 | bytes 8388608 | tf_op jit(solution)/shard_map/pallas_call | solution.py:372
  178.6 1.0 copy.76
  (154 shorter events, 20.5 us)
Async XLA Ops:
  7.2 27.7 %copy-start.18 = (s32[3]{0:T(128)S(1)}, s32[3]{0:T(128)}, u32[]{:S(2)}) copy-start(s32[3]{0:T(128)} %constant.122) | copy-start | bytes 40
  7.2 27.6 %copy-start.13 = (s32[8,26]{1,0:T(8,128)S(1)}, s32[8,26]{1,0:T(8,128)}, u32[]{:S(2)}) copy-start(s32[8,26]{1,0:T(8,128)} %param.26) | copy-start | bytes 2500
  7.2 28.2 %copy-start.9 = (bf16[64,64]{1,0:T(8,128)(2,1)S(1)}, bf16[64,64]{1,0:T(8,128)(2,1)}, u32[]{:S(2)}) copy-start(bf16[64,64]{1,0:T(8,128)(2,1)} %param.30) | copy-start | bytes 24580
  7.2 28.3 %copy-start.5 = (bf16[27,32,64]{2,1,0:T(8,128)(2,1)S(1)}, bf16[27,32,64]{2,1,0:T(8,128)(2,1)}, u32[]{:S(2)}) copy-start(bf16[27,32,64]{2,1,0:T(8,128)(2,1)} %param.28) | copy-start | bytes 331780
  7.2 30.5 %copy-start.8 = (bf16[27,64,64]{2,1,0:T(8,128)(2,1)S(1)}, bf16[27,64,64]{2,1,0:T(8,128)(2,1)}, u32[]{:S(2)}) copy-start(bf16[27,64,64]{2,1,0:T(8,128)(2,1)} %param.29) | copy-start | bytes 663556
  7.2 69.9 %all-gather.7.cloned.1.call-start = ((), (), s32[]{:S(2)}) async-start(), calls=%async_computation.1 | async-start | bytes 2359296 | tf_op jit(solution)/shard_map/all_gather | solution.py:475
  8.0 12.9 %copy-start.11 = (f32[8]{0:T(128)}, f32[8]{0:T(128)S(1)}, u32[]{:S(2)}) copy-start(f32[8]{0:T(128)S(1)} %compare_convert_fusion.2) | copy-start | bytes 100
  9.1 41.8 %collective-permute-start.7 = (bf16[8,32,512]{2,1,0:T(8,128)(2,1)S(1)}, bf16[8,32,512]{2,1,0:T(8,128)(2,1)}, u32[]{:S(2)}, u32[]{:S(2)}) collective-permute-start(bf16[8,32,512]{2,1,0:T(8,128)(2,1)S(1)} %multiply_convert_fusion.refs_4_), channel_id=1, source_target_pairs={{2,0},{4,2},{6,4},{8,6},{10,8},{12,10},{14,12},{16,14},{18,16},{20... | collective-permute-start | bytes 786440 | tf_op jit(solution)/shard_map/ppermute | solution.py:242
  18.9 31.9 %collective-permute-start.6 = (bf16[8,32,512]{2,1,0:T(8,128)(2,1)S(1)}, bf16[8,32,512]{2,1,0:T(8,128)(2,1)}, u32[]{:S(2)}, u32[]{:S(2)}) collective-permute-start(bf16[8,32,512]{2,1,0:T(8,128)(2,1)S(1)} %multiply_convert_fusion.refs_4_), channel_id=1, source_target_pairs={{0,2},{2,4},{4,6},{6,8},{8,10},{10,12},{12,14},{14,16},{16,18},{18... | collective-permute-start | bytes 786440 | tf_op jit(solution)/shard_map/ppermute | solution.py:241
  24.6 22.0 %collective-permute-start = (bf16[1,2176]{1,0:T(2,128)(2,1)}, bf16[1,2176]{1,0:T(2,128)(2,1)S(1)}, u32[]{:S(2)}, u32[]{:S(2)}) collective-permute-start(bf16[1,2176]{1,0:T(2,128)(2,1)} %get-tuple-element.18), channel_id=1, source_target_pairs={{0,2},{2,4},{4,6},{6,8},{8,10},{10,12},{12,14},{14,16},{16,18},{18... | collective-permute-start | bytes 13064 | tf_op jit(solution)/shard_map/ppermute | solution.py:88
  26.5 20.1 %collective-permute-start.1 = (bf16[1,2176]{1,0:T(2,128)(2,1)S(1)}, bf16[1,2176]{1,0:T(2,128)(2,1)S(1)}, u32[]{:S(2)}, u32[]{:S(2)}) collective-permute-start(bf16[1,2176]{1,0:T(2,128)(2,1)S(1)} %get-tuple-element.19), channel_id=1, source_target_pairs={{2,0},{4,2},{6,4},{8,6},{10,8},{12,10},{14,12},{16,14},{18,16},{20... | collective-permute-start | bytes 13064 | tf_op jit(solution)/shard_map/ppermute | solution.py:89
  35.4 7.9 %copy-start.10 = (s32[1024]{0:T(1024)}, s32[1024]{0:T(1024)S(1)}, u32[]{:S(2)}) copy-start(s32[1024]{0:T(1024)S(1)} %get-tuple-element.25) | copy-start | bytes 12292
  44.4 2.7 %copy-start.2 = (bf16[8,64,512]{2,1,0:T(8,128)(2,1)S(1)}, bf16[8,64,512]{2,1,0:T(8,128)(2,1)}, u32[]{:S(2)}) copy-start(bf16[8,64,512]{2,1,0:T(8,128)(2,1)} %constant.120) | copy-start | bytes 1572868
  46.9 6.9 %copy-start.14 = (s32[10]{0:T(128)}, s32[10]{0:T(128)S(1)}, u32[]{:S(2)}) copy-start(s32[10]{0:T(128)S(1)} %pad_add_fusion.1) | copy-start | bytes 124
  52.9 66.8 %all-gather.5.cloned.1.call-start = ((), (), s32[]{:S(2)}) async-start(), calls=%async_computation | async-start | bytes 2359296 | tf_op jit(solution)/shard_map/all_gather | solution.py:480
  53.0 11.9 %copy-start.6 = (bf16[1,128,512]{2,1,0:T(8,128)(2,1)}, bf16[1,128,512]{2,1,0:T(8,128)(2,1)S(1)}, u32[]{:S(2)}) copy-start(bf16[1,128,512]{2,1,0:T(8,128)(2,1)S(1)} %multiply_convert_fusion.1) | copy-start | bytes 393220
  54.0 13.0 %collective-permute-start.2 = (bf16[1,2048]{1,0:T(2,128)(2,1)S(1)}, bf16[1,2048]{1,0:T(2,128)(2,1)S(1)}, u32[]{:S(2)}, u32[]{:S(2)}) collective-permute-start(bf16[1,2048]{1,0:T(2,128)(2,1)S(1)} %get-tuple-element.16), channel_id=1, source_target_pairs={{0,2},{2,4},{4,6},{6,8},{8,10},{10,12},{12,14},{14,16},{16,18},{18... | collective-permute-start | bytes 12296 | tf_op jit(solution)/shard_map/ppermute | solution.py:88
  55.9 11.0 %collective-permute-start.3 = (bf16[1,2048]{1,0:T(2,128)(2,1)S(1)}, bf16[1,2048]{1,0:T(2,128)(2,1)}, u32[]{:S(2)}, u32[]{:S(2)}) collective-permute-start(bf16[1,2048]{1,0:T(2,128)(2,1)S(1)} %get-tuple-element.17), channel_id=1, source_target_pairs={{2,0},{4,2},{6,4},{8,6},{10,8},{12,10},{14,12},{16,14},{18,16},{20... | collective-permute-start | bytes 12296 | tf_op jit(solution)/shard_map/ppermute | solution.py:89
  65.3 1.6 copy-start.17
  65.5 2.4 %copy-start.3 = (bf16[8,32,512]{2,1,0:T(8,128)(2,1)S(1)}, bf16[8,32,512]{2,1,0:T(8,128)(2,1)}, u32[]{:S(2)}) copy-start(bf16[8,32,512]{2,1,0:T(8,128)(2,1)} %param.24) | copy-start | bytes 786436
  65.5 2.4 %copy-start.4 = (bf16[512,64,1]{0,1,2:T(8,128)(2,1)S(1)}, bf16[512,64,1]{0,1,2:T(8,128)(2,1)}, u32[]{:S(2)}) copy-start(bf16[512,64,1]{0,1,2:T(8,128)(2,1)} %constant.129) | copy-start | bytes 196612
  65.5 2.4 %copy-start.12 = (f32[8]{0:T(128)S(1)}, f32[8]{0:T(128)}, u32[]{:S(2)}) copy-start(f32[8]{0:T(128)} %copy-done.11) | copy-start | bytes 100
  68.2 31.0 %collective-permute-start.5 = (bf16[8,32,512]{2,1,0:T(8,128)(2,1)S(1)}, bf16[8,32,512]{2,1,0:T(8,128)(2,1)S(1)}, u32[]{:S(2)}, u32[]{:S(2)}) collective-permute-start(bf16[8,32,512]{2,1,0:T(8,128)(2,1)S(1)} %fusion.4), channel_id=1, source_target_pairs={{2,0},{4,2},{6,4},{8,6},{10,8},{12,10},{14,12},{16,14},{18,16},{20... | collective-permute-start | bytes 786440 | tf_op jit(solution)/shard_map/ppermute | solution.py:242
  75.2 24.1 %collective-permute-start.4 = (bf16[8,32,512]{2,1,0:T(8,128)(2,1)S(1)}, bf16[8,32,512]{2,1,0:T(8,128)(2,1)S(1)}, u32[]{:S(2)}, u32[]{:S(2)}) collective-permute-start(bf16[8,32,512]{2,1,0:T(8,128)(2,1)S(1)} %fusion.4), channel_id=1, source_target_pairs={{0,2},{2,4},{4,6},{6,8},{8,10},{10,12},{12,14},{14,16},{16,18},{18... | collective-permute-start | bytes 786440 | tf_op jit(solution)/shard_map/ppermute | solution.py:241
  77.1 1.4 copy-start.1
  89.1 11.1 %collective-permute-start.8 = (bf16[1,2048]{1,0:T(2,128)(2,1)S(1)}, bf16[1,2048]{1,0:T(2,128)(2,1)S(1)}, u32[]{:S(2)}, u32[]{:S(2)}) collective-permute-start(bf16[1,2048]{1,0:T(2,128)(2,1)S(1)} %get-tuple-element.20), channel_id=1, source_target_pairs={{0,2},{2,4},{4,6},{6,8},{8,10},{10,12},{12,14},{14,16},{16,18},{18... | collective-permute-start | bytes 12296 | tf_op jit(solution)/shard_map/ppermute | solution.py:88
  91.1 9.5 %copy-start.15 = (s32[10]{0:T(128)S(1)}, s32[10]{0:T(128)}, u32[]{:S(2)}) copy-start(s32[10]{0:T(128)} %copy-done.14) | copy-start | bytes 124
  91.1 9.5 %collective-permute-start.9 = (bf16[1,2048]{1,0:T(2,128)(2,1)S(1)}, bf16[1,2048]{1,0:T(2,128)(2,1)S(1)}, u32[]{:S(2)}, u32[]{:S(2)}) collective-permute-start(bf16[1,2048]{1,0:T(2,128)(2,1)S(1)} %get-tuple-element.21), channel_id=1, source_target_pairs={{2,0},{4,2},{6,4},{8,6},{10,8},{12,10},{14,12},{16,14},{18,16},{20... | collective-permute-start | bytes 12296 | tf_op jit(solution)/shard_map/ppermute | solution.py:89
  103.1 13.8 %copy-start.7 = (bf16[1,128,512]{2,1,0:T(8,128)(2,1)S(1)}, bf16[1,128,512]{2,1,0:T(8,128)(2,1)}, u32[]{:S(2)}) copy-start(bf16[1,128,512]{2,1,0:T(8,128)(2,1)} %copy-done.6) | copy-start | bytes 393220
  106.4 12.1 %collective-permute-start.10 = (bf16[1,2048]{1,0:T(2,128)(2,1)S(1)}, bf16[1,2048]{1,0:T(2,128)(2,1)S(1)}, u32[]{:S(2)}, u32[]{:S(2)}) collective-permute-start(bf16[1,2048]{1,0:T(2,128)(2,1)S(1)} %get-tuple-element.14), channel_id=1, source_target_pairs={{0,2},{2,4},{4,6},{6,8},{8,10},{10,12},{12,14},{14,16},{16,18},{18... | collective-permute-start | bytes 12296 | tf_op jit(solution)/shard_map/ppermute | solution.py:88
  108.3 10.1 %collective-permute-start.11 = (bf16[1,2048]{1,0:T(2,128)(2,1)S(1)}, bf16[1,2048]{1,0:T(2,128)(2,1)S(1)}, u32[]{:S(2)}, u32[]{:S(2)}) collective-permute-start(bf16[1,2048]{1,0:T(2,128)(2,1)S(1)} %get-tuple-element.15), channel_id=1, source_target_pairs={{2,0},{4,2},{6,4},{8,6},{10,8},{12,10},{14,12},{16,14},{18,16},{20... | collective-permute-start | bytes 12296 | tf_op jit(solution)/shard_map/ppermute | solution.py:89
  119.7 1.4 copy-start
  (1 other events, 0.6 us)
Sparse Core Ops, SparseCore 0:
  53.0 10.4 all-gather.6
  100.4 10.5 all-gather.4

commit v2 on v1

--- a/solution.py
+++ b/solution.py
@@ -83,18 +83,17 @@
     ).astype(jnp.int32)
 
 
-def from_sides(rows, moving):
-    count = lax.axis_size("space")
-    low = lax.ppermute(rows[moving:], "space", [(i, i + 1) for i in range(count - 1)])
-    high = lax.ppermute(rows[:moving], "space", [(i + 1, i) for i in range(count - 1)])
-    return jnp.concatenate([low, high], axis=0)
-
-
 def lone_bricks(amount):
     centre = jnp.arange(27, dtype=jnp.int32)[None, :] == 13
     return jnp.where(centre, jnp.arange(amount, dtype=jnp.int32)[:, None], amount)
 
 
+def select_both(picker, body, moved):
+    values = jnp.concatenate([body.reshape(2, -1, 2048), moved], axis=1)
+    picked = jnp.einsum("rs,csv->rcv", picker, values, preferred_element_type=jnp.float32)
+    return picked.astype(jnp.bfloat16).reshape(picker.shape[0], -1, 64)
+
+
 def gather_back(local_part, send_pick, returned):
     total = local_part.astype(jnp.float32) + jnp.dot(
         send_pick.T, returned, preferred_element_type=jnp.float32
@@ -106,29 +105,162 @@
 KZ_ORDER = np.array([1, 0, 2])
 
 
-def brick_kernel(with_conv, with_grad, masked, *refs):
+def greet(devices):
+    barrier = pltpu.get_barrier_semaphore()
+    for device in devices:
+        pl.semaphore_signal(
+            barrier, inc=1, device_id=device, device_id_type=pl.DeviceIdType.MESH
+        )
+    pl.semaphore_wait(barrier, len(devices))
+
+
+def nearby(count):
+    me, core = lax.axis_index("space"), lax.axis_index("chan")
+    return ((me + count - 1) % count, core), ((me + 1) % count, core), (me, 1 - core)
+
+
+def sender(send_sems, recv_sems):
+    def send(number, source, target, device):
+        copy = pltpu.make_async_remote_copy(
+            src_ref=source,
+            dst_ref=target,
+            send_sem=send_sems.at[number],
+            recv_sem=recv_sems.at[number],
+            device_id=device,
+            device_id_type=pl.DeviceIdType.MESH,
+        )
+        copy.start()
+        return copy
+
+    return send
+
+
+def trade_kernel(count, amount, *refs):
+    rows, own = refs[:2]
+    shares = refs[2 : 2 + amount]
+    rows_all, fields = refs[2 + amount : 4 + amount]
+    shares_all = refs[4 + amount : 4 + 2 * amount]
+    send_sems, recv_sems = refs[4 + 2 * amount :]
+    core = lax.axis_index("chan")
+    left, right, mate = nearby(count)
+    left_mate, right_mate = (left[0], 1 - core), (right[0], 1 - core)
+    greet((left, right, mate, left_mate, right_mate))
+    send = sender(send_sems, recv_sems)
+    quick = [
+        send(0, rows.at[0], rows_all.at[core, 1], left),
+        send(1, rows.at[1], rows_all.at[core, 0], right),
+        send(2, rows.at[0], rows_all.at[core, 1], left_mate),
+        send(3, rows.at[1], rows_all.at[core, 0], right_mate),
+    ]
+    to_right = send(4, own, fields.at[core, 0], right)
+    to_left = send(5, own, fields.at[core, 2], left)
+    for number, (share, share_all) in enumerate(zip(shares, shares_all)):
+        quick.append(send(8 + number, share, share_all.at[core], mate))
+        share_all[core] = share[...]
+    quick.append(send(8 + amount, own, fields.at[core, 1], mate))
+    fields[core, 1] = own[...]
+    to_right.wait_recv()
+    quick.append(send(6, fields.at[core, 0], fields.at[core, 0], mate))
+    to_left.wait_recv()
+    quick.append(send(7, fields.at[core, 2], fields.at[core, 2], mate))
+    for copy in quick:
+        copy.wait_recv()
+    for copy in quick + [to_right, to_left]:
+        copy.wait_send()
+
+
+def trade(rows, own, shares, number):
+    count = lax.axis_size("space")
+    amount = len(shares)
+    shapes = [(2,) + rows.shape, (2, 3) + own.shape] + [(2,) + share.shape for share in shares]
+    return pl.pallas_call(
+        lambda *refs: trade_kernel(count, amount, *refs),
+        in_specs=[pl.BlockSpec(memory_space=pltpu.VMEM)] * (2 + amount),
+        out_specs=[pl.BlockSpec(memory_space=pltpu.VMEM)] * (2 + amount),
+        out_shape=[jax.ShapeDtypeStruct(shape, rows.dtype) for shape in shapes],
+        scratch_shapes=[
+            pltpu.SemaphoreType.DMA((9 + amount,)),
+            pltpu.SemaphoreType.DMA((9 + amount,)),
+        ],
+        compiler_params=pltpu.CompilerParams(
+            collective_id=number, has_side_effects=True, vmem_limit_bytes=32 * 1024 * 1024
+        ),
+    )(rows, own, *shares)
+
+
+def ride_along(count, ride, ride_out, ride_in, send_sems, recv_sems):
+    brick = pl.program_id(0)
+    left, right, _ = nearby(count)
+
+    def copies():
+        return [
+            pltpu.make_async_remote_copy(
+                src_ref=ride.at[side],
+                dst_ref=ride_in.at[1 - side],
+                send_sem=send_sems.at[side],
+                recv_sem=recv_sems.at[side],
+                device_id=device,
+                device_id_type=pl.DeviceIdType.MESH,
+            )
+            for side, device in enumerate((left, right))
+        ]
+
+    @pl.when(brick == 0)
+    def hail():
+        barrier = pltpu.get_barrier_semaphore()
+        for device in (left, right):
+            pl.semaphore_signal(
+                barrier, inc=1, device_id=device, device_id_type=pl.DeviceIdType.MESH
+            )
+
+    @pl.when(brick == 1)
+    def depart():
+        pl.semaphore_wait(pltpu.get_barrier_semaphore(), 2)
+        for copy in copies():
+            copy.start()
+
+    @pl.when(brick == pl.num_programs(0) - 1)
+    def arrive():
+        for copy in copies():
+            copy.wait()
+        ride_out[...] = ride_in[...]
+
+
+def brick_kernel(count, with_conv, with_grad, masked, *refs):
     refs = list(refs)
     near_ref, live_ref, field_ref = refs[:3]
     del refs[:3]
     weight_ref = refs.pop(0) if with_conv else None
     grad_ref = refs.pop(0) if with_grad else None
+    ride_ref = refs.pop(0) if count else None
     out_ref = refs.pop(0) if with_conv else None
     total_ref = refs.pop(0) if with_grad else None
-    table, padded, columns = refs
+    ride_out = refs.pop(0) if count else None
+    table, padded, columns = refs[:3]
     brick = pl.program_id(0)
+    if count:
+        ride_along(count, ride_ref, ride_out, *refs[3:])
 
     @pl.when(brick == 0)
     def fill():
-        slots = field_ref.shape[0]
+        slots = table.shape[0] - 1
+        table[slots] = jnp.zeros((8, 8, 8, 128), jnp.float32)
+        halves = len(field_ref.shape) == 5
+        amount = field_ref.shape[2]
 
         def turn(slot, carry):
-            field = field_ref[slot].astype(jnp.float32)
+            if halves:
+                place, one = slot // amount, slot % amount
+                field = jnp.concatenate(
+                    [field_ref[0, place, one], field_ref[1, place, one]], axis=0
+                ).astype(jnp.float32)
+            else:
+                field = field_ref[slot].astype(jnp.float32)
             turned = jnp.concatenate([field, field], axis=0).T
             table[slot] = turned.reshape(8, 8, 8, 128)
             return carry
 
         lax.fori_loop(0, slots, turn, 0)
-        table[slots] = jnp.zeros((8, 8, 8, 128), jnp.float32)
 
     for index, (lean_x, lean_y, lean_z) in enumerate(lean_list()):
         slot = near_ref[brick, index]
@@ -176,15 +308,18 @@
             )
 
 
-def brick_pass(field_in, near, live_count, weight, grad_rows, out_dtype, masked):
+def brick_pass(
+    field_in, near, live_count, weight, grad_rows, out_dtype, masked, ride=None, number=None
+):
     amount = near.shape[0]
-    slots = field_in.shape[0]
+    count = 0 if ride is None else lax.axis_size("space")
+    slots = 3 * field_in.shape[2] if field_in.ndim == 5 else field_in.shape[0]
     rows = weight.shape[2] if weight is not None else grad_rows.shape[1]
     operands = [near, live_count, field_in]
     in_specs = [
         pl.BlockSpec(memory_space=pltpu.SMEM),
         pl.BlockSpec(memory_space=pltpu.SMEM),
-        pl.BlockSpec((slots, 64, 512), lambda b: (0, 0, 0)),
+        pl.BlockSpec(field_in.shape, lambda b: (0,) * field_in.ndim),
     ]
     outs, out_specs = [], []
     if weight is not None:
@@ -198,19 +333,31 @@
         in_specs.append(pl.BlockSpec((1, rows, 512), lambda b: (b, 0, 0)))
         outs.append(jax.ShapeDtypeStruct((3, rows, 768), jnp.float32))
         out_specs.append(pl.BlockSpec((3, rows, 768), lambda b: (0, 0, 0)))
+    scratch = [
+        pltpu.VMEM((slots + 1, 8, 8, 8, 128), jnp.float32),
+        pltpu.VMEM((3, 10, 10, 8, 128), jnp.float32),
+        pltpu.VMEM((640, 768), jnp.bfloat16),
+    ]
+    if count:
+        operands.append(ride)
+        in_specs.append(pl.BlockSpec(ride.shape, lambda b: (0, 0, 0)))
+        outs.append(jax.ShapeDtypeStruct(ride.shape, ride.dtype))
+        out_specs.append(pl.BlockSpec(ride.shape, lambda b: (0, 0, 0)))
+        scratch += [
+            pltpu.VMEM(ride.shape, ride.dtype),
+            pltpu.SemaphoreType.DMA((2,)),
+            pltpu.SemaphoreType.DMA((2,)),
+        ]
+    remote = {"collective_id": number, "has_side_effects": True} if count else {}
     products = (weight is not None) + (grad_rows is not None)
     return pl.pallas_call(
-        lambda *refs: brick_kernel(weight is not None, grad_rows is not None, masked, *refs),
+        lambda *refs: brick_kernel(count, weight is not None, grad_rows is not None, masked, *refs),
         grid=(amount,),
         in_specs=in_specs,
         out_specs=out_specs,
         out_shape=outs,
-        scratch_shapes=[
-            pltpu.VMEM((slots + 1, 8, 8, 8, 128), jnp.float32),
-            pltpu.VMEM((3, 10, 10, 8, 128), jnp.float32),
-            pltpu.VMEM((640, 768), jnp.bfloat16),
-        ],
-        compiler_params=pltpu.CompilerParams(vmem_limit_bytes=48 * 1024 * 1024),
+        scratch_shapes=scratch,
+        compiler_params=pltpu.CompilerParams(vmem_limit_bytes=48 * 1024 * 1024, **remote),
         cost_estimate=pl.CostEstimate(
             flops=amount * products * 2 * rows * 2304 * 512,
             bytes_accessed=slots * 64 * 512 * 2,
@@ -225,22 +372,6 @@
     taps = jnp.concatenate([taps, jnp.zeros_like(taps[:, :1])], axis=1)
     taps = taps.reshape(3, 3, 4, rows, channels)
     return jnp.transpose(taps, (0, 3, 1, 2, 4)).reshape(3, rows, 768)
-
-
-def grad_taps(total):
-    rows = total.shape[1]
-    taps = total.reshape(3, rows, 3, 4, 64)
-    taps = jnp.transpose(taps, (0, 2, 3, 1, 4)).reshape(9, 4, rows, 64)[:, KZ_ORDER]
-    return taps.reshape(27, rows, 64)
-
-
-def around(block):
-    count = lax.axis_size("space")
-    forward = [(i, i + 1) for i in range(count - 1)]
-    backward = [(i + 1, i) for i in range(count - 1)]
-    low = lax.ppermute(block, "space", forward)
-    high = lax.ppermute(block, "space", backward)
-    return jnp.concatenate([low, block, high], axis=0)
 
 
 def torus_sizes(count):
@@ -393,23 +524,43 @@
     return summed.reshape(tiles.shape)
 
 
-def sum_over_space(fine, coarse, project):
+def finish_kernel(places, tiles, *outs):
+    for (start, scale), out in zip(places, outs):
+        blocks = out.shape[1] // 8
+        for tap_x in range(3):
+            for block in range(blocks):
+                first = start + 6 * (tap_x * blocks + block)
+                for tap_y in range(3):
+                    pair = tiles[first + 2 * tap_y]
+                    last = tiles[first + 2 * tap_y + 1]
+                    rows = slice(8 * block, 8 * block + 8)
+                    tap = 9 * tap_x + 3 * tap_y
+                    out[tap, rows, :] = pair[:, 64:] * scale
+                    out[tap + 1, rows, :] = pair[:, :64] * scale
+                    out[tap + 2, rows, :] = last[:, :64] * scale
+
+
+def sum_over_space(fine, coarse, project, fine_scale, coarse_scale):
     wide = jnp.concatenate([fine.reshape(-1, 768), coarse.reshape(-1, 768)], axis=0)
     tiles = jnp.transpose(wide.reshape(-1, 8, 6, 128), (0, 2, 1, 3)).reshape(-1, 8, 128)
     small = project.reshape(-1, 8, 128)
     count = lax.axis_size("space")
+    fine_tiles = 3 * fine.shape[1] // 8 * 6
     used = tiles.shape[0] + small.shape[0]
     spare = -used % (2 * count)
     tiles = jnp.concatenate([tiles, small, jnp.zeros((spare, 8, 128), jnp.float32)], axis=0)
     tiles = sum_tiles(tiles)
-    wide_tiles = wide.shape[0] // 8 * 6
-    wide = jnp.transpose(tiles[:wide_tiles].reshape(-1, 6, 8, 128), (0, 2, 1, 3)).reshape(-1, 768)
-    fine_rows = 3 * fine.shape[1]
-    return (
-        wide[:fine_rows].reshape(fine.shape),
-        wide[fine_rows:].reshape(coarse.shape),
-        tiles[wide_tiles:used].reshape(project.shape),
-    )
+    places = ((0, fine_scale), (fine_tiles, coarse_scale))
+    fine_sum, coarse_sum = pl.pallas_call(
+        lambda *refs: finish_kernel(places, *refs),
+        in_specs=[pl.BlockSpec(memory_space=pltpu.VMEM)],
+        out_specs=[pl.BlockSpec(memory_space=pltpu.VMEM)] * 2,
+        out_shape=[
+            jax.ShapeDtypeStruct((27, fine.shape[1], 64), jnp.float32),
+            jax.ShapeDtypeStruct((27, coarse.shape[1], 64), jnp.float32),
+        ],
+    )(tiles)
+    return fine_sum, coarse_sum, tiles[used - small.shape[0] : used].reshape(project.shape)
 
 
 def per_device(
@@ -425,28 +576,34 @@
         :, None, None
     ]
     core = lax.axis_index("chan")
-    whole_coarse = lax.all_gather(coarse_weight, "chan", axis=1, tiled=True)
-    whole_project = lax.all_gather(project_weight, "chan", axis=1, tiled=True)
-    whole_fine = lax.all_gather(fine_weight, "chan", axis=1, tiled=True)
     send_place = route_places(parent, own_index, moving, bricks)
     send_pick = (jnp.arange(2 * moving, dtype=jnp.int32)[:, None] == send_place[None, :]).astype(
         jnp.bfloat16
     )
     pooled = (pool_sum(feats) * 0.125 * live_mask).astype(jnp.bfloat16).reshape(bricks, -1)
     slot_rows = jnp.broadcast_to(
-        (parent % bricks + 1).astype(jnp.bfloat16)[:, None], (bricks, 128)
+        (parent % bricks + 1).astype(jnp.bfloat16)[:, None], (bricks, 2048)
     )
     outgoing = select_rows(send_pick, jnp.concatenate([pooled, slot_rows], axis=1))
-    incoming = from_sides(outgoing, moving)
-    incoming_slots = incoming[:, -1].astype(jnp.int32) - 1
+    grad_rows = (cotangent.astype(jnp.float32) * live_mask).astype(jnp.bfloat16)
+    incoming, grad_fields, both_pooled, both_coarse, both_fine, both_project = trade(
+        outgoing.reshape(2, moving * 32, 128),
+        grad_rows,
+        [pooled.reshape(bricks * 16, 128), coarse_weight, fine_weight, project_weight],
+        2,
+    )
+    whole_coarse = jnp.concatenate([both_coarse[0], both_coarse[1]], axis=1)
+    whole_fine = jnp.concatenate([both_fine[0], both_fine[1]], axis=1)
+    whole_project = jnp.concatenate([both_project[0], both_project[1]], axis=1)
+    incoming = incoming.reshape(2, 2 * moving, 4096)
+    incoming_slots = incoming[0, :, -1].astype(jnp.int32) - 1
     local_slots = jnp.where(parent // bricks == own_index, parent % bricks, -1)
     all_slots = jnp.concatenate([local_slots, incoming_slots])
     receive_pick = (jnp.arange(bricks, dtype=jnp.int32)[:, None] == all_slots[None, :]).astype(
         jnp.bfloat16
     )
-    arrived = select_rows(receive_pick, jnp.concatenate([pooled, incoming[:, :-128]], axis=0))
-    coarse_half = place_octants(arrived.reshape(bricks, half_channels, 64))
-    coarse_in = lax.all_gather(coarse_half, "chan", axis=1, tiled=True)
+    arrived = select_both(receive_pick, both_pooled, incoming[:, :, :2048])
+    coarse_in = place_octants(arrived)
     lone = lone_bricks(coarse_bricks)
     preactivation = brick_pass(
         coarse_in, lone, live_count, whole_coarse[None], None, jnp.float32, False
@@ -459,35 +616,41 @@
         "cj,bjv->bcv", own_project, hidden, preferred_element_type=jnp.float32
     ).astype(jnp.bfloat16)
     back_source = select_rows(receive_pick.T, split_octants(coarse_out).reshape(bricks, -1))
-    up_octants = gather_back(
-        back_source[:bricks], send_pick, from_sides(back_source[bricks:], moving)
-    ).reshape(bricks, half_channels, 64)
-    mixed_feats = ((feats.astype(jnp.float32) + enlarge(up_octants)) * live_mask).astype(
-        jnp.bfloat16
-    )
     last_brick = devices * bricks
     near_local = jnp.where(
         neighbours >= last_brick, 3 * bricks, neighbours - (own_index - 1) * bricks
     ).astype(jnp.int32)
     slots = jnp.arange(bricks, dtype=jnp.int32)[:, None] + bricks
     near = jnp.concatenate([near_local[:, :13], slots, near_local[:, 13:]], axis=1)
-    grad_rows = (cotangent.astype(jnp.float32) * live_mask).astype(jnp.bfloat16)
-    grad_table = lax.all_gather(around(grad_rows), "chan", axis=1, tiled=True)
     own_weight = lax.dynamic_slice_in_dim(whole_fine, core * half_channels, half_channels, 2)
-    back_feats = brick_pass(
-        grad_table, near, live_count, flip_weight(own_weight)[None], None, jnp.bfloat16, True
-    )[0]
-    feat_table = lax.all_gather(around(mixed_feats), "chan", axis=1, tiled=True)
-    out_feats, fine_total = brick_pass(
-        feat_table, near, live_count, fine_weight[None], grad_rows, jnp.bfloat16, True
+    back_feats, rode_back = brick_pass(
+        grad_fields,
+        near,
+        live_count,
+        flip_weight(own_weight)[None],
+        None,
+        jnp.bfloat16,
+        True,
+        back_source[bricks:].reshape(2, moving * 16, 128),
+        3,
+    )
+    up_octants = gather_back(
+        back_source[:bricks], send_pick, rode_back.reshape(2 * moving, -1)
+    ).reshape(bricks, half_channels, 64)
+    mixed_feats = ((feats.astype(jnp.float32) + enlarge(up_octants)) * live_mask).astype(
+        jnp.bfloat16
     )
     up_grad = pool_sum(back_feats).astype(jnp.bfloat16).reshape(bricks, -1)
     outgoing_grad = select_rows(send_pick, up_grad)
-    arrived_grad = select_rows(
-        receive_pick, jnp.concatenate([up_grad, from_sides(outgoing_grad, moving)], axis=0)
-    )
-    coarse_grad_half = place_octants(arrived_grad.reshape(bricks, half_channels, 64))
-    coarse_grad = lax.all_gather(coarse_grad_half, "chan", axis=1, tiled=True)
+    incoming_grad, feat_fields, both_grad = trade(
+        outgoing_grad.reshape(2, moving * 16, 128),
+        mixed_feats,
+        [up_grad.reshape(bricks * 16, 128)],
+        4,
+    )
+    coarse_grad = place_octants(
+        select_both(receive_pick, both_grad, incoming_grad.reshape(2, 2 * moving, 2048))
+    )
     hidden_half = hidden.shape[1] // 2
     own_hidden = lax.dynamic_slice_in_dim(hidden, core * hidden_half, hidden_half, 1)
     project_matrix = jnp.einsum(
@@ -520,20 +683,28 @@
         coarse_terms.reshape(coarse_bricks, 2, half_channels, 512).sum(1).astype(jnp.bfloat16)
     )
     down_source = select_rows(receive_pick.T, split_octants(coarse_back).reshape(bricks, -1))
+    out_feats, fine_total, rode_down = brick_pass(
+        feat_fields,
+        near,
+        live_count,
+        fine_weight[None],
+        grad_rows,
+        jnp.bfloat16,
+        True,
+        down_source[bricks:].reshape(2, moving * 16, 128),
+        5,
+    )
     down_grad = gather_back(
-        down_source[:bricks], send_pick, from_sides(down_source[bricks:], moving)
+        down_source[:bricks], send_pick, rode_down.reshape(2 * moving, -1)
     ).reshape(bricks, half_channels, 64)
     grad_feats = (back_feats.astype(jnp.float32) + live_mask * enlarge(down_grad) * 0.125).astype(
         jnp.bfloat16
     )
-    fine_sum, coarse_sum, project_total = sum_over_space(
-        fine_total, coarse_total, project_matrix
-    )
-    fine_sum, coarse_sum = grad_taps(fine_sum), grad_taps(coarse_sum)
     fine_scale = 1.0 / math.sqrt(512.0 * bricks * devices)
     coarse_scale = 1.0 / math.sqrt(512.0 * coarse_bricks * devices)
-    fine_weight_grad = fine_sum * fine_scale
-    coarse_weight_grad = coarse_sum * coarse_scale
+    fine_weight_grad, coarse_weight_grad, project_total = sum_over_space(
+        fine_total, coarse_total, project_matrix, fine_scale, coarse_scale
+    )
     project_weight_grad = project_total * coarse_scale
     return (out_feats, grad_feats, fine_weight_grad, coarse_weight_grad, project_weight_grad)
 

time: 188 us -> 139 us (0.74)
  starting transfers between devices: 61.4 us -> 0 us
  Pallas kernels: 67.9 us -> 107 us
  between operations: 15.7 us -> 2.02 us
  blocking collectives: 10.1 us -> 0 us
    ppermute x12 -> x0, starting transfers between devices: 61.4 us -> none  [the longest x4 33 us: from_sides(): lax.ppermute(rows[:moving], 'space', [(i + 1, i) for i in range(count - 1)])]
    pallas_call x5 -> x8, Pallas kernels: 29.7 us -> 66.7 us  [the longest x2 32.6 us: trade(): pl.pallas_call(lambda *refs: trade_kernel(count, amount, *refs), in_specs...]
    all_gather x5 -> x0, blocking collectives: 10.1 us -> none  [the longest x1 2.43 us: per_device(): whole_coarse = lax.all_gather(coarse_weight, 'chan', axis=1, tiled=True)]
    unnamed x40 -> x46, local copies, waits for them, and re-layouts: 3.51 us -> 8.77 us
    concatenate x2 -> x3, other arithmetic: 2.96 us -> 0.79 us  [the longest x2 0.6 us: per_device(): whole_coarse = jnp.concatenate([both_coarse[0], both_coarse[1]], axis=1)]
    pallas_call x1, Pallas kernels: 38.2 us -> 40.3 us  [sum_tiles(): pl.pallas_call(lambda *refs: sum_kernel(sizes, *refs), in_specs=[pl.Block...]
  transfers between devices with their start and end apart: 14 -> 0, of which waited for: 1 -> 0; matrix products, arithmetic and copies ran while one was open for 10% -> 0% of each run, Pallas kernels for 8% -> 0%
where the time goes in v2:
time: 139 us
  Pallas kernels  107 us (77%)
  local copies, waits for them, and re-layouts  18.8 us (14%)
  matrix products  5.66 us (4%)
  other arithmetic  5.26 us (4%)
  between operations  2.02 us (1%)
    pallas_call x1, Pallas kernels, sum_tiles(): pl.pallas_call(lambda *refs: sum_kernel(sizes, *refs), in_specs=[pl.Block...  40.3 us
    pallas_call x2, Pallas kernels, trade(): pl.pallas_call(lambda *refs: trade_kernel(count, amount, *refs), in_specs...  32.6 us
    pallas_call x5, Pallas kernels, brick_pass(): pl.pallas_call(lambda *refs: brick_kernel(count, weight is not None, grad...  31.7 us
    unnamed x46, local copies, waits for them, and re-layouts  8.77 us
    gather x5, local copies, waits for them, and re-layouts, weight_blocks(): taps = weight.reshape(9, 3, rows, channels)[:, KZ_ORDER]  2.99 us

profile of v2, /device:TPU:8, one launch (start us, length us, event | category | flops | bytes accessed | tf_op | source)
XLA Modules:
  0.0 138.7 jit_solution(9972206752001394314)
XLA Ops:
  0.6 0.7 subtract_select_fusion
  2.2 0.7 compare_select_fusion.1
  3.3 1.2 fusion.16
  4.8 1.1 multiply_convert_fusion.refs_1_.refs_4_
  6.0 0.9 copy-done.1
  7.0 0.7 copy-done.4
  7.7 17.7 %shard_map.245 = (bf16[2,2,32,128]{3,2,1,0:T(8,128)(2,1)S(1)}, bf16[2,3,8,32,512]{4,3,2,1,0:T(8,128)(2,1)S(1)}, bf16[2,128,128]{2,1,0:T(8,128)(2,1)S(1)}, bf16[2...) custom-call(bf16[2,32,128]{2,1,0:T(8,128)(2,1)S(1)} %bitcast.193, ...), custom_call_target="tpu_custom_call" | custom-call | tf_op jit(solution)/shard_map/pallas_call | solution.py:176
  25.4 1.2 copy-done.5
  27.2 0.6 gather_fusion
  29.2 1.1 slice_bitcast_fusion.7
  31.2 0.6 gather_fusion.1
  32.2 1.6 %shard_map.246 = f32[1,128,512]{2,1,0:T(8,128)S(1)} custom-call(s32[1,27]{1,0:T(1,128)S(1)} %compare_select_fusion.refs_0_, s32[1]{0:T(128)} %copy.79.refs_1_, bf16[1,64,512]{2,1,0:T(8,128)(2,1)S(1)} %fusion.13.refs_2_, bf16[1,3,128,768]{3,2,1,0:T(8,128)(2,1)S(1)} %copy.41.refs_3_), custom_call_target="tpu_custom_call" | custom-call | flops 301989888 | bytes 65536 | tf_op jit(solution)/shard_map/pallas_call | solution.py:353
  33.9 0.5 fusion.14
  34.8 1.4 %copy-done.6 = bf16[2,3,8,32,512]{4,3,2,1,0:T(8,128)(2,1)S(1)} copy-done((bf16[2,3,8,32,512]{4,3,2,1,0:T(8,128)(2,1)S(1)}, bf16[2,3,8,32,512]{4,3,2,1,0:T(8,128)(2,1)}, u32[]{:S(2)}) %copy-start.6) | copy-done | bytes 1572888
  36.2 11.8 %shard_map.247 = (bf16[8,32,512]{2,1,0:T(8,128)(2,1)S(1)}, bf16[2,16,128]{2,1,0:T(8,128)(2,1)S(1)}) custom-call(s32[8,27]{1,0:T(8,128)S(1)} %pad_add_fusion.refs_0_, s32[1]{0:T(128)} %copy.79.refs_1_, bf16[2,3,8,32,512]{4,3,2,1,0:T(8,128)(2,1)S(1)} %copy-done.6, bf16[1,3,32,768]{3,2,1,0:T(8,128)(2,1)S(1)} %stack_reshape.15.refs_3_, ...), custom_call_target="tpu_custom_call" | custom-call | flops 603979776 | bytes 1572864 | tf_op jit(solution)/shard_map/pallas_call | solution.py:353
  49.2 14.9 %shard_map.248 = (bf16[2,2,16,128]{3,2,1,0:T(8,128)(2,1)S(1)}, bf16[2,3,8,32,512]{4,3,2,1,0:T(8,128)(2,1)S(1)}, bf16[2,128,128]{2,1,0:T(8,128)(2,1)S(1)}) custom-call(bf16[2,16,128]{2,1,0:T(8,128)(2,1)S(1)} %bitcast.194, bf16[8,32,512]{2,1,0:T(8,128)(2,1)S(1)} %fusion.6.refs_1_, bf16[128,128]{1,0:T(8,128)(2,1)S(1)} %reshape_reshape.16.refs_2_), custom_call_target="tpu_custom_call" | custom-call | tf_op jit(solution)/shard_map/pallas_call | solution.py:176
  64.1 1.2 copy-done.7
  65.3 0.6 gather_fusion.2
  67.4 0.3 dynamic-slice_maximum_fusion
  68.2 0.6 gather_fusion.4
  69.4 0.6 gather_fusion.3
  70.5 2.5 %shard_map.249 = f32[2,32,512]{2,1,0:T(8,128)S(1)} custom-call(s32[2,27]{1,0:T(2,128)S(1)} %iota_select_fusion.refs_0_, s32[1]{0:T(128)} %copy.79.refs_1_, bf16[2,64,512]{2,1,0:T(8,128)(2,1)S(1)} %bitcast.195, bf16[2,3,32,768]{3,2,1,0:T(8,128)(2,1)S(1)} %pad_maximum_fusion.2.refs_3_), custom_call_target="tpu_custom_call" | custom-call | flops 150994944 | bytes 131072 | tf_op jit(solution)/shard_map/pallas_call | solution.py:353
  73.8 1.4 %copy-done.8 = bf16[2,3,8,32,512]{4,3,2,1,0:T(8,128)(2,1)S(1)} copy-done((bf16[2,3,8,32,512]{4,3,2,1,0:T(8,128)(2,1)S(1)}, bf16[2,3,8,32,512]{4,3,2,1,0:T(8,128)(2,1)}, u32[]{:S(2)}) %copy-start.8) | copy-done | bytes 1572888
  75.2 14.5 %shard_map.250 = (bf16[8,32,512]{2,1,0:T(8,128)(2,1)S(1)}, f32[3,32,768]{2,1,0:T(8,128)S(1)}, bf16[2,16,128]{2,1,0:T(8,128)(2,1)S(1)}) custom-call(s32[8,27]{1,0:T(8,128)S(1)} %pad_add_fusion.refs_0_, s32[1]{0:T(128)} %copy.79.refs_1_, bf16[2,3,8,32,512]{4,3,2,1,0:T(8,128)(2,1)S(1)} %copy-done.8, bf16[1,3,32,768]{3,2,1,0:T(8,128)(2,1)S(1)} %stack_reshape.17.refs_3_, ...), custom_call_target="tpu_custom_call" | custom-call | flops 1207959552 | bytes 1572864 | tf_op jit(solution)/shard_map/pallas_call | solution.py:353
  90.0 0.9 fusion.5
  91.2 1.3 shard_map.251
  92.9 40.3 %shard_map.252 = f32[2,4,4,8,1,8,128]{6,5,4,3,2,1,0:T(8,128)S(1)} custom-call(f32[2,4,4,8,1,8,128]{6,5,4,3,2,1,0:T(8,128)S(1)} %bitcast.189), custom_call_target="tpu_custom_call" | custom-call | flops 1048576 | bytes 8388608 | tf_op jit(solution)/shard_map/pallas_call | solution.py:503
  133.2 1.0 copy-done
  134.2 2.4 %shard_map.253 = (f32[27,32,64]{2,1,0:T(8,128)}, f32[27,64,64]{2,1,0:T(8,128)}) custom-call(f32[256,8,128]{2,1,0:T(8,128)} %bitcast.187), custom_call_target="tpu_custom_call" | custom-call | tf_op jit(solution)/shard_map/pallas_call | solution.py:554
  136.6 0.7 slice_multiply_fusion
  137.4 0.7 mul.93
  138.0 0.7 copy.80
  (121 shorter events, 10.3 us)
Async XLA Ops:
  0.6 5.4 %copy-start.3 = (bf16[27,64,64]{2,1,0:T(8,128)(2,1)S(1)}, bf16[27,64,64]{2,1,0:T(8,128)(2,1)}, u32[]{:S(2)}) copy-start(bf16[27,64,64]{2,1,0:T(8,128)(2,1)} %refs_3_.1) | copy-start | bytes 663556
  6.0 0.9 copy-start.1
  7.0 0.7 copy-start.4
  25.4 1.2 copy-start.5
  26.5 0.7 copy-start.18
  26.8 2.2 %copy-start.9 = (bf16[8,64,512]{2,1,0:T(8,128)(2,1)S(1)}, bf16[8,64,512]{2,1,0:T(8,128)(2,1)}, u32[]{:S(2)}) copy-start(bf16[8,64,512]{2,1,0:T(8,128)(2,1)} %constant.116) | copy-start | bytes 1572868
  33.9 0.9 copy-start.14
  33.9 14.1 %copy-start.16 = (bf16[64,64]{1,0:T(8,128)(2,1)}, bf16[64,64]{1,0:T(8,128)(2,1)S(1)}, u32[]{:S(2)}) copy-start(bf16[64,64]{1,0:T(8,128)(2,1)S(1)} %get-tuple-element.49) | copy-start | bytes 24580
  33.9 14.1 %copy-start.13 = (bf16[512,64,1]{0,1,2:T(8,128)(2,1)S(1)}, bf16[512,64,1]{0,1,2:T(8,128)(2,1)}, u32[]{:S(2)}) copy-start(bf16[512,64,1]{0,1,2:T(8,128)(2,1)} %constant.122) | copy-start | bytes 196612
  33.9 15.0 %copy-start.12 = (bf16[8,32,512]{2,1,0:T(8,128)(2,1)S(1)}, bf16[8,32,512]{2,1,0:T(8,128)(2,1)}, u32[]{:S(2)}) copy-start(bf16[8,32,512]{2,1,0:T(8,128)(2,1)} %param.22) | copy-start | bytes 786436
  34.8 1.4 %copy-start.6 = (bf16[2,3,8,32,512]{4,3,2,1,0:T(8,128)(2,1)S(1)}, bf16[2,3,8,32,512]{4,3,2,1,0:T(8,128)(2,1)}, u32[]{:S(2)}) copy-start(bf16[2,3,8,32,512]{4,3,2,1,0:T(8,128)(2,1)} %copy-done.5) | copy-start | bytes 4718596
  36.2 29.1 %copy-start.2 = (bf16[27,32,64]{2,1,0:T(8,128)(2,1)S(1)}, bf16[27,32,64]{2,1,0:T(8,128)(2,1)}, u32[]{:S(2)}) copy-start(bf16[27,32,64]{2,1,0:T(8,128)(2,1)} %refs_4_.1) | copy-start | bytes 331780
  64.1 1.2 copy-start.7
  65.9 1.2 copy-start.17
  66.1 1.3 copy-start.10
  66.1 1.3 copy-start.11
  73.8 1.4 %copy-start.8 = (bf16[2,3,8,32,512]{4,3,2,1,0:T(8,128)(2,1)S(1)}, bf16[2,3,8,32,512]{4,3,2,1,0:T(8,128)(2,1)}, u32[]{:S(2)}) copy-start(bf16[2,3,8,32,512]{4,3,2,1,0:T(8,128)(2,1)} %copy-done.7) | copy-start | bytes 4718596
  75.2 15.8 %copy-start.15 = (bf16[1,128,512]{2,1,0:T(8,128)(2,1)S(1)}, bf16[1,128,512]{2,1,0:T(8,128)(2,1)}, u32[]{:S(2)}) copy-start(bf16[1,128,512]{2,1,0:T(8,128)(2,1)} %copy-done.14) | copy-start | bytes 393220
  133.2 1.0 copy-start

commit v3 on v2

v3 whole, which is shorter than its diff:
```python
import math

import jax
import jax.numpy as jnp
import numpy as np
from jax import lax
from jax.experimental import pallas as pl
from jax.experimental.pallas import tpu as pltpu
from jax.sharding import PartitionSpec as P


def lean_list():
    leans = []
    for lean_x in (-1, 0, 1):
        for lean_y in (-1, 0, 1):
            for lean_z in (-1, 0, 1):
                leans.append((lean_x, lean_y, lean_z))
    return leans


def pool_table():
    voxel = np.arange(512)
    octant_voxel = 16 * (voxel // 128) + 4 * (voxel // 16 % 4) + voxel % 8 // 2
    return (octant_voxel[:, None] == np.arange(64)[None, :]).astype(np.float32)


def octant_table():
    voxel = np.arange(512)
    coord_x = voxel // 64
    coord_y = voxel // 8 % 8
    coord_z = voxel % 8
    octant = 4 * (coord_x // 4) + 2 * (coord_y // 4) + coord_z // 4
    inner = 16 * (coord_x % 4) + 4 * (coord_y % 4) + coord_z % 4
    table = np.zeros((8, 64, 512), np.float32)
    table[octant, inner, voxel] = 1.0
    return table


def flip_weight(weight):
    return jnp.transpose(weight[::-1], (0, 2, 1))


def pool_sum(field_in):
    table = jnp.asarray(pool_table()).astype(jnp.bfloat16)
    return jnp.einsum("bcv,vu->bcu", field_in, table, preferred_element_type=jnp.float32)


def enlarge(octants):
    table = jnp.asarray(pool_table()).astype(jnp.bfloat16)
    return jnp.einsum("bcu,vu->bcv", octants, table, preferred_element_type=jnp.float32)


def place_octants(octants):
    amount, channels = (octants.shape[0] // 8, octants.shape[1])
    grouped = octants.reshape(amount, 8, channels, 64)
    table = jnp.asarray(octant_table()).astype(jnp.bfloat16)
    return jnp.einsum("jocu,ouv->jcv", grouped, table, preferred_element_type=jnp.float32).astype(
        jnp.bfloat16
    )


def split_octants(coarse):
    amount, channels = (coarse.shape[0], coarse.shape[1])
    table = jnp.asarray(octant_table()).astype(jnp.bfloat16)
    parts = jnp.einsum("jcv,ouv->jocu", coarse, table, preferred_element_type=jnp.float32).astype(
        jnp.bfloat16
    )
    return parts.reshape(amount * 8, channels, 64)


def select_rows(picker, values):
    return jnp.dot(picker, values, preferred_element_type=jnp.float32).astype(jnp.bfloat16)


def route_places(slot_list, dev_index, moving, bricks):
    direction = slot_list // bricks - dev_index
    to_left = (direction == -1).astype(jnp.int32)
    to_right = (direction == 1).astype(jnp.int32)
    left_rank = jnp.cumsum(to_left) - to_left
    right_rank = jnp.cumsum(to_right) - to_right
    return jnp.where(
        to_left == 1, left_rank, jnp.where(to_right == 1, moving + right_rank, 2 * moving)
    ).astype(jnp.int32)


def lone_bricks(amount):
    centre = jnp.arange(27, dtype=jnp.int32)[None, :] == 13
    return jnp.where(centre, jnp.arange(amount, dtype=jnp.int32)[:, None], amount)


def select_both(picker, body, moved):
    values = jnp.concatenate([body.reshape(2, -1, 2048), moved], axis=1)
    picked = jnp.einsum("rs,csv->rcv", picker, values, preferred_element_type=jnp.float32)
    return picked.astype(jnp.bfloat16).reshape(picker.shape[0], -1, 64)


def gather_back(local_part, send_pick, returned):
    total = local_part.astype(jnp.float32) + jnp.dot(
        send_pick.T, returned, preferred_element_type=jnp.float32
    )
    return total.astype(jnp.bfloat16)


SPANS = {-1: (slice(0, 1), slice(7, 8)), 0: (slice(1, 9), slice(0, 8)), 1: (slice(9, 10), slice(0, 1))}
TAP_ORDER = np.array([1, 0, 2, 5, 4, 3, 7, 6, 8])
WIDTH = 640


def greet(devices):
    barrier = pltpu.get_barrier_semaphore()
    for device in devices:
        pl.semaphore_signal(
            barrier, inc=1, device_id=device, device_id_type=pl.DeviceIdType.MESH
        )
    pl.semaphore_wait(barrier, len(devices))


def nearby(count):
    me, core = lax.axis_index("space"), lax.axis_index("chan")
    return ((me + count - 1) % count, core), ((me + 1) % count, core), (me, 1 - core)


def sender(send_sems, recv_sems):
    def send(number, source, target, device):
        copy = pltpu.make_async_remote_copy(
            src_ref=source,
            dst_ref=target,
            send_sem=send_sems.at[number],
            recv_sem=recv_sems.at[number],
            device_id=device,
            device_id_type=pl.DeviceIdType.MESH,
        )
        copy.start()
        return copy

    return send


def trade_kernel(count, amount, *refs):
    rows, own = refs[:2]
    shares = refs[2 : 2 + amount]
    rows_all, fields = refs[2 + amount : 4 + amount]
    shares_all = refs[4 + amount : 4 + 2 * amount]
    send_sems, recv_sems = refs[4 + 2 * amount :]
    core = lax.axis_index("chan")
    left, right, mate = nearby(count)
    left_mate, right_mate = (left[0], 1 - core), (right[0], 1 - core)
    greet((left, right, mate, left_mate, right_mate))
    send = sender(send_sems, recv_sems)
    quick = [
        send(0, rows.at[0], rows_all.at[core, 1], left),
        send(1, rows.at[1], rows_all.at[core, 0], right),
        send(2, rows.at[0], rows_all.at[core, 1], left_mate),
        send(3, rows.at[1], rows_all.at[core, 0], right_mate),
    ]
    to_right = send(4, own, fields.at[core, 0], right)
    to_left = send(5, own, fields.at[core, 2], left)
    for number, (share, share_all) in enumerate(zip(shares, shares_all)):
        quick.append(send(8 + number, share, share_all.at[core], mate))
        share_all[core] = share[...]
    quick.append(send(8 + amount, own, fields.at[core, 1], mate))
    fields[core, 1] = own[...]
    to_right.wait_recv()
    quick.append(send(6, fields.at[core, 0], fields.at[core, 0], mate))
    to_left.wait_recv()
    quick.append(send(7, fields.at[core, 2], fields.at[core, 2], mate))
    for copy in quick:
        copy.wait_recv()
    for copy in quick + [to_right, to_left]:
        copy.wait_send()


def trade(rows, own, shares, number):
    count = lax.axis_size("space")
    amount = len(shares)
    shapes = [(2,) + rows.shape, (2, 3) + own.shape] + [(2,) + share.shape for share in shares]
    return pl.pallas_call(
        lambda *refs: trade_kernel(count, amount, *refs),
        in_specs=[pl.BlockSpec(memory_space=pltpu.VMEM)] * (2 + amount),
        out_specs=[pl.BlockSpec(memory_space=pltpu.VMEM)] * (2 + amount),
        out_shape=[jax.ShapeDtypeStruct(shape, rows.dtype) for shape in shapes],
        scratch_shapes=[
            pltpu.SemaphoreType.DMA((9 + amount,)),
            pltpu.SemaphoreType.DMA((9 + amount,)),
        ],
        compiler_params=pltpu.CompilerParams(
            collective_id=number, has_side_effects=True, vmem_limit_bytes=32 * 1024 * 1024
        ),
    )(rows, own, *shares)


def ride_copies(count, refs):
    return [
        pltpu.make_async_remote_copy(
            src_ref=refs["ride"].at[side],
            dst_ref=refs["ride_in"].at[1 - side],
            send_sem=refs["ride_send"].at[side],
            recv_sem=refs["ride_recv"].at[side],
            device_id=device,
            device_id_type=pl.DeviceIdType.MESH,
        )
        for side, device in enumerate(nearby(count)[:2])
    ]


def hail(devices):
    barrier = pltpu.get_barrier_semaphore()
    for device in devices:
        pl.semaphore_signal(
            barrier, inc=1, device_id=device, device_id_type=pl.DeviceIdType.MESH
        )


def torus_sizes(count):
    return (4, 4, 8) if count == 128 else (1, 1, count)


class TorusSum:
    def __init__(self, count, axes, refs, label):
        size_y, size_x, size_z = torus_sizes(count)
        me, self.core = lax.axis_index("space"), lax.axis_index("chan")
        self.sizes = {"y": size_y, "x": size_x, "z": size_z}
        self.place = {
            "y": me // (size_z * size_x),
            "x": me // size_z % size_x,
            "z": me % size_z,
        }
        self.axes = axes
        self.refs = {name: refs[label + name] for name in SUM_NAMES}

    def device(self, axis, step):
        at = dict(self.place)
        at[axis] = (at[axis] + step) % self.sizes[axis]
        return (at["y"] * self.sizes["x"] + at["x"]) * self.sizes["z"] + at["z"], self.core

    def peers(self):
        return [
            self.device(axis, step) for axis in self.axes for step in range(1, self.sizes[axis])
        ]

    def copies(self, phase):
        refs = self.refs
        axis = (self.axes + self.axes[::-1])[phase]
        made = []
        for step in range(1, self.sizes[axis]):
            other = (self.place[axis] + step) % self.sizes[axis]
            if phase < 3:
                source = refs[("data", "own_a", "own_b")[phase]].at[other]
                target = refs[("part_a", "part_b", "part_z")[phase]].at[step - 1]
            else:
                here = [self.place[name] for name in self.axes]
                if phase == 3:
                    source = refs["whole"].at[here[2]]
                elif phase == 4:
                    source = refs["total"].at[here[0], here[1]]
                else:
                    source = refs["total"].at[here[0]]
                target = source
            made.append(
                pltpu.make_async_remote_copy(
                    src_ref=source,
                    dst_ref=target,
                    send_sem=refs["send"].at[phase, step - 1],
                    recv_sem=refs["recv"].at[phase, step - 1],
                    device_id=self.device(axis, step),
                    device_id_type=pl.DeviceIdType.MESH,
                )
            )
        return made

    def summed(self, kept, parts, axis):
        value = self.refs[kept][self.place[axis]]
        for step in range(1, self.sizes[axis]):
            value = value + self.refs[parts][step - 1]
        return value

    def start(self, phase):
        refs = self.refs
        at_a, at_b, at_z = [self.place[axis] for axis in self.axes]
        if phase == 1:
            refs["own_a"][...] = self.summed("data", "part_a", self.axes[0])
        elif phase == 2:
            refs["own_b"][...] = self.summed("own_a", "part_b", self.axes[1])
        elif phase == 3:
            refs["whole"][at_z] = self.summed("own_b", "part_z", "z")
        elif phase == 4:
            refs["total"][at_a, at_b] = refs["whole"][...]
        for copy in self.copies(phase):
            copy.start()

    def wait(self, phase):
        for copy in self.copies(phase):
            copy.wait_recv()

    def leave(self):
        for phase in range(6):
            for copy in self.copies(phase):
                copy.wait_send()


SUM_NAMES = (
    "data", "part_a", "own_a", "part_b", "own_b", "part_z", "whole", "total", "send", "recv"
)


def sum_scratch(count, axes, rows, label, with_data):
    sizes = dict(zip("yxz", torus_sizes(count)))
    a, b, z = [sizes[axis] for axis in axes]
    piece = (128 // count, rows, 128)
    shapes = {
        "part_a": (max(1, a - 1), b, z),
        "own_a": (b, z),
        "part_b": (max(1, b - 1), z),
        "own_b": (z,),
        "part_z": (z - 1,),
        "whole": (z,),
        "total": (a, b, z),
    }
    if with_data:
        shapes["data"] = (a, b, z)
    scratch = {
        label + name: pltpu.VMEM(shape + piece, jnp.float32) for name, shape in shapes.items()
    }
    most = max(a, b, z) - 1
    scratch[label + "send"] = pltpu.SemaphoreType.DMA((6, most))
    scratch[label + "recv"] = pltpu.SemaphoreType.DMA((6, most))
    return scratch, (a, b, z) + piece


def fine_pieces(acc):
    pieces = []
    for tap_x in range(3):
        for block in range(acc.shape[1] // 4):
            for lane in range(WIDTH // 128):
                pieces.append((tap_x, slice(4 * block, 4 * block + 4), slice(128 * lane, 128 * lane + 128)))
    return pieces


def brick_kernel(count, masked, names, *refs):
    refs = dict(zip(names, refs))
    field_ref, table, padded, columns = [
        refs[name] for name in ("field", "table", "padded", "columns")
    ]
    brick = pl.program_id(0)
    last = pl.num_programs(0) - 1
    sums = "wide_data" in refs
    if sums:
        wide = TorusSum(count, ("x", "y", "z"), refs, "wide_")
        slim = TorusSum(count, ("y", "x", "z"), refs, "slim_")

    @pl.when(brick == 0)
    def fill():
        if count:
            greeted = list(nearby(count)[:2]) + (wide.peers() if sums else [])
            hail(greeted)
        slots = table.shape[0] - 1
        table[slots] = jnp.zeros((8, 8, 8, 128), jnp.float32)
        halves = len(field_ref.shape) == 5
        amount = field_ref.shape[2]

        def turn(slot, carry):
            if halves:
                place, one = slot // amount, slot % amount
                field = jnp.concatenate(
                    [field_ref[0, place, one], field_ref[1, place, one]], axis=0
                ).astype(jnp.float32)
            else:
                field = field_ref[slot].astype(jnp.float32)
            turned = jnp.concatenate([field, field], axis=0).T
            table[slot] = turned.reshape(8, 8, 8, 128)
            return carry

        lax.fori_loop(0, slots, turn, 0)
        if "acc" in refs:
            refs["acc"][...] = jnp.zeros_like(refs["acc"])
        if count:
            pl.semaphore_wait(pltpu.get_barrier_semaphore(), len(greeted))
            for copy in ride_copies(count, refs):
                copy.start()
        if sums:
            wide.start(0)

    if sums:

        @pl.when(brick == last - 2)
        def second():
            wide.wait(0)
            wide.start(1)

        @pl.when(brick == last)
        def third():
            wide.wait(1)
            wide.start(2)

    for index, (lean_x, lean_y, lean_z) in enumerate(lean_list()):
        slot = refs["near"][brick, index]
        to_x, from_x = SPANS[lean_x]
        to_y, from_y = SPANS[lean_y]
        padded[lean_z + 1, to_x, to_y] = table[slot, from_x, from_y]
    shape = (10, 8, 8, 128)
    place_z = lax.broadcasted_iota(jnp.int32, shape, 2)
    low_half = lax.broadcasted_iota(jnp.int32, shape, 3) < 64

    def put(position, low, high):
        both = jnp.where(low_half, low, high).reshape(640, 128)
        columns[:, 128 * position : 128 * position + 128] = both.astype(jnp.bfloat16)

    ahead = []
    for tap_y, position in enumerate((0, 2, 3)):
        below = padded[0, :, tap_y : tap_y + 8]
        level = padded[1, :, tap_y : tap_y + 8]
        above = padded[2, :, tap_y : tap_y + 8]
        minus = pltpu.roll(jnp.where(place_z == 7, below, level), 1, 2)
        put(position, level, minus)
        ahead.append(pltpu.roll(jnp.where(place_z == 0, above, level), 7, 2))
        if tap_y == 1:
            put(1, ahead[0], ahead[1])
    put(4, ahead[2], 0.0)
    if "weight" in refs:
        total = None
        for tap_x in range(3):
            part = lax.dot_general(
                refs["weight"][0, tap_x],
                columns[64 * tap_x : 64 * tap_x + 512, :],
                (((1,), (1,)), ((), ())),
                preferred_element_type=jnp.float32,
            )
            total = part if total is None else total + part
        if masked:
            total = jnp.where(brick < refs["live"][0], total, 0.0)
        refs["out"][0] = total.astype(refs["out"].dtype)
    if "grad" in refs:
        for tap_x in range(3):
            refs["acc"][tap_x] += jnp.dot(
                refs["grad"][0],
                columns[64 * tap_x : 64 * tap_x + 512, :],
                preferred_element_type=jnp.float32,
            )

    @pl.when(brick == last)
    def close():
        if sums:
            acc, data = refs["acc"], refs["slim_data"]
            cells = list(np.ndindex(data.shape[:4]))
            spans = fine_pieces(acc)
            for cell, span in zip(cells, spans):
                data[cell] = acc[span]
            for cell in cells[len(spans) :]:
                data[cell] = jnp.zeros(data.shape[4:], jnp.float32)
            slim.start(0)
            for phase in range(3):
                wide.wait(2 + phase)
                wide.start(3 + phase)
                slim.wait(phase)
                slim.start(phase + 1)
            wide.wait(5)
            refs["wide_out"][...] = refs["wide_total"][...]
            for phase in range(3, 5):
                slim.wait(phase)
                slim.start(phase + 1)
            slim.wait(5)
            refs["slim_out"][...] = refs["slim_total"][...]
            wide.leave()
            slim.leave()
        elif "acc" in refs:
            refs["total"][...] = refs["acc"][...]
        if count:
            for copy in ride_copies(count, refs):
                copy.wait()
            refs["ride_out"][...] = refs["ride_in"][...]


def brick_pass(
    field_in, near, live_count, weight, grad_rows, out_dtype, masked, ride=None, number=None,
    wide=None,
):
    amount = near.shape[0]
    count = 0 if ride is None else lax.axis_size("space")
    slots = 3 * field_in.shape[2] if field_in.ndim == 5 else field_in.shape[0]
    rows = weight.shape[2] if weight is not None else grad_rows.shape[1]
    ins, outs, scratch = {}, {}, {}

    def whole(shape):
        return pl.BlockSpec(shape, lambda b: (0,) * len(shape))

    def result(name, shape, dtype, spec=None):
        outs[name] = (jax.ShapeDtypeStruct(shape, dtype), spec or whole(shape))

    ins["near"] = (near, pl.BlockSpec(memory_space=pltpu.SMEM))
    ins["live"] = (live_count, pl.BlockSpec(memory_space=pltpu.SMEM))
    ins["field"] = (field_in, whole(field_in.shape))
    scratch["table"] = pltpu.VMEM((slots + 1, 8, 8, 8, 128), jnp.float32)
    scratch["padded"] = pltpu.VMEM((3, 10, 10, 8, 128), jnp.float32)
    scratch["columns"] = pltpu.VMEM((640, WIDTH), jnp.bfloat16)
    by_brick = pl.BlockSpec((1, rows, 512), lambda b: (b, 0, 0))
    if weight is not None:
        parts = weight.shape[0]
        blocks = jnp.stack([weight_blocks(part) for part in weight])
        ins["weight"] = (
            blocks, pl.BlockSpec((1, 3, rows, WIDTH), lambda b: (b % parts, 0, 0, 0))
        )
        result("out", (amount, rows, 512), out_dtype, by_brick)
    if grad_rows is not None:
        ins["grad"] = (grad_rows, by_brick)
        scratch["acc"] = pltpu.VMEM((3, rows, WIDTH), jnp.float32)
        if wide is None:
            result("total", (3, rows, WIDTH), jnp.float32)
    if wide is not None:
        wide_scratch, wide_shape = sum_scratch(count, "xyz", 8, "wide_", False)
        slim_scratch, slim_shape = sum_scratch(count, "yxz", 4, "slim_", True)
        scratch.update(wide_scratch)
        scratch.update(slim_scratch)
        ins["wide_data"] = (wide.reshape(wide_shape), whole(wide_shape))
        result("wide_out", wide_shape, jnp.float32)
        result("slim_out", slim_shape, jnp.float32)
    if count:
        ins["ride"] = (ride, whole(ride.shape))
        result("ride_out", ride.shape, ride.dtype)
        scratch["ride_in"] = pltpu.VMEM(ride.shape, ride.dtype)
        scratch["ride_send"] = pltpu.SemaphoreType.DMA((2,))
        scratch["ride_recv"] = pltpu.SemaphoreType.DMA((2,))
    names = list(ins) + list(outs) + list(scratch)
    remote = {"collective_id": number, "has_side_effects": True} if count else {}
    products = (weight is not None) + (grad_rows is not None)
    return pl.pallas_call(
        lambda *refs: brick_kernel(count, masked, names, *refs),
        grid=(amount,),
        in_specs=[spec for _, spec in ins.values()],
        out_specs=[spec for _, spec in outs.values()],
        out_shape=[shape for shape, _ in outs.values()],
        scratch_shapes=list(scratch.values()),
        compiler_params=pltpu.CompilerParams(vmem_limit_bytes=48 * 1024 * 1024, **remote),
        cost_estimate=pl.CostEstimate(
            flops=amount * products * 2 * rows * 3 * WIDTH * 512,
            bytes_accessed=slots * 64 * 512 * 2,
            transcendentals=0,
        ),
    )(*[value for value, _ in ins.values()])


def weight_blocks(weight):
    rows, channels = weight.shape[1:]
    taps = weight.reshape(3, 9, rows, channels)[:, TAP_ORDER]
    taps = jnp.concatenate([taps, jnp.zeros_like(taps[:, :1])], axis=1)
    return jnp.transpose(taps, (0, 2, 1, 3)).reshape(3, rows, WIDTH)


def finish_kernel(scales, slim, wide, fine_out, coarse_out):
    for pieces, out, scale in zip((slim, wide), (fine_out, coarse_out), scales):
        high = pieces.shape[1]
        blocks = out.shape[1] // high
        for tap_x in range(3):
            for block in range(blocks):
                first = WIDTH // 128 * (tap_x * blocks + block)
                rows = slice(high * block, high * block + high)
                for place, tap in enumerate(TAP_ORDER):
                    lanes = slice(64 * (place % 2), 64 * (place % 2) + 64)
                    out[9 * tap_x + int(tap), rows, :] = pieces[first + place // 2, :, lanes] * scale


def wide_pieces(coarse, project):
    tiles = jnp.transpose(coarse.reshape(-1, 8, WIDTH // 128, 128), (0, 2, 1, 3))
    tiles = tiles.reshape(-1, 8, 128)
    small = project.reshape(-1, 8, 128)
    spare = 128 - tiles.shape[0] - small.shape[0]
    return jnp.concatenate([tiles, small, jnp.zeros((spare, 8, 128), jnp.float32)], axis=0)


def finish(slim, wide, fine_rows, coarse_rows, scales):
    slim, wide = slim.reshape(128, 4, 128), wide.reshape(128, 8, 128)
    fine_sum, coarse_sum = pl.pallas_call(
        lambda *refs: finish_kernel(scales, *refs),
        in_specs=[pl.BlockSpec(memory_space=pltpu.VMEM)] * 2,
        out_specs=[pl.BlockSpec(memory_space=pltpu.VMEM)] * 2,
        out_shape=[
            jax.ShapeDtypeStruct((27, rows, 64), jnp.float32) for rows in (fine_rows, coarse_rows)
        ],
    )(slim, wide)
    used = 3 * coarse_rows // 8 * (WIDTH // 128)
    return fine_sum, coarse_sum, wide[used : used + 4].reshape(64, 64)


def per_device(
    feats, live_count, neighbours, parent, fine_weight, coarse_weight, project_weight, cotangent
):
    bricks = feats.shape[0]
    half_channels = feats.shape[1]
    devices = lax.axis_size("space")
    own_index = lax.axis_index("space")
    moving = max(1, bricks // 8)
    coarse_bricks = bricks // 8
    live_mask = (jnp.arange(bricks, dtype=jnp.int32) < live_count[0]).astype(jnp.float32)[
        :, None, None
    ]
    core = lax.axis_index("chan")
    send_place = route_places(parent, own_index, moving, bricks)
    send_pick = (jnp.arange(2 * moving, dtype=jnp.int32)[:, None] == send_place[None, :]).astype(
        jnp.bfloat16
    )
    pooled = (pool_sum(feats) * 0.125 * live_mask).astype(jnp.bfloat16).reshape(bricks, -1)
    slot_rows = jnp.broadcast_to(
        (parent % bricks + 1).astype(jnp.bfloat16)[:, None], (bricks, 2048)
    )
    outgoing = select_rows(send_pick, jnp.concatenate([pooled, slot_rows], axis=1))
    grad_rows = (cotangent.astype(jnp.float32) * live_mask).astype(jnp.bfloat16)
    incoming, grad_fields, both_pooled, both_coarse, both_fine, both_project = trade(
        outgoing.reshape(2, moving * 32, 128),
        grad_rows,
        [pooled.reshape(bricks * 16, 128), coarse_weight, fine_weight, project_weight],
        2,
    )
    whole_coarse = jnp.concatenate([both_coarse[0], both_coarse[1]], axis=1)
    whole_fine = jnp.concatenate([both_fine[0], both_fine[1]], axis=1)
    whole_project = jnp.concatenate([both_project[0], both_project[1]], axis=1)
    incoming = incoming.reshape(2, 2 * moving, 4096)
    incoming_slots = incoming[0, :, -1].astype(jnp.int32) - 1
    local_slots = jnp.where(parent // bricks == own_index, parent % bricks, -1)
    all_slots = jnp.concatenate([local_slots, incoming_slots])
    receive_pick = (jnp.arange(bricks, dtype=jnp.int32)[:, None] == all_slots[None, :]).astype(
        jnp.bfloat16
    )
    arrived = select_both(receive_pick, both_pooled, incoming[:, :, :2048])
    coarse_in = place_octants(arrived)
    lone = lone_bricks(coarse_bricks)
    preactivation = brick_pass(
        coarse_in, lone, live_count, whole_coarse[None], None, jnp.float32, False
    )[0]
    hidden = jax.nn.silu(preactivation).astype(jnp.bfloat16)
    own_project = lax.dynamic_slice_in_dim(
        whole_project, core * half_channels, half_channels, 0
    )
    coarse_out = jnp.einsum(
        "cj,bjv->bcv", own_project, hidden, preferred_element_type=jnp.float32
    ).astype(jnp.bfloat16)
    back_source = select_rows(receive_pick.T, split_octants(coarse_out).reshape(bricks, -1))
    last_brick = devices * bricks
    near_local = jnp.where(
        neighbours >= last_brick, 3 * bricks, neighbours - (own_index - 1) * bricks
    ).astype(jnp.int32)
    slots = jnp.arange(bricks, dtype=jnp.int32)[:, None] + bricks
    near = jnp.concatenate([near_local[:, :13], slots, near_local[:, 13:]], axis=1)
    own_weight = lax.dynamic_slice_in_dim(whole_fine, core * half_channels, half_channels, 2)
    back_feats, rode_back = brick_pass(
        grad_fields,
        near,
        live_count,
        flip_weight(own_weight)[None],
        None,
        jnp.bfloat16,
        True,
        back_source[bricks:].reshape(2, moving * 16, 128),
        3,
    )
    up_octants = gather_back(
        back_source[:bricks], send_pick, rode_back.reshape(2 * moving, -1)
    ).reshape(bricks, half_channels, 64)
    mixed_feats = ((feats.astype(jnp.float32) + enlarge(up_octants)) * live_mask).astype(
        jnp.bfloat16
    )
    up_grad = pool_sum(back_feats).astype(jnp.bfloat16).reshape(bricks, -1)
    outgoing_grad = select_rows(send_pick, up_grad)
    incoming_grad, feat_fields, both_grad = trade(
        outgoing_grad.reshape(2, moving * 16, 128),
        mixed_feats,
        [up_grad.reshape(bricks * 16, 128)],
        4,
    )
    coarse_grad = place_octants(
        select_both(receive_pick, both_grad, incoming_grad.reshape(2, 2 * moving, 2048))
    )
    hidden_half = hidden.shape[1] // 2
    own_hidden = lax.dynamic_slice_in_dim(hidden, core * hidden_half, hidden_half, 1)
    project_matrix = jnp.einsum(
        "bcv,bjv->cj", coarse_grad, own_hidden, preferred_element_type=jnp.float32
    )
    hidden_grad = jnp.einsum(
        "cj,bcv->bjv", whole_project, coarse_grad, preferred_element_type=jnp.float32
    )
    sigmoid_pre = jax.nn.sigmoid(preactivation)
    pre_grad = (hidden_grad * sigmoid_pre * (1.0 + preactivation * (1.0 - sigmoid_pre))).astype(
        jnp.bfloat16
    )
    own_pre_grad = lax.dynamic_slice_in_dim(pre_grad, core * hidden_half, hidden_half, 1)
    coarse_total = brick_pass(
        coarse_in, lone, live_count, None, own_pre_grad, None, False
    )[0]
    own_coarse = flip_weight(
        lax.dynamic_slice_in_dim(whole_coarse, core * half_channels, half_channels, 2)
    )
    coarse_terms = brick_pass(
        pre_grad.reshape(2 * coarse_bricks, hidden_half, 512),
        lone_bricks(2 * coarse_bricks),
        live_count,
        jnp.stack([own_coarse[:, :, :hidden_half], own_coarse[:, :, hidden_half:]]),
        None,
        jnp.float32,
        False,
    )[0]
    coarse_back = (
        coarse_terms.reshape(coarse_bricks, 2, half_channels, 512).sum(1).astype(jnp.bfloat16)
    )
    down_source = select_rows(receive_pick.T, split_octants(coarse_back).reshape(bricks, -1))
    out_feats, wide_sum, slim_sum, rode_down = brick_pass(
        feat_fields,
        near,
        live_count,
        fine_weight[None],
        grad_rows,
        jnp.bfloat16,
        True,
        down_source[bricks:].reshape(2, moving * 16, 128),
        5,
        wide_pieces(coarse_total, project_matrix),
    )
    down_grad = gather_back(
        down_source[:bricks], send_pick, rode_down.reshape(2 * moving, -1)
    ).reshape(bricks, half_channels, 64)
    grad_feats = (back_feats.astype(jnp.float32) + live_mask * enlarge(down_grad) * 0.125).astype(
        jnp.bfloat16
    )
    fine_scale = 1.0 / math.sqrt(512.0 * bricks * devices)
    coarse_scale = 1.0 / math.sqrt(512.0 * coarse_bricks * devices)
    fine_weight_grad, coarse_weight_grad, project_total = finish(
        slim_sum, wide_sum, half_channels, hidden_half, (fine_scale, coarse_scale)
    )
    project_weight_grad = project_total * coarse_scale
    return (out_feats, grad_feats, fine_weight_grad, coarse_weight_grad, project_weight_grad)


def solution(mesh):
    placed = (
        P("space", "chan", None),
        P("space"),
        P("space", None),
        P("space"),
        P(None, "chan", None),
        P(None, "chan", None),
        P(None, "chan"),
        P("space", "chan", None),
    )
    return jax.shard_map(
        per_device,
        mesh=mesh,
        in_specs=placed,
        out_specs=(
            P("space", "chan", None),
            P("space", "chan", None),
            P(None, "chan", None),
            P(None, "chan", None),
            P(None, "chan"),
        ),
        check_vma=False,
    )
```

time: 139 us -> 133 us (0.957)
  Pallas kernels: 107 us -> 99.7 us
    pallas_call x7 -> x6, Pallas kernels: 74.4 us -> 67.1 us  [the longest x5 64.7 us: brick_pass(): pl.pallas_call(lambda *refs: brick_kernel(count, masked, names, *refs), g...]
    unnamed x46 -> x39, local copies, waits for them, and re-layouts: 8.77 us -> 9.22 us
where the time goes in v3:
time: 133 us; the launch traced here: 132 us
  Pallas kernels  99.7 us (75%)
  local copies, waits for them, and re-layouts  19.5 us (15%)
  matrix products  5.66 us (4%)
  other arithmetic  5.07 us (4%)
  between operations  1.93 us (1%)
    pallas_call x5, Pallas kernels, brick_pass(): pl.pallas_call(lambda *refs: brick_kernel(count, masked, names, *refs), g...  64.7 us
    pallas_call x2, Pallas kernels, trade(): pl.pallas_call(lambda *refs: trade_kernel(count, amount, *refs), in_specs...  32.6 us
    unnamed x39, local copies, waits for them, and re-layouts  9.22 us
    gather x5, local copies, waits for them, and re-layouts, weight_blocks(): taps = weight.reshape(3, 9, rows, channels)[:, TAP_ORDER]  2.99 us

profile of v3, /device:TPU:8, one launch (start us, length us, event | category | flops | bytes accessed | tf_op | source)
XLA Modules:
  0.0 131.9 jit_solution(14294928382583276802)
XLA Ops:
  0.6 0.7 subtract_select_fusion
  2.2 0.7 compare_select_fusion.1
  3.3 1.2 fusion.16
  4.8 1.1 multiply_convert_fusion.refs_1_.refs_4_
  6.0 0.9 copy-done
  7.0 0.7 copy-done.5
  7.7 17.7 %shard_map.245 = (bf16[2,2,32,128]{3,2,1,0:T(8,128)(2,1)S(1)}, bf16[2,3,8,32,512]{4,3,2,1,0:T(8,128)(2,1)S(1)}, bf16[2,128,128]{2,1,0:T(8,128)(2,1)S(1)}, bf16[2...) custom-call(bf16[2,32,128]{2,1,0:T(8,128)(2,1)S(1)} %bitcast.187, ...), custom_call_target="tpu_custom_call" | custom-call | tf_op jit(solution)/shard_map/pallas_call | solution.py:177
  25.4 1.2 copy-done.8
  27.2 0.6 gather_fusion
  29.2 1.3 %slice_bitcast_fusion.7 = (bf16[27,64,64]{2,1,0:T(8,128)(2,1)}, bf16[27,64,64]{2,1,0:T(8,128)(2,1)}, bf16[1,27,64,64]{3,2,1,0:T(8,128)(2,1)S(1)}, bf16[1,27,64,64]{3,2,1,0:T(8,128)(2,1)S(1)}) fusion(bf16[2,27,64,64]{3,2,1,0:T(8,128)(2,1)S(1)} %get-tuple-element.26), kind=kLoop, calls=%fused_computation.140 | loop fusion | bytes 1327104 | tf_op jit(solution)/shard_map/squeeze | solution.py:612
  31.3 0.6 gather_fusion.1
  32.3 1.5 %shard_map.246 = f32[1,128,512]{2,1,0:T(8,128)S(1)} custom-call(s32[1,27]{1,0:T(1,128)S(1)} %compare_select_fusion.refs_0_, s32[1]{0:T(128)} %copy.63.refs_1_, bf16[1,64,512]{2,1,0:T(8,128)(2,1)S(1)} %fusion.13.refs_2_, bf16[1,3,128,640]{3,2,1,0:T(8,128)(2,1)S(1)} %copy.33.refs_3_), custom_call_target="tpu_custom_call" | custom-call | flops 251658240 | bytes 65536 | tf_op jit(solution)/shard_map/pallas_call | solution.py:525
  33.9 0.5 fusion.14
  34.8 1.4 %copy-done.9 = bf16[2,3,8,32,512]{4,3,2,1,0:T(8,128)(2,1)S(1)} copy-done((bf16[2,3,8,32,512]{4,3,2,1,0:T(8,128)(2,1)S(1)}, bf16[2,3,8,32,512]{4,3,2,1,0:T(8,128)(2,1)}, u32[]{:S(2)}) %copy-start.9) | copy-done | bytes 1572888
  36.2 11.6 %shard_map.247 = (bf16[8,32,512]{2,1,0:T(8,128)(2,1)S(1)}, bf16[2,16,128]{2,1,0:T(8,128)(2,1)S(1)}) custom-call(s32[8,27]{1,0:T(8,128)S(1)} %pad_add_fusion.refs_0_, s32[1]{0:T(128)} %copy.63.refs_1_, bf16[2,3,8,32,512]{4,3,2,1,0:T(8,128)(2,1)S(1)} %copy-done.9, bf16[1,3,32,640]{3,2,1,0:T(8,128)(2,1)S(1)} %stack_reshape.15.refs_3_, ...), custom_call_target="tpu_custom_call" | custom-call | flops 503316480 | bytes 1572864 | tf_op jit(solution)/shard_map/pallas_call | solution.py:525
  49.0 14.9 %shard_map.248 = (bf16[2,2,16,128]{3,2,1,0:T(8,128)(2,1)S(1)}, bf16[2,3,8,32,512]{4,3,2,1,0:T(8,128)(2,1)S(1)}, bf16[2,128,128]{2,1,0:T(8,128)(2,1)S(1)}) custom-call(bf16[2,16,128]{2,1,0:T(8,128)(2,1)S(1)} %bitcast.188, bf16[8,32,512]{2,1,0:T(8,128)(2,1)S(1)} %fusion.6.refs_1_, bf16[128,128]{1,0:T(8,128)(2,1)S(1)} %reshape_reshape.16.refs_2_), custom_call_target="tpu_custom_call" | custom-call | tf_op jit(solution)/shard_map/pallas_call | solution.py:177
  63.9 1.2 copy-done.6
  65.1 0.6 gather_fusion.2
  67.4 1.2 shard_map.249
  68.9 0.3 dynamic-slice_maximum_fusion
  69.7 0.6 gather_fusion.4
  70.9 0.6 gather_fusion.3
  72.0 2.3 %shard_map.250 = f32[2,32,512]{2,1,0:T(8,128)S(1)} custom-call(s32[2,27]{1,0:T(2,128)S(1)} %iota_select_fusion.refs_0_, s32[1]{0:T(128)} %copy.63.refs_1_, bf16[2,64,512]{2,1,0:T(8,128)(2,1)S(1)} %bitcast.185, bf16[2,3,32,640]{3,2,1,0:T(8,128)(2,1)S(1)} %pad_maximum_fusion.1.refs_3_), custom_call_target="tpu_custom_call" | custom-call | flops 125829120 | bytes 131072 | tf_op jit(solution)/shard_map/pallas_call | solution.py:525
  75.1 1.4 %copy-done.7 = bf16[2,3,8,32,512]{4,3,2,1,0:T(8,128)(2,1)S(1)} copy-done((bf16[2,3,8,32,512]{4,3,2,1,0:T(8,128)(2,1)S(1)}, bf16[2,3,8,32,512]{4,3,2,1,0:T(8,128)(2,1)}, u32[]{:S(2)}) %copy-start.7) | copy-done | bytes 1572888
  76.5 48.1 %shard_map.251 = (bf16[8,32,512]{2,1,0:T(8,128)(2,1)S(1)}, f32[4,4,8,1,8,128]{5,4,3,2,1,0:T(8,128)S(1)}, f32[4,4,8,1,4,128]{5,4,3,2,1,0:T(4,128)S(1)}, bf16[2,16,128]{2,1,0:T(8,128)(2,1)S(1)}) custom-call(s32[8,27]{1,0:T(8,128)S(1)} %pad_add_fusion.refs_0_, s32[1]{0:T(128)} %copy.63.refs_1_, bf16[2,3,8,32,512]{4,3,2,1,0:T(8,128)(2,1)S(1)} %copy-done.7, ...), custom_call_target="tpu_custom_call" | custom-call | flops 1006632960 | bytes 1572864 | tf_op jit(solution)/shard_map/pallas_call | solution.py:525
  124.6 0.8 copy-done.2
  125.4 0.7 copy-done.4
  126.4 0.9 fusion.5
  127.4 2.4 %shard_map.252 = (f32[27,32,64]{2,1,0:T(8,128)}, f32[27,64,64]{2,1,0:T(8,128)}) custom-call(f32[128,4,128]{2,1,0:T(4,128)} %bitcast.186, f32[128,8,128]{2,1,0:T(8,128)} %bitcast.182), custom_call_target="tpu_custom_call" | custom-call | tf_op jit(solution)/shard_map/pallas_call | solution.py:571
  129.8 0.7 slice_multiply_fusion
  130.5 0.7 mul.93
  131.2 0.7 copy.64
  (113 shorter events, 10.1 us)
Async XLA Ops:
  0.6 5.4 %copy-start.3 = (bf16[27,64,64]{2,1,0:T(8,128)(2,1)S(1)}, bf16[27,64,64]{2,1,0:T(8,128)(2,1)}, u32[]{:S(2)}) copy-start(bf16[27,64,64]{2,1,0:T(8,128)(2,1)} %refs_3_.1) | copy-start | bytes 663556
  6.0 0.9 copy-start
  7.0 0.7 copy-start.5
  25.4 1.2 copy-start.8
  26.5 0.7 copy-start.15
  27.2 1.8 %copy-start.10 = (bf16[8,64,512]{2,1,0:T(8,128)(2,1)S(1)}, bf16[8,64,512]{2,1,0:T(8,128)(2,1)}, u32[]{:S(2)}) copy-start(bf16[8,64,512]{2,1,0:T(8,128)(2,1)} %constant.117) | copy-start | bytes 1572868
  33.8 14.1 %copy-start.14 = (bf16[512,64,1]{0,1,2:T(8,128)(2,1)S(1)}, bf16[512,64,1]{0,1,2:T(8,128)(2,1)}, u32[]{:S(2)}) copy-start(bf16[512,64,1]{0,1,2:T(8,128)(2,1)} %constant.123) | copy-start | bytes 196612
  33.9 14.8 %copy-start.13 = (bf16[8,32,512]{2,1,0:T(8,128)(2,1)S(1)}, bf16[8,32,512]{2,1,0:T(8,128)(2,1)}, u32[]{:S(2)}) copy-start(bf16[8,32,512]{2,1,0:T(8,128)(2,1)} %param.22) | copy-start | bytes 786436
  34.8 1.4 %copy-start.9 = (bf16[2,3,8,32,512]{4,3,2,1,0:T(8,128)(2,1)S(1)}, bf16[2,3,8,32,512]{4,3,2,1,0:T(8,128)(2,1)}, u32[]{:S(2)}) copy-start(bf16[2,3,8,32,512]{4,3,2,1,0:T(8,128)(2,1)} %copy-done.8) | copy-start | bytes 4718596
  36.2 28.9 %copy-start.1 = (bf16[27,32,64]{2,1,0:T(8,128)(2,1)S(1)}, bf16[27,32,64]{2,1,0:T(8,128)(2,1)}, u32[]{:S(2)}) copy-start(bf16[27,32,64]{2,1,0:T(8,128)(2,1)} %refs_4_.1) | copy-start | bytes 331780
  63.9 1.2 copy-start.6
  67.1 1.9 %copy-start.11 = (bf16[27,64,64]{2,1,0:T(8,128)(2,1)S(1)}, bf16[27,64,64]{2,1,0:T(8,128)(2,1)}, u32[]{:S(2)}) copy-start(bf16[27,64,64]{2,1,0:T(8,128)(2,1)} %get-tuple-element.44) | copy-start | bytes 663556
  67.1 1.9 %copy-start.12 = (bf16[27,64,64]{2,1,0:T(8,128)(2,1)S(1)}, bf16[27,64,64]{2,1,0:T(8,128)(2,1)}, u32[]{:S(2)}) copy-start(bf16[27,64,64]{2,1,0:T(8,128)(2,1)} %get-tuple-element.45) | copy-start | bytes 663556
  75.1 1.4 %copy-start.7 = (bf16[2,3,8,32,512]{4,3,2,1,0:T(8,128)(2,1)S(1)}, bf16[2,3,8,32,512]{4,3,2,1,0:T(8,128)(2,1)}, u32[]{:S(2)}) copy-start(bf16[2,3,8,32,512]{4,3,2,1,0:T(8,128)(2,1)} %copy-done.6) | copy-start | bytes 4718596
  124.6 0.8 copy-start.2
  125.4 0.7 copy-start.4

commit v4 on v3

--- a/solution.py
+++ b/solution.py
@@ -141,7 +141,7 @@
     shares = refs[2 : 2 + amount]
     rows_all, fields = refs[2 + amount : 4 + amount]
     shares_all = refs[4 + amount : 4 + 2 * amount]
-    send_sems, recv_sems = refs[4 + 2 * amount :]
+    send_sems, recv_sems, keep_sem = refs[4 + 2 * amount :]
     core = lax.axis_index("chan")
     left, right, mate = nearby(count)
     left_mate, right_mate = (left[0], 1 - core), (right[0], 1 - core)
@@ -159,7 +159,8 @@
         quick.append(send(8 + number, share, share_all.at[core], mate))
         share_all[core] = share[...]
     quick.append(send(8 + amount, own, fields.at[core, 1], mate))
-    fields[core, 1] = own[...]
+    keep = pltpu.make_async_copy(own, fields.at[core, 1], keep_sem)
+    keep.start()
     to_right.wait_recv()
     quick.append(send(6, fields.at[core, 0], fields.at[core, 0], mate))
     to_left.wait_recv()
@@ -168,6 +169,7 @@
         copy.wait_recv()
     for copy in quick + [to_right, to_left]:
         copy.wait_send()
+    keep.wait()
 
 
 def trade(rows, own, shares, number):
@@ -177,14 +179,18 @@
     return pl.pallas_call(
         lambda *refs: trade_kernel(count, amount, *refs),
         in_specs=[pl.BlockSpec(memory_space=pltpu.VMEM)] * (2 + amount),
-        out_specs=[pl.BlockSpec(memory_space=pltpu.VMEM)] * (2 + amount),
+        out_specs=[
+            pl.BlockSpec(memory_space=pl.ANY if place == 1 else pltpu.VMEM)
+            for place in range(2 + amount)
+        ],
         out_shape=[jax.ShapeDtypeStruct(shape, rows.dtype) for shape in shapes],
         scratch_shapes=[
             pltpu.SemaphoreType.DMA((9 + amount,)),
             pltpu.SemaphoreType.DMA((9 + amount,)),
+            pltpu.SemaphoreType.DMA,
         ],
         compiler_params=pltpu.CompilerParams(
-            collective_id=number, has_side_effects=True, vmem_limit_bytes=32 * 1024 * 1024
+            collective_id=number, has_side_effects=True, vmem_limit_bytes=12 * 1024 * 1024
         ),
     )(rows, own, *shares)
 
@@ -212,79 +218,62 @@
 
 
 def torus_sizes(count):
-    return (4, 4, 8) if count == 128 else (1, 1, count)
+    return (16, 8) if count == 128 else (1, count)
 
 
 class TorusSum:
-    def __init__(self, count, axes, refs, label):
-        size_y, size_x, size_z = torus_sizes(count)
+    def __init__(self, count, refs, label):
+        self.plane, self.depth = torus_sizes(count)
         me, self.core = lax.axis_index("space"), lax.axis_index("chan")
-        self.sizes = {"y": size_y, "x": size_x, "z": size_z}
-        self.place = {
-            "y": me // (size_z * size_x),
-            "x": me // size_z % size_x,
-            "z": me % size_z,
-        }
-        self.axes = axes
+        self.at, self.level = me // self.depth, me % self.depth
         self.refs = {name: refs[label + name] for name in SUM_NAMES}
 
-    def device(self, axis, step):
-        at = dict(self.place)
-        at[axis] = (at[axis] + step) % self.sizes[axis]
-        return (at["y"] * self.sizes["x"] + at["x"]) * self.sizes["z"] + at["z"], self.core
+    def across(self, step):
+        return (self.at + step) % self.plane * self.depth + self.level, self.core
+
+    def along(self, step):
+        return self.at * self.depth + (self.level + step) % self.depth, self.core
 
     def peers(self):
-        return [
-            self.device(axis, step) for axis in self.axes for step in range(1, self.sizes[axis])
+        return [self.across(step) for step in range(1, self.plane)] + [
+            self.along(step) for step in range(1, self.depth)
         ]
 
     def copies(self, phase):
         refs = self.refs
-        axis = (self.axes + self.axes[::-1])[phase]
         made = []
-        for step in range(1, self.sizes[axis]):
-            other = (self.place[axis] + step) % self.sizes[axis]
-            if phase < 3:
-                source = refs[("data", "own_a", "own_b")[phase]].at[other]
-                target = refs[("part_a", "part_b", "part_z")[phase]].at[step - 1]
+        for step in range(1, self.depth if phase == 1 else self.plane):
+            if phase == 0:
+                source = refs["data"].at[(self.at + step) % self.plane]
+                target = refs["part"].at[step - 1]
+            elif phase == 1:
+                source = target = refs["levels"].at[self.level]
             else:
-                here = [self.place[name] for name in self.axes]
-                if phase == 3:
-                    source = refs["whole"].at[here[2]]
-                elif phase == 4:
-                    source = refs["total"].at[here[0], here[1]]
-                else:
-                    source = refs["total"].at[here[0]]
-                target = source
+                source = target = refs["total"].at[self.at]
             made.append(
                 pltpu.make_async_remote_copy(
                     src_ref=source,
                     dst_ref=target,
                     send_sem=refs["send"].at[phase, step - 1],
                     recv_sem=refs["recv"].at[phase, step - 1],
-                    device_id=self.device(axis, step),
+                    device_id=self.along(step) if phase == 1 else self.across(step),
                     device_id_type=pl.DeviceIdType.MESH,
                 )
             )
         return made
 
-    def summed(self, kept, parts, axis):
-        value = self.refs[kept][self.place[axis]]
-        for step in range(1, self.sizes[axis]):
-            value = value + self.refs[parts][step - 1]
-        return value
-
     def start(self, phase):
         refs = self.refs
-        at_a, at_b, at_z = [self.place[axis] for axis in self.axes]
         if phase == 1:
-            refs["own_a"][...] = self.summed("data", "part_a", self.axes[0])
+            value = refs["data"][self.at]
+            for step in range(1, self.plane):
+                value = value + refs["part"][step - 1]
+            refs["levels"][self.level] = value
         elif phase == 2:
-            refs["own_b"][...] = self.summed("own_a", "part_b", self.axes[1])
-        elif phase == 3:
-            refs["whole"][at_z] = self.summed("own_b", "part_z", "z")
-        elif phase == 4:
-            refs["total"][at_a, at_b] = refs["whole"][...]
+            value = refs["levels"][0]
+            for level in range(1, self.depth):
+                value = value + refs["levels"][level]
+            refs["total"][self.at] = value
         for copy in self.copies(phase):
             copy.start()
 
@@ -293,38 +282,27 @@
             copy.wait_recv()
 
     def leave(self):
-        for phase in range(6):
+        for phase in range(3):
             for copy in self.copies(phase):
                 copy.wait_send()
 
 
-SUM_NAMES = (
-    "data", "part_a", "own_a", "part_b", "own_b", "part_z", "whole", "total", "send", "recv"
-)
-
-
-def sum_scratch(count, axes, rows, label, with_data):
-    sizes = dict(zip("yxz", torus_sizes(count)))
-    a, b, z = [sizes[axis] for axis in axes]
-    piece = (128 // count, rows, 128)
-    shapes = {
-        "part_a": (max(1, a - 1), b, z),
-        "own_a": (b, z),
-        "part_b": (max(1, b - 1), z),
-        "own_b": (z,),
-        "part_z": (z - 1,),
-        "whole": (z,),
-        "total": (a, b, z),
+SUM_NAMES = ("data", "part", "levels", "total", "send", "recv")
+
+
+def sum_scratch(count, rows, label, with_data):
+    plane, depth = torus_sizes(count)
+    piece = (128 // plane, rows, 128)
+    firsts = {"part": max(1, plane - 1), "levels": depth, "total": plane}
+    if with_data:
+        firsts["data"] = plane
+    scratch = {
+        label + name: pltpu.VMEM((first,) + piece, jnp.float32) for name, first in firsts.items()
     }
-    if with_data:
-        shapes["data"] = (a, b, z)
-    scratch = {
-        label + name: pltpu.VMEM(shape + piece, jnp.float32) for name, shape in shapes.items()
-    }
-    most = max(a, b, z) - 1
-    scratch[label + "send"] = pltpu.SemaphoreType.DMA((6, most))
-    scratch[label + "recv"] = pltpu.SemaphoreType.DMA((6, most))
-    return scratch, (a, b, z) + piece
+    most = max(plane, depth) - 1
+    scratch[label + "send"] = pltpu.SemaphoreType.DMA((3, most))
+    scratch[label + "recv"] = pltpu.SemaphoreType.DMA((3, most))
+    return scratch, (plane,) + piece
 
 
 def fine_pieces(acc):
@@ -345,8 +323,8 @@
     last = pl.num_programs(0) - 1
     sums = "wide_data" in refs
     if sums:
-        wide = TorusSum(count, ("x", "y", "z"), refs, "wide_")
-        slim = TorusSum(count, ("y", "x", "z"), refs, "slim_")
+        wide = TorusSum(count, refs, "wide_")
+        slim = TorusSum(count, refs, "slim_")
 
     @pl.when(brick == 0)
     def fill():
@@ -441,24 +419,20 @@
     def close():
         if sums:
             acc, data = refs["acc"], refs["slim_data"]
-            cells = list(np.ndindex(data.shape[:4]))
+            cells = list(np.ndindex(data.shape[:2]))
             spans = fine_pieces(acc)
             for cell, span in zip(cells, spans):
                 data[cell] = acc[span]
             for cell in cells[len(spans) :]:
-                data[cell] = jnp.zeros(data.shape[4:], jnp.float32)
+                data[cell] = jnp.zeros(data.shape[2:], jnp.float32)
             slim.start(0)
-            for phase in range(3):
-                wide.wait(2 + phase)
-                wide.start(3 + phase)
-                slim.wait(phase)
-                slim.start(phase + 1)
-            wide.wait(5)
+            wide.wait(2)
             refs["wide_out"][...] = refs["wide_total"][...]
-            for phase in range(3, 5):
-                slim.wait(phase)
-                slim.start(phase + 1)
-            slim.wait(5)
+            slim.wait(0)
+            slim.start(1)
+            slim.wait(1)
+            slim.start(2)
+            slim.wait(2)
             refs["slim_out"][...] = refs["slim_total"][...]
             wide.leave()
             slim.leave()
@@ -506,8 +480,8 @@
         if wide is None:
             result("total", (3, rows, WIDTH), jnp.float32)
     if wide is not None:
-        wide_scratch, wide_shape = sum_scratch(count, "xyz", 8, "wide_", False)
-        slim_scratch, slim_shape = sum_scratch(count, "yxz", 4, "slim_", True)
+        wide_scratch, wide_shape = sum_scratch(count, 8, "wide_", False)
+        slim_scratch, slim_shape = sum_scratch(count, 4, "slim_", True)
         scratch.update(wide_scratch)
         scratch.update(slim_scratch)
         ins["wide_data"] = (wide.reshape(wide_shape), whole(wide_shape))
@@ -521,6 +495,7 @@
         scratch["ride_recv"] = pltpu.SemaphoreType.DMA((2,))
     names = list(ins) + list(outs) + list(scratch)
     remote = {"collective_id": number, "has_side_effects": True} if count else {}
+    room = 12 if slots < 8 else 20 if wide is None else 30
     products = (weight is not None) + (grad_rows is not None)
     return pl.pallas_call(
         lambda *refs: brick_kernel(count, masked, names, *refs),
@@ -529,7 +504,7 @@
         out_specs=[spec for _, spec in outs.values()],
         out_shape=[shape for shape, _ in outs.values()],
         scratch_shapes=list(scratch.values()),
-        compiler_params=pltpu.CompilerParams(vmem_limit_bytes=48 * 1024 * 1024, **remote),
+        compiler_params=pltpu.CompilerParams(vmem_limit_bytes=room * 1024 * 1024, **remote),
         cost_estimate=pl.CostEstimate(
             flops=amount * products * 2 * rows * 3 * WIDTH * 512,
             bytes_accessed=slots * 64 * 512 * 2,
@@ -540,8 +515,10 @@
 
 def weight_blocks(weight):
     rows, channels = weight.shape[1:]
-    taps = weight.reshape(3, 9, rows, channels)[:, TAP_ORDER]
-    taps = jnp.concatenate([taps, jnp.zeros_like(taps[:, :1])], axis=1)
+    taps = weight.reshape(3, 9, rows, channels)
+    taps = jnp.stack(
+        [taps[:, tap] for tap in TAP_ORDER] + [jnp.zeros_like(taps[:, 0])], axis=1
+    )
     return jnp.transpose(taps, (0, 2, 1, 3)).reshape(3, rows, WIDTH)
 
 

time: 133 us -> 137 us (1.030)
  local copies, waits for them, and re-layouts: 19.5 us -> 21.8 us
    unnamed x39 -> x73, local copies, waits for them, and re-layouts: 9.22 us -> 12.3 us
    another operation x5 -> x8, local copies, waits for them, and re-layouts: 0.92 us -> 3.95 us  [the longest x5 3.64 us: weight_blocks(): jnp.stack([taps[:, tap] for tap in TAP_ORDER] + [jnp.zeros_like(taps[:, 0...]
    gather x5 -> x0, local copies, waits for them, and re-layouts: 2.99 us -> none  [weight_blocks(): taps = weight.reshape(3, 9, rows, channels)[:, TAP_ORDER]]
where the time goes in v4:
time: 137 us; the launch traced here: 136 us
  Pallas kernels  100 us (73%)
  local copies, waits for them, and re-layouts  21.8 us (16%)
  other arithmetic  5.7 us (4%)
  matrix products  5.67 us (4%)
  between operations  2.15 us (2%)
    pallas_call x5, Pallas kernels, brick_pass(): pl.pallas_call(lambda *refs: brick_kernel(count, masked, names, *refs), g...  65.4 us
    pallas_call x2, Pallas kernels, trade(): pl.pallas_call(lambda *refs: trade_kernel(count, amount, *refs), in_specs...  32.6 us
    unnamed x73, local copies, waits for them, and re-layouts  12.3 us
    another operation x5, local copies, waits for them, and re-layouts, weight_blocks(): jnp.stack([taps[:, tap] for tap in TAP_ORDER] + [jnp.zeros_like(taps[:, 0...  3.64 us

profile of v4, /device:TPU:8, one launch (start us, length us, event | category | flops | bytes accessed | tf_op | source)
XLA Modules:
  0.0 135.7 jit_solution(18106175853105172544)
XLA Ops:
  0.6 0.7 subtract_select_fusion
  2.2 0.7 compare_select_fusion.1
  3.3 1.2 fusion.16
  4.8 1.1 multiply_convert_fusion.refs_1_.refs_4_
  6.0 0.9 copy-done
  7.0 0.7 copy-done.5
  7.7 17.7 %shard_map.191 = (bf16[2,2,32,128]{3,2,1,0:T(8,128)(2,1)S(1)}, bf16[2,3,8,32,512]{4,3,2,1,0:T(8,128)(2,1)S(1)}, bf16[2,128,128]{2,1,0:T(8,128)(2,1)S(1)}, bf16[2...) custom-call(bf16[2,32,128]{2,1,0:T(8,128)(2,1)S(1)} %bitcast.178, ...), custom_call_target="tpu_custom_call" | custom-call | tf_op jit(solution)/shard_map/pallas_call | solution.py:179
  25.4 1.2 copy-done.8
  27.9 0.9 stack.18
  30.1 1.1 slice_bitcast_fusion.7
  33.0 1.5 %shard_map.192 = f32[1,128,512]{2,1,0:T(8,128)S(1)} custom-call(s32[1,27]{1,0:T(1,128)S(1)} %compare_select_fusion.refs_0_, s32[1]{0:T(128)} %copy.168.refs_1_, bf16[1,64,512]{2,1,0:T(8,128)(2,1)S(1)} %fusion.13.refs_2_, bf16[1,3,128,640]{3,2,1,0:T(8,128)(2,1)S(1)} %copy.71.refs_3_), custom_call_target="tpu_custom_call" | custom-call | flops 251658240 | bytes 65536 | tf_op jit(solution)/shard_map/pallas_call | solution.py:500
  34.5 0.5 fusion.14
  35.4 1.4 %copy-done.9 = bf16[2,3,8,32,512]{4,3,2,1,0:T(8,128)(2,1)S(1)} copy-done((bf16[2,3,8,32,512]{4,3,2,1,0:T(8,128)(2,1)S(1)}, bf16[2,3,8,32,512]{4,3,2,1,0:T(8,128)(2,1)}, u32[]{:S(2)}) %copy-start.9) | copy-done | bytes 1572888
  36.8 11.7 %shard_map.193 = (bf16[8,32,512]{2,1,0:T(8,128)(2,1)S(1)}, bf16[2,16,128]{2,1,0:T(8,128)(2,1)S(1)}) custom-call(s32[8,27]{1,0:T(8,128)S(1)} %pad_add_fusion.refs_0_, s32[1]{0:T(128)} %copy.168.refs_1_, bf16[2,3,8,32,512]{4,3,2,1,0:T(8,128)(2,1)S(1)} %copy-done.9, bf16[1,3,32,640]{3,2,1,0:T(8,128)(2,1)S(1)} %stack_reshape.15.refs_3_, ...), custom_call_target="tpu_custom_call" | custom-call | flops 503316480 | bytes 1572864 | tf_op jit(solution)/shard_map/pallas_call | solution.py:500
  49.7 14.9 %shard_map.194 = (bf16[2,2,16,128]{3,2,1,0:T(8,128)(2,1)S(1)}, bf16[2,3,8,32,512]{4,3,2,1,0:T(8,128)(2,1)S(1)}, bf16[2,128,128]{2,1,0:T(8,128)(2,1)S(1)}) custom-call(bf16[2,16,128]{2,1,0:T(8,128)(2,1)S(1)} %bitcast.179, bf16[8,32,512]{2,1,0:T(8,128)(2,1)S(1)} %fusion.6.refs_1_, bf16[128,128]{1,0:T(8,128)(2,1)S(1)} %reshape_reshape.16.refs_2_), custom_call_target="tpu_custom_call" | custom-call | tf_op jit(solution)/shard_map/pallas_call | solution.py:179
  64.7 1.2 copy-done.6
  66.3 0.9 stack.20
  68.7 1.2 shard_map.195
  70.3 0.3 dynamic-slice_maximum_fusion
  71.9 0.9 stack.22
  74.1 0.9 stack.21
  75.3 2.3 %shard_map.196 = f32[2,32,512]{2,1,0:T(8,128)S(1)} custom-call(s32[2,27]{1,0:T(2,128)S(1)} %iota_select_fusion.refs_0_, s32[1]{0:T(128)} %copy.168.refs_1_, bf16[2,64,512]{2,1,0:T(8,128)(2,1)S(1)} %bitcast.176, bf16[2,3,32,640]{3,2,1,0:T(8,128)(2,1)S(1)} %pad_maximum_fusion.refs_3_), custom_call_target="tpu_custom_call" | custom-call | flops 125829120 | bytes 131072 | tf_op jit(solution)/shard_map/pallas_call | solution.py:500
  77.7 0.3 fusion.15
  78.4 1.4 %copy-done.7 = bf16[2,3,8,32,512]{4,3,2,1,0:T(8,128)(2,1)S(1)} copy-done((bf16[2,3,8,32,512]{4,3,2,1,0:T(8,128)(2,1)S(1)}, bf16[2,3,8,32,512]{4,3,2,1,0:T(8,128)(2,1)}, u32[]{:S(2)}) %copy-start.7) | copy-done | bytes 1572888
  79.8 48.6 %shard_map.197 = (bf16[8,32,512]{2,1,0:T(8,128)(2,1)S(1)}, f32[16,8,8,128]{3,2,1,0:T(8,128)S(1)}, f32[16,8,4,128]{3,2,1,0:T(4,128)S(1)}, bf16[2,16,128]{2,1,0:T(8,128)(2,1)S(1)}) custom-call(s32[8,27]{1,0:T(8,128)S(1)} %pad_add_fusion.refs_0_, s32[1]{0:T(128)} %copy.168.refs_1_, bf16[2,3,8,32,512]{4,3,2,1,0:T(8,128)(2,1)S(1)} %copy-done.7, ...), custom_call_target="tpu_custom_call" | custom-call | flops 1006632960 | bytes 1572864 | tf_op jit(solution)/shard_map/pallas_call | solution.py:500
  128.5 0.8 copy-done.2
  129.2 0.7 copy-done.4
  130.3 0.9 fusion.5
  131.2 2.4 %shard_map.198 = (f32[27,32,64]{2,1,0:T(8,128)}, f32[27,64,64]{2,1,0:T(8,128)}) custom-call(f32[128,4,128]{2,1,0:T(4,128)} %bitcast.177, f32[128,8,128]{2,1,0:T(8,128)} %bitcast.173), custom_call_target="tpu_custom_call" | custom-call | tf_op jit(solution)/shard_map/pallas_call | solution.py:548
  133.6 0.7 slice_multiply_fusion
  134.3 0.7 mul.93
  135.0 0.7 copy.169
  (146 shorter events, 12.3 us)
Async XLA Ops:
  0.6 5.4 %copy-start.3 = (bf16[27,64,64]{2,1,0:T(8,128)(2,1)S(1)}, bf16[27,64,64]{2,1,0:T(8,128)(2,1)}, u32[]{:S(2)}) copy-start(bf16[27,64,64]{2,1,0:T(8,128)(2,1)} %refs_3_.1) | copy-start | bytes 663556
  6.0 0.9 copy-start
  7.0 0.7 copy-start.5
  25.4 1.2 copy-start.8
  26.9 3.0 %copy-start.10 = (bf16[8,64,512]{2,1,0:T(8,128)(2,1)S(1)}, bf16[8,64,512]{2,1,0:T(8,128)(2,1)}, u32[]{:S(2)}) copy-start(bf16[8,64,512]{2,1,0:T(8,128)(2,1)} %constant.98) | copy-start | bytes 1572868
  34.4 14.2 %copy-start.14 = (bf16[512,64,1]{0,1,2:T(8,128)(2,1)S(1)}, bf16[512,64,1]{0,1,2:T(8,128)(2,1)}, u32[]{:S(2)}) copy-start(bf16[512,64,1]{0,1,2:T(8,128)(2,1)} %constant.99) | copy-start | bytes 196612
  34.5 14.9 %copy-start.13 = (bf16[8,32,512]{2,1,0:T(8,128)(2,1)S(1)}, bf16[8,32,512]{2,1,0:T(8,128)(2,1)}, u32[]{:S(2)}) copy-start(bf16[8,32,512]{2,1,0:T(8,128)(2,1)} %param.16) | copy-start | bytes 786436
  35.4 1.4 %copy-start.9 = (bf16[2,3,8,32,512]{4,3,2,1,0:T(8,128)(2,1)S(1)}, bf16[2,3,8,32,512]{4,3,2,1,0:T(8,128)(2,1)}, u32[]{:S(2)}) copy-start(bf16[2,3,8,32,512]{4,3,2,1,0:T(8,128)(2,1)} %copy-done.8) | copy-start | bytes 4718596
  36.8 29.0 %copy-start.1 = (bf16[27,32,64]{2,1,0:T(8,128)(2,1)S(1)}, bf16[27,32,64]{2,1,0:T(8,128)(2,1)}, u32[]{:S(2)}) copy-start(bf16[27,32,64]{2,1,0:T(8,128)(2,1)} %refs_4_.1) | copy-start | bytes 331780
  64.7 1.2 copy-start.6
  68.4 1.9 %copy-start.11 = (bf16[27,64,64]{2,1,0:T(8,128)(2,1)S(1)}, bf16[27,64,64]{2,1,0:T(8,128)(2,1)}, u32[]{:S(2)}) copy-start(bf16[27,64,64]{2,1,0:T(8,128)(2,1)} %get-tuple-element.44) | copy-start | bytes 663556
  68.4 1.9 %copy-start.12 = (bf16[27,64,64]{2,1,0:T(8,128)(2,1)S(1)}, bf16[27,64,64]{2,1,0:T(8,128)(2,1)}, u32[]{:S(2)}) copy-start(bf16[27,64,64]{2,1,0:T(8,128)(2,1)} %get-tuple-element.45) | copy-start | bytes 663556
  78.4 1.4 %copy-start.7 = (bf16[2,3,8,32,512]{4,3,2,1,0:T(8,128)(2,1)S(1)}, bf16[2,3,8,32,512]{4,3,2,1,0:T(8,128)(2,1)}, u32[]{:S(2)}) copy-start(bf16[2,3,8,32,512]{4,3,2,1,0:T(8,128)(2,1)} %copy-done.6) | copy-start | bytes 4718596
  128.4 0.8 copy-start.2
  129.2 0.7 copy-start.4

commit v5 on v4

--- a/solution.py
+++ b/solution.py
@@ -141,7 +141,7 @@
     shares = refs[2 : 2 + amount]
     rows_all, fields = refs[2 + amount : 4 + amount]
     shares_all = refs[4 + amount : 4 + 2 * amount]
-    send_sems, recv_sems, keep_sem = refs[4 + 2 * amount :]
+    send_sems, recv_sems, keep_sems = refs[4 + 2 * amount :]
     core = lax.axis_index("chan")
     left, right, mate = nearby(count)
     left_mate, right_mate = (left[0], 1 - core), (right[0], 1 - core)
@@ -155,12 +155,19 @@
     ]
     to_right = send(4, own, fields.at[core, 0], right)
     to_left = send(5, own, fields.at[core, 2], left)
+    kept = []
     for number, (share, share_all) in enumerate(zip(shares, shares_all)):
-        quick.append(send(8 + number, share, share_all.at[core], mate))
-        share_all[core] = share[...]
+        if len(share.shape) == 3:
+            half = share.shape[1]
+            spot = share_all.at[:, pl.ds(pl.multiple_of(core * half, half), half)]
+        else:
+            spot = share_all.at[core]
+        quick.append(send(8 + number, share, spot, mate))
+        kept.append(pltpu.make_async_copy(share, spot, keep_sems.at[1 + number]))
     quick.append(send(8 + amount, own, fields.at[core, 1], mate))
-    keep = pltpu.make_async_copy(own, fields.at[core, 1], keep_sem)
-    keep.start()
+    kept.append(pltpu.make_async_copy(own, fields.at[core, 1], keep_sems.at[0]))
+    for copy in kept:
+        copy.start()
     to_right.wait_recv()
     quick.append(send(6, fields.at[core, 0], fields.at[core, 0], mate))
     to_left.wait_recv()
@@ -169,25 +176,32 @@
         copy.wait_recv()
     for copy in quick + [to_right, to_left]:
         copy.wait_send()
-    keep.wait()
+    for copy in kept:
+        copy.wait()
 
 
 def trade(rows, own, shares, number):
     count = lax.axis_size("space")
     amount = len(shares)
-    shapes = [(2,) + rows.shape, (2, 3) + own.shape] + [(2,) + share.shape for share in shares]
+    shapes = [(2,) + rows.shape, (2, 3) + own.shape]
+    for share in shares:
+        if share.ndim == 3:
+            shapes.append((share.shape[0], 2 * share.shape[1], share.shape[2]))
+        else:
+            shapes.append((2,) + share.shape)
     return pl.pallas_call(
         lambda *refs: trade_kernel(count, amount, *refs),
-        in_specs=[pl.BlockSpec(memory_space=pltpu.VMEM)] * (2 + amount),
+        in_specs=[pl.BlockSpec(memory_space=pltpu.VMEM)] * 2
+        + [pl.BlockSpec(memory_space=pltpu.HBM if share.ndim == 3 else pltpu.VMEM) for share in shares],
         out_specs=[
-            pl.BlockSpec(memory_space=pl.ANY if place == 1 else pltpu.VMEM)
-            for place in range(2 + amount)
+            pl.BlockSpec(memory_space=pltpu.HBM if len(shape) in (3, 5) and place else pltpu.VMEM)
+            for place, shape in enumerate(shapes)
         ],
         out_shape=[jax.ShapeDtypeStruct(shape, rows.dtype) for shape in shapes],
         scratch_shapes=[
             pltpu.SemaphoreType.DMA((9 + amount,)),
             pltpu.SemaphoreType.DMA((9 + amount,)),
-            pltpu.SemaphoreType.DMA,
+            pltpu.SemaphoreType.DMA((1 + amount,)),
         ],
         compiler_params=pltpu.CompilerParams(
             collective_id=number, has_side_effects=True, vmem_limit_bytes=12 * 1024 * 1024
@@ -329,6 +343,8 @@
     @pl.when(brick == 0)
     def fill():
         if count:
+            fetch = pltpu.make_async_copy(refs["far_field"], field_ref, refs["field_sem"])
+            fetch.start()
             greeted = list(nearby(count)[:2]) + (wide.peers() if sums else [])
             hail(greeted)
         slots = table.shape[0] - 1
@@ -348,27 +364,22 @@
             table[slot] = turned.reshape(8, 8, 8, 128)
             return carry
 
+        if count:
+            fetch.wait()
         lax.fori_loop(0, slots, turn, 0)
         if "acc" in refs:
             refs["acc"][...] = jnp.zeros_like(refs["acc"])
-        if count:
-            pl.semaphore_wait(pltpu.get_barrier_semaphore(), len(greeted))
+
+    if count:
+
+        @pl.when(brick == 3)
+        def depart():
+            met = 2 + (len(wide.peers()) if sums else 0)
+            pl.semaphore_wait(pltpu.get_barrier_semaphore(), met)
             for copy in ride_copies(count, refs):
                 copy.start()
-        if sums:
-            wide.start(0)
-
-    if sums:
-
-        @pl.when(brick == last - 2)
-        def second():
-            wide.wait(0)
-            wide.start(1)
-
-        @pl.when(brick == last)
-        def third():
-            wide.wait(1)
-            wide.start(2)
+            if sums:
+                wide.start(0)
 
     for index, (lean_x, lean_y, lean_z) in enumerate(lean_list()):
         slot = refs["near"][brick, index]
@@ -426,12 +437,16 @@
             for cell in cells[len(spans) :]:
                 data[cell] = jnp.zeros(data.shape[2:], jnp.float32)
             slim.start(0)
+            wide.wait(0)
+            wide.start(1)
+            slim.wait(0)
+            slim.start(1)
+            wide.wait(1)
+            wide.start(2)
+            slim.wait(1)
+            slim.start(2)
             wide.wait(2)
             refs["wide_out"][...] = refs["wide_total"][...]
-            slim.wait(0)
-            slim.start(1)
-            slim.wait(1)
-            slim.start(2)
             slim.wait(2)
             refs["slim_out"][...] = refs["slim_total"][...]
             wide.leave()
@@ -462,7 +477,12 @@
 
     ins["near"] = (near, pl.BlockSpec(memory_space=pltpu.SMEM))
     ins["live"] = (live_count, pl.BlockSpec(memory_space=pltpu.SMEM))
-    ins["field"] = (field_in, whole(field_in.shape))
+    if count:
+        ins["far_field"] = (field_in, pl.BlockSpec(memory_space=pltpu.HBM))
+        scratch["field"] = pltpu.VMEM(field_in.shape, field_in.dtype)
+        scratch["field_sem"] = pltpu.SemaphoreType.DMA
+    else:
+        ins["field"] = (field_in, whole(field_in.shape))
     scratch["table"] = pltpu.VMEM((slots + 1, 8, 8, 8, 128), jnp.float32)
     scratch["padded"] = pltpu.VMEM((3, 10, 10, 8, 128), jnp.float32)
     scratch["columns"] = pltpu.VMEM((640, WIDTH), jnp.bfloat16)
@@ -515,10 +535,8 @@
 
 def weight_blocks(weight):
     rows, channels = weight.shape[1:]
-    taps = weight.reshape(3, 9, rows, channels)
-    taps = jnp.stack(
-        [taps[:, tap] for tap in TAP_ORDER] + [jnp.zeros_like(taps[:, 0])], axis=1
-    )
+    taps = weight.reshape(3, 9, rows, channels)[:, TAP_ORDER]
+    taps = jnp.concatenate([taps, jnp.zeros_like(taps[:, :1])], axis=1)
     return jnp.transpose(taps, (0, 2, 1, 3)).reshape(3, rows, WIDTH)
 
 
@@ -580,14 +598,12 @@
     )
     outgoing = select_rows(send_pick, jnp.concatenate([pooled, slot_rows], axis=1))
     grad_rows = (cotangent.astype(jnp.float32) * live_mask).astype(jnp.bfloat16)
-    incoming, grad_fields, both_pooled, both_coarse, both_fine, both_project = trade(
+    incoming, grad_fields, both_pooled, whole_coarse, whole_fine, both_project = trade(
         outgoing.reshape(2, moving * 32, 128),
         grad_rows,
         [pooled.reshape(bricks * 16, 128), coarse_weight, fine_weight, project_weight],
         2,
     )
-    whole_coarse = jnp.concatenate([both_coarse[0], both_coarse[1]], axis=1)
-    whole_fine = jnp.concatenate([both_fine[0], both_fine[1]], axis=1)
     whole_project = jnp.concatenate([both_project[0], both_project[1]], axis=1)
     incoming = incoming.reshape(2, 2 * moving, 4096)
     incoming_slots = incoming[0, :, -1].astype(jnp.int32) - 1

time: 137 us -> 121 us (0.88)
  Pallas kernels: 100 us -> 91.4 us
  local copies, waits for them, and re-layouts: 21.8 us -> 17.5 us
  other arithmetic: 5.7 us -> 3.21 us
    pallas_call x5, Pallas kernels: 65.4 us -> 56.1 us  [brick_pass(): pl.pallas_call(lambda *refs: brick_kernel(count, masked, names, *refs), g...]
    unnamed x73 -> x53, local copies, waits for them, and re-layouts: 12.3 us -> 6.66 us
    gather x0 -> x5, local copies, waits for them, and re-layouts: none -> 3.93 us  [weight_blocks(): taps = weight.reshape(3, 9, rows, channels)[:, TAP_ORDER]]
    another operation x8 -> x6, local copies, waits for them, and re-layouts: 3.95 us -> 1.29 us  [the longest x4 1.01 us: weight_blocks(): taps = weight.reshape(3, 9, rows, channels)[:, TAP_ORDER]]
where the time goes in v5:
time: 121 us; the launch traced here: 120 us
  Pallas kernels  91.4 us (76%)
  local copies, waits for them, and re-layouts  17.5 us (14%)
  matrix products  5.71 us (5%)
  other arithmetic  3.21 us (3%)
  between operations  2.07 us (2%)
    pallas_call x5, Pallas kernels, brick_pass(): pl.pallas_call(lambda *refs: brick_kernel(count, masked, names, *refs), g...  56.1 us
    pallas_call x2, Pallas kernels, trade(): pl.pallas_call(lambda *refs: trade_kernel(count, amount, *refs), in_specs...  32.9 us
    unnamed x53, local copies, waits for them, and re-layouts  6.66 us
    gather x5, local copies, waits for them, and re-layouts, weight_blocks(): taps = weight.reshape(3, 9, rows, channels)[:, TAP_ORDER]  3.93 us
    pallas_call x1, Pallas kernels, finish(): pl.pallas_call(lambda *refs: finish_kernel(scales, *refs), in_specs=[pl.B...  2.43 us

profile of v5, /device:TPU:8, one launch (start us, length us, event | category | flops | bytes accessed | tf_op | source)
XLA Modules:
  0.0 119.9 jit_solution(17923351869898442327)
XLA Ops:
  1.4 0.7 pad.9.clone
  2.1 0.7 compare_select_fusion.1
  3.1 0.7 subtract_select_fusion
  3.8 0.7 pad_clamp_fusion
  4.7 1.3 %fusion.16 = bf16[8,32,64]{2,1,0:T(8,128)(2,1)S(1)} fusion(bf16[512,64,1]{0,1,2:T(8,128)(2,1)} %constant.123, bf16[8,32,512]{2,1,0:T(8,128)(2,1)} %param.22, f32[8]{0:T(128)S(1)} %compare_select_fusion.7), kind=kOutput, calls=%fused_computation.38 | convolution fusion | flops 16809984 | bytes 360480 | tf_op jit(solution)/shard_map/bcv,vu->bcu/dot_general | solution.py:45
  6.4 1.5 %gather_fusion.2 = bf16[9,3,32,64]{3,2,1,0:T(8,128)(2,1)S(1)} fusion(bf16[3,9,32,64]{3,2,1,0:T(8,128)(2,1)} %bitcast.173, s32[1024]{0:T(1024)S(1)} %pad_clamp_fusion), kind=kCustom, calls=%fused_computation.2 | custom fusion | bytes 221220 | tf_op jit(solution)/shard_map/gather | solution.py:538
  8.5 17.9 %shard_map.245 = (bf16[2,2,32,128]{3,2,1,0:T(8,128)(2,1)S(1)}, bf16[2,3,8,32,512]{4,3,2,1,0:T(8,128)(2,1)S(1)}, bf16[2,128,128]{2,1,0:T(8,128)(2,1)S(1)}, bf16[2...) custom-call(bf16[2,32,128]{2,1,0:T(8,128)(2,1)S(1)} %bitcast.179, ...), custom_call_target="tpu_custom_call" | custom-call | tf_op jit(solution)/shard_map/pallas_call | solution.py:192
  26.5 1.2 copy-done.5
  29.1 0.6 gather_fusion
  30.1 0.4 copy.30
  30.5 0.6 gather_fusion.1
  31.2 0.3 copy.32.refs_3_
  31.5 1.5 %shard_map.246 = f32[1,128,512]{2,1,0:T(8,128)S(1)} custom-call(s32[1,27]{1,0:T(1,128)S(1)} %compare_select_fusion.refs_0_, s32[1]{0:T(128)} %copy.62.refs_1_, bf16[1,64,512]{2,1,0:T(8,128)(2,1)S(1)} %fusion.13.refs_2_, bf16[1,3,128,640]{3,2,1,0:T(8,128)(2,1)S(1)} %copy.32.refs_3_), custom_call_target="tpu_custom_call" | custom-call | flops 251658240 | bytes 65536 | tf_op jit(solution)/shard_map/pallas_call | solution.py:520
  33.1 0.5 fusion.14
  33.7 0.3 constant_dynamic-slice_fusion
  34.4 0.6 gather_fusion.3
  35.2 0.6 gather_fusion.4
  36.2 1.4 %copy-done.6 = bf16[2,3,8,32,512]{4,3,2,1,0:T(8,128)(2,1)S(1)} copy-done((bf16[2,3,8,32,512]{4,3,2,1,0:T(8,128)(2,1)S(1)}, bf16[2,3,8,32,512]{4,3,2,1,0:T(8,128)(2,1)}, u32[]{:S(2)}) %copy-start.6) | copy-done | bytes 1572888
  37.6 12.2 %shard_map.247 = (bf16[8,32,512]{2,1,0:T(8,128)(2,1)S(1)}, bf16[2,16,128]{2,1,0:T(8,128)(2,1)S(1)}) custom-call(s32[8,27]{1,0:T(8,128)S(1)} %pad_add_fusion.refs_0_, s32[1]{0:T(128)} %copy.62.refs_1_, bf16[2,3,8,32,512]{4,3,2,1,0:T(8,128)(2,1)S(1)} %copy-done.6, bf16[1,3,32,640]{3,2,1,0:T(8,128)(2,1)S(1)} %stack_reshape.15.refs_3_, ...), custom_call_target="tpu_custom_call" | custom-call | flops 503316480 | bytes 1572864 | tf_op jit(solution)/shard_map/pallas_call | solution.py:520
  51.9 14.9 %shard_map.248 = (bf16[2,2,16,128]{3,2,1,0:T(8,128)(2,1)S(1)}, bf16[2,3,8,32,512]{4,3,2,1,0:T(8,128)(2,1)S(1)}, bf16[2,128,128]{2,1,0:T(8,128)(2,1)S(1)}) custom-call(bf16[2,16,128]{2,1,0:T(8,128)(2,1)S(1)} %bitcast.180, bf16[8,32,512]{2,1,0:T(8,128)(2,1)S(1)} %fusion.6.refs_1_, bf16[128,128]{1,0:T(8,128)(2,1)S(1)} %reshape_reshape.16.refs_2_), custom_call_target="tpu_custom_call" | custom-call | tf_op jit(solution)/shard_map/pallas_call | solution.py:192
  66.8 1.2 copy-done.7
  68.7 0.3 fusion.9
  69.2 2.3 %shard_map.250 = f32[2,32,512]{2,1,0:T(8,128)S(1)} custom-call(s32[2,27]{1,0:T(2,128)S(1)} %iota_select_fusion.refs_0_, s32[1]{0:T(128)} %copy.62.refs_1_, bf16[2,64,512]{2,1,0:T(8,128)(2,1)S(1)} %bitcast.177, bf16[2,3,32,640]{3,2,1,0:T(8,128)(2,1)S(1)} %pad_maximum_fusion.refs_3_), custom_call_target="tpu_custom_call" | custom-call | flops 125829120 | bytes 131072 | tf_op jit(solution)/shard_map/pallas_call | solution.py:520
  71.5 0.3 fusion.15
  72.3 1.2 %shard_map.249 = f32[3,64,640]{2,1,0:T(8,128)S(1)} custom-call(s32[1,27]{1,0:T(1,128)S(1)} %compare_select_fusion.refs_0_, s32[1]{0:T(128)} %copy.62.refs_1_, bf16[1,64,512]{2,1,0:T(8,128)(2,1)S(1)} %fusion.13.refs_2_, bf16[1,64,512]{2,1,0:T(8,128)(2,1)S(1)} %constant_dynamic-slice_fusion.1.refs_3_), custom_call_target="tpu_custom_call" | custom-call | flops 125829120 | bytes 65536 | tf_op jit(solution)/shard_map/pallas_call | solution.py:520
  73.7 1.4 %copy-done.8 = bf16[2,3,8,32,512]{4,3,2,1,0:T(8,128)(2,1)S(1)} copy-done((bf16[2,3,8,32,512]{4,3,2,1,0:T(8,128)(2,1)S(1)}, bf16[2,3,8,32,512]{4,3,2,1,0:T(8,128)(2,1)}, u32[]{:S(2)}) %copy-start.8) | copy-done | bytes 1572888
  75.1 38.9 %shard_map.251 = (bf16[8,32,512]{2,1,0:T(8,128)(2,1)S(1)}, f32[16,8,8,128]{3,2,1,0:T(8,128)S(1)}, f32[16,8,4,128]{3,2,1,0:T(4,128)S(1)}, bf16[2,16,128]{2,1,0:T(8,128)(2,1)S(1)}) custom-call(s32[8,27]{1,0:T(8,128)S(1)} %pad_add_fusion.refs_0_, s32[1]{0:T(128)} %copy.62.refs_1_, bf16[2,3,8,32,512]{4,3,2,1,0:T(8,128)(2,1)S(1)} %copy-done.8, ...), custom_call_target="tpu_custom_call" | custom-call | flops 1006632960 | bytes 1572864 | tf_op jit(solution)/shard_map/pallas_call | solution.py:520
  114.1 0.7 copy-done.3
  115.0 0.7 mul.93
  115.8 0.9 fusion.5
  116.7 2.4 %shard_map.252 = (f32[27,32,64]{2,1,0:T(8,128)}, f32[27,64,64]{2,1,0:T(8,128)}) custom-call(f32[128,4,128]{2,1,0:T(4,128)} %bitcast.178, f32[128,8,128]{2,1,0:T(8,128)} %bitcast.175), custom_call_target="tpu_custom_call" | custom-call | tf_op jit(solution)/shard_map/pallas_call | solution.py:566
  119.2 0.7 copy.63
  (123 shorter events, 8.4 us)
Async XLA Ops:
  0.6 7.7 %copy-start.12 = (bf16[8,32,512]{2,1,0:T(8,128)(2,1)S(1)}, bf16[8,32,512]{2,1,0:T(8,128)(2,1)}, u32[]{:S(2)}) copy-start(bf16[8,32,512]{2,1,0:T(8,128)(2,1)} %param.29) | copy-start | bytes 786436
  1.3 7.0 %copy-start.15 = (f32[8]{0:T(128)}, f32[8]{0:T(128)S(1)}, u32[]{:S(2)}) copy-start(f32[8]{0:T(128)S(1)} %compare_convert_fusion.2) | copy-start | bytes 100
  3.1 3.2 %copy-start.20 = (s32[8]{0:T(128)}, s32[8]{0:T(128)S(1)}, u32[]{:S(2)}) copy-start(s32[8]{0:T(128)S(1)} %get-tuple-element.50) | copy-start | bytes 100
  4.7 3.8 %copy-start = (bf16[27,32,64]{2,1,0:T(8,128)(2,1)S(1)}, bf16[27,32,64]{2,1,0:T(8,128)(2,1)}, u32[]{:S(2)}) copy-start(bf16[27,32,64]{2,1,0:T(8,128)(2,1)} %refs_4_.1) | copy-start | bytes 331780
  4.7 3.8 %copy-start.2 = (bf16[27,64,64]{2,1,0:T(8,128)(2,1)S(1)}, bf16[27,64,64]{2,1,0:T(8,128)(2,1)}, u32[]{:S(2)}) copy-start(bf16[27,64,64]{2,1,0:T(8,128)(2,1)} %refs_3_.1) | copy-start | bytes 663556
  4.7 3.8 %copy-start.4 = (bf16[64,64]{1,0:T(8,128)(2,1)S(1)}, bf16[64,64]{1,0:T(8,128)(2,1)}, u32[]{:S(2)}) copy-start(bf16[64,64]{1,0:T(8,128)(2,1)} %refs_5_.1) | copy-start | bytes 24580
  8.1 20.3 %copy-start.9 = (bf16[8,64,512]{2,1,0:T(8,128)(2,1)S(1)}, bf16[8,64,512]{2,1,0:T(8,128)(2,1)}, u32[]{:S(2)}) copy-start(bf16[8,64,512]{2,1,0:T(8,128)(2,1)} %constant.117) | copy-start | bytes 1572868
  26.5 1.2 copy-start.5
  27.9 0.9 copy-start.17
  27.9 5.1 %copy-start.13 = (bf16[64,64]{1,0:T(8,128)(2,1)}, bf16[64,64]{1,0:T(8,128)(2,1)S(1)}, u32[]{:S(2)}) copy-start(bf16[64,64]{1,0:T(8,128)(2,1)S(1)} %get-tuple-element.45) | copy-start | bytes 24580
  34.2 1.8 %copy-start.18 = (s32[10]{0:T(128)S(1)}, s32[10]{0:T(128)}, u32[]{:S(2)}) copy-start(s32[10]{0:T(128)} %copy-done.17) | copy-start | bytes 124
  35.8 14.0 %copy-start.21 = (s32[8]{0:T(128)S(1)}, s32[8]{0:T(128)}, u32[]{:S(2)}) copy-start(s32[8]{0:T(128)} %copy-done.20) | copy-start | bytes 100
  35.8 14.3 %copy-start.11 = (bf16[512,64,1]{0,1,2:T(8,128)(2,1)S(1)}, bf16[512,64,1]{0,1,2:T(8,128)(2,1)}, u32[]{:S(2)}) copy-start(bf16[512,64,1]{0,1,2:T(8,128)(2,1)} %constant.123) | copy-start | bytes 196612
  36.2 1.4 %copy-start.6 = (bf16[2,3,8,32,512]{4,3,2,1,0:T(8,128)(2,1)S(1)}, bf16[2,3,8,32,512]{4,3,2,1,0:T(8,128)(2,1)}, u32[]{:S(2)}) copy-start(bf16[2,3,8,32,512]{4,3,2,1,0:T(8,128)(2,1)} %copy-done.5) | copy-start | bytes 4718596
  50.4 1.2 %copy-start.10 = (bf16[8,32,512]{2,1,0:T(8,128)(2,1)S(1)}, bf16[8,32,512]{2,1,0:T(8,128)(2,1)}, u32[]{:S(2)}) copy-start(bf16[8,32,512]{2,1,0:T(8,128)(2,1)} %param.22) | copy-start | bytes 786436
  50.4 1.2 %copy-start.16 = (f32[8]{0:T(128)S(1)}, f32[8]{0:T(128)}, u32[]{:S(2)}) copy-start(f32[8]{0:T(128)} %copy-done.15) | copy-start | bytes 100
  50.9 17.1 %copy-start.19 = (s32[10]{0:T(128)S(1)}, s32[10]{0:T(128)}, u32[]{:S(2)}) copy-start(s32[10]{0:T(128)} %copy-done.17) | copy-start | bytes 124
  51.3 17.3 %copy-start.14 = (bf16[64,64]{1,0:T(8,128)(2,1)S(1)}, bf16[64,64]{1,0:T(8,128)(2,1)}, u32[]{:S(2)}) copy-start(bf16[64,64]{1,0:T(8,128)(2,1)} %copy-done.13) | copy-start | bytes 24580
  66.8 1.2 copy-start.7
  69.0 4.6 %copy-start.22 = (f32[128]{0:T(128)S(1)}, f32[128]{0:T(128)}, u32[]{:S(2)}) copy-start(f32[128]{0:T(128)} %pad.9.clone) | copy-start | bytes 1540
  73.7 1.4 %copy-start.8 = (bf16[2,3,8,32,512]{4,3,2,1,0:T(8,128)(2,1)S(1)}, bf16[2,3,8,32,512]{4,3,2,1,0:T(8,128)(2,1)}, u32[]{:S(2)}) copy-start(bf16[2,3,8,32,512]{4,3,2,1,0:T(8,128)(2,1)} %copy-done.7) | copy-start | bytes 4718596
  114.1 0.7 copy-start.3
  114.8 1.9 %copy-start.1 = (f32[16,8,8,128]{3,2,1,0:T(8,128)}, f32[16,8,8,128]{3,2,1,0:T(8,128)S(1)}, u32[]{:S(2)}) copy-start(f32[16,8,8,128]{3,2,1,0:T(8,128)S(1)} %get-tuple-element.36) | copy-start | bytes 1572868

commit v6 on v5

--- a/solution.py
+++ b/solution.py
@@ -328,7 +328,7 @@
     return pieces
 
 
-def brick_kernel(count, masked, names, *refs):
+def brick_kernel(count, masked, scales, names, *refs):
     refs = dict(zip(names, refs))
     field_ref, table, padded, columns = [
         refs[name] for name in ("field", "table", "padded", "columns")
@@ -372,7 +372,7 @@
 
     if count:
 
-        @pl.when(brick == 3)
+        @pl.when(brick == 2)
         def depart():
             met = 2 + (len(wide.peers()) if sums else 0)
             pl.semaphore_wait(pltpu.get_barrier_semaphore(), met)
@@ -380,6 +380,13 @@
                 copy.start()
             if sums:
                 wide.start(0)
+
+    if sums:
+
+        @pl.when(brick == last - 1)
+        def second():
+            wide.wait(0)
+            wide.start(1)
 
     for index, (lean_x, lean_y, lean_z) in enumerate(lean_list()):
         slot = refs["near"][brick, index]
@@ -437,18 +444,21 @@
             for cell in cells[len(spans) :]:
                 data[cell] = jnp.zeros(data.shape[2:], jnp.float32)
             slim.start(0)
-            wide.wait(0)
-            wide.start(1)
+            wide.wait(1)
+            wide.start(2)
             slim.wait(0)
             slim.start(1)
-            wide.wait(1)
-            wide.start(2)
+            wide.wait(2)
+            unpack(refs["wide_total"], refs["coarse_out"], scales[1])
+            used = 3 * refs["coarse_out"].shape[1] // 8 * (WIDTH // 128)
+            plain = refs["wide_total"]
+            for tile in range(refs["project_out"].shape[0]):
+                at = divmod(used + tile, plain.shape[1])
+                refs["project_out"][tile] = plain[at] * scales[1]
             slim.wait(1)
             slim.start(2)
-            wide.wait(2)
-            refs["wide_out"][...] = refs["wide_total"][...]
             slim.wait(2)
-            refs["slim_out"][...] = refs["slim_total"][...]
+            unpack(refs["slim_total"], refs["fine_out"], scales[0])
             wide.leave()
             slim.leave()
         elif "acc" in refs:
@@ -461,7 +471,7 @@
 
 def brick_pass(
     field_in, near, live_count, weight, grad_rows, out_dtype, masked, ride=None, number=None,
-    wide=None,
+    wide=None, scales=None,
 ):
     amount = near.shape[0]
     count = 0 if ride is None else lax.axis_size("space")
@@ -505,8 +515,9 @@
         scratch.update(wide_scratch)
         scratch.update(slim_scratch)
         ins["wide_data"] = (wide.reshape(wide_shape), whole(wide_shape))
-        result("wide_out", wide_shape, jnp.float32)
-        result("slim_out", slim_shape, jnp.float32)
+        result("fine_out", (27, rows, 64), jnp.float32)
+        result("coarse_out", (27, 64, 64), jnp.float32)
+        result("project_out", (4, 8, 128), jnp.float32)
     if count:
         ins["ride"] = (ride, whole(ride.shape))
         result("ride_out", ride.shape, ride.dtype)
@@ -518,7 +529,7 @@
     room = 12 if slots < 8 else 20 if wide is None else 30
     products = (weight is not None) + (grad_rows is not None)
     return pl.pallas_call(
-        lambda *refs: brick_kernel(count, masked, names, *refs),
+        lambda *refs: brick_kernel(count, masked, scales, names, *refs),
         grid=(amount,),
         in_specs=[spec for _, spec in ins.values()],
         out_specs=[spec for _, spec in outs.values()],
@@ -540,17 +551,17 @@
     return jnp.transpose(taps, (0, 2, 1, 3)).reshape(3, rows, WIDTH)
 
 
-def finish_kernel(scales, slim, wide, fine_out, coarse_out):
-    for pieces, out, scale in zip((slim, wide), (fine_out, coarse_out), scales):
-        high = pieces.shape[1]
-        blocks = out.shape[1] // high
-        for tap_x in range(3):
-            for block in range(blocks):
-                first = WIDTH // 128 * (tap_x * blocks + block)
-                rows = slice(high * block, high * block + high)
-                for place, tap in enumerate(TAP_ORDER):
-                    lanes = slice(64 * (place % 2), 64 * (place % 2) + 64)
-                    out[9 * tap_x + int(tap), rows, :] = pieces[first + place // 2, :, lanes] * scale
+def unpack(total, out, scale):
+    high = total.shape[2]
+    blocks = out.shape[1] // high
+    for tap_x in range(3):
+        for block in range(blocks):
+            first = WIDTH // 128 * (tap_x * blocks + block)
+            rows = slice(high * block, high * block + high)
+            for place, tap in enumerate(TAP_ORDER):
+                lanes = slice(64 * (place % 2), 64 * (place % 2) + 64)
+                plane, piece = divmod(first + place // 2, total.shape[1])
+                out[9 * tap_x + int(tap), rows, :] = total[plane, piece, :, lanes] * scale
 
 
 def wide_pieces(coarse, project):
@@ -559,20 +570,6 @@
     small = project.reshape(-1, 8, 128)
     spare = 128 - tiles.shape[0] - small.shape[0]
     return jnp.concatenate([tiles, small, jnp.zeros((spare, 8, 128), jnp.float32)], axis=0)
-
-
-def finish(slim, wide, fine_rows, coarse_rows, scales):
-    slim, wide = slim.reshape(128, 4, 128), wide.reshape(128, 8, 128)
-    fine_sum, coarse_sum = pl.pallas_call(
-        lambda *refs: finish_kernel(scales, *refs),
-        in_specs=[pl.BlockSpec(memory_space=pltpu.VMEM)] * 2,
-        out_specs=[pl.BlockSpec(memory_space=pltpu.VMEM)] * 2,
-        out_shape=[
-            jax.ShapeDtypeStruct((27, rows, 64), jnp.float32) for rows in (fine_rows, coarse_rows)
-        ],
-    )(slim, wide)
-    used = 3 * coarse_rows // 8 * (WIDTH // 128)
-    return fine_sum, coarse_sum, wide[used : used + 4].reshape(64, 64)
 
 
 def per_device(
@@ -693,7 +690,9 @@
         coarse_terms.reshape(coarse_bricks, 2, half_channels, 512).sum(1).astype(jnp.bfloat16)
     )
     down_source = select_rows(receive_pick.T, split_octants(coarse_back).reshape(bricks, -1))
-    out_feats, wide_sum, slim_sum, rode_down = brick_pass(
+    fine_scale = 1.0 / math.sqrt(512.0 * bricks * devices)
+    coarse_scale = 1.0 / math.sqrt(512.0 * coarse_bricks * devices)
+    out_feats, fine_weight_grad, coarse_weight_grad, project_tiles, rode_down = brick_pass(
         feat_fields,
         near,
         live_count,
@@ -704,6 +703,7 @@
         down_source[bricks:].reshape(2, moving * 16, 128),
         5,
         wide_pieces(coarse_total, project_matrix),
+        (fine_scale, coarse_scale),
     )
     down_grad = gather_back(
         down_source[:bricks], send_pick, rode_down.reshape(2 * moving, -1)
@@ -711,12 +711,7 @@
     grad_feats = (back_feats.astype(jnp.float32) + live_mask * enlarge(down_grad) * 0.125).astype(
         jnp.bfloat16
     )
-    fine_scale = 1.0 / math.sqrt(512.0 * bricks * devices)
-    coarse_scale = 1.0 / math.sqrt(512.0 * coarse_bricks * devices)
-    fine_weight_grad, coarse_weight_grad, project_total = finish(
-        slim_sum, wide_sum, half_channels, hidden_half, (fine_scale, coarse_scale)
-    )
-    project_weight_grad = project_total * coarse_scale
+    project_weight_grad = project_tiles.reshape(project_matrix.shape)
     return (out_feats, grad_feats, fine_weight_grad, coarse_weight_grad, project_weight_grad)
 
 

time: 121 us -> 121 us (level)
    unnamed x53 -> x51, local copies, waits for them, and re-layouts: 6.66 us -> 7.66 us
    pallas_call x6 -> x5, Pallas kernels: 58.5 us -> 58 us  [brick_pass(): pl.pallas_call(lambda *refs: brick_kernel(count, masked, scales, names, *...]
where the time goes in v6:
time: 121 us; the launch traced here: 120 us
  Pallas kernels  90.8 us (75%)
  local copies, waits for them, and re-layouts  18.5 us (15%)
  matrix products  5.71 us (5%)
  other arithmetic  3.2 us (3%)
  between operations  2.06 us (2%)
    pallas_call x5, Pallas kernels, brick_pass(): pl.pallas_call(lambda *refs: brick_kernel(count, masked, scales, names, *...  58 us
    pallas_call x2, Pallas kernels, trade(): pl.pallas_call(lambda *refs: trade_kernel(count, amount, *refs), in_specs...  32.9 us
    unnamed x51, local copies, waits for them, and re-layouts  7.66 us
    gather x5, local copies, waits for them, and re-layouts, weight_blocks(): taps = weight.reshape(3, 9, rows, channels)[:, TAP_ORDER]  3.93 us

profile of v6, /device:TPU:8, one launch (start us, length us, event | category | flops | bytes accessed | tf_op | source)
XLA Modules:
  0.0 120.3 jit_solution(1602563880375203332)
XLA Ops:
  1.4 0.7 pad.9.clone
  2.1 0.7 compare_select_fusion.1
  3.1 0.7 subtract_select_fusion
  3.8 0.7 pad_clamp_fusion
  4.7 1.3 %fusion.16 = bf16[8,32,64]{2,1,0:T(8,128)(2,1)S(1)} fusion(bf16[512,64,1]{0,1,2:T(8,128)(2,1)} %constant.121, bf16[8,32,512]{2,1,0:T(8,128)(2,1)} %param.22, f32[8]{0:T(128)S(1)} %compare_select_fusion.7), kind=kOutput, calls=%fused_computation.38 | convolution fusion | flops 16809984 | bytes 360480 | tf_op jit(solution)/shard_map/bcv,vu->bcu/dot_general | solution.py:45
  6.4 1.5 %gather_fusion.2 = bf16[9,3,32,64]{3,2,1,0:T(8,128)(2,1)S(1)} fusion(bf16[3,9,32,64]{3,2,1,0:T(8,128)(2,1)} %bitcast.171, s32[1024]{0:T(1024)S(1)} %pad_clamp_fusion), kind=kCustom, calls=%fused_computation.2 | custom fusion | bytes 221220 | tf_op jit(solution)/shard_map/gather | solution.py:549
  8.5 17.9 %shard_map.245 = (bf16[2,2,32,128]{3,2,1,0:T(8,128)(2,1)S(1)}, bf16[2,3,8,32,512]{4,3,2,1,0:T(8,128)(2,1)S(1)}, bf16[2,128,128]{2,1,0:T(8,128)(2,1)S(1)}, bf16[2...) custom-call(bf16[2,32,128]{2,1,0:T(8,128)(2,1)S(1)} %bitcast.174, ...), custom_call_target="tpu_custom_call" | custom-call | tf_op jit(solution)/shard_map/pallas_call | solution.py:192
  26.5 1.2 copy-done.3
  29.1 0.6 gather_fusion
  30.1 0.4 copy.30
  30.5 0.6 gather_fusion.1
  31.2 0.3 copy.32.refs_3_
  31.5 1.5 %shard_map.246 = f32[1,128,512]{2,1,0:T(8,128)S(1)} custom-call(s32[1,27]{1,0:T(1,128)S(1)} %compare_select_fusion.refs_0_, s32[1]{0:T(128)} %copy.64.refs_1_, bf16[1,64,512]{2,1,0:T(8,128)(2,1)S(1)} %fusion.13.refs_2_, bf16[1,3,128,640]{3,2,1,0:T(8,128)(2,1)S(1)} %copy.32.refs_3_), custom_call_target="tpu_custom_call" | custom-call | flops 251658240 | bytes 65536 | tf_op jit(solution)/shard_map/pallas_call | solution.py:531
  33.1 0.5 fusion.14
  33.7 0.3 constant_dynamic-slice_fusion
  34.4 0.6 gather_fusion.3
  35.3 0.6 gather_fusion.4
  36.2 1.4 %copy-done.4 = bf16[2,3,8,32,512]{4,3,2,1,0:T(8,128)(2,1)S(1)} copy-done((bf16[2,3,8,32,512]{4,3,2,1,0:T(8,128)(2,1)S(1)}, bf16[2,3,8,32,512]{4,3,2,1,0:T(8,128)(2,1)}, u32[]{:S(2)}) %copy-start.4) | copy-done | bytes 1572888
  37.6 11.4 %shard_map.247 = (bf16[8,32,512]{2,1,0:T(8,128)(2,1)S(1)}, bf16[2,16,128]{2,1,0:T(8,128)(2,1)S(1)}) custom-call(s32[8,27]{1,0:T(8,128)S(1)} %pad_add_fusion.refs_0_, s32[1]{0:T(128)} %copy.64.refs_1_, bf16[2,3,8,32,512]{4,3,2,1,0:T(8,128)(2,1)S(1)} %copy-done.4, bf16[1,3,32,640]{3,2,1,0:T(8,128)(2,1)S(1)} %stack_reshape.15.refs_3_, ...), custom_call_target="tpu_custom_call" | custom-call | flops 503316480 | bytes 1572864 | tf_op jit(solution)/shard_map/pallas_call | solution.py:531
  51.1 14.9 %shard_map.248 = (bf16[2,2,16,128]{3,2,1,0:T(8,128)(2,1)S(1)}, bf16[2,3,8,32,512]{4,3,2,1,0:T(8,128)(2,1)S(1)}, bf16[2,128,128]{2,1,0:T(8,128)(2,1)S(1)}) custom-call(bf16[2,16,128]{2,1,0:T(8,128)(2,1)S(1)} %bitcast.175, bf16[8,32,512]{2,1,0:T(8,128)(2,1)S(1)} %fusion.6.refs_1_, bf16[128,128]{1,0:T(8,128)(2,1)S(1)} %reshape_reshape.16.refs_2_), custom_call_target="tpu_custom_call" | custom-call | tf_op jit(solution)/shard_map/pallas_call | solution.py:192
  66.1 1.2 copy-done.5
  67.9 0.3 fusion.9
  68.5 2.3 %shard_map.250 = f32[2,32,512]{2,1,0:T(8,128)S(1)} custom-call(s32[2,27]{1,0:T(2,128)S(1)} %iota_select_fusion.refs_0_, s32[1]{0:T(128)} %copy.64.refs_1_, bf16[2,64,512]{2,1,0:T(8,128)(2,1)S(1)} %bitcast.173, bf16[2,3,32,640]{3,2,1,0:T(8,128)(2,1)S(1)} %pad_maximum_fusion.refs_3_), custom_call_target="tpu_custom_call" | custom-call | flops 125829120 | bytes 131072 | tf_op jit(solution)/shard_map/pallas_call | solution.py:531
  70.8 0.3 fusion.15
  71.6 1.2 %shard_map.249 = f32[3,64,640]{2,1,0:T(8,128)S(1)} custom-call(s32[1,27]{1,0:T(1,128)S(1)} %compare_select_fusion.refs_0_, s32[1]{0:T(128)} %copy.64.refs_1_, bf16[1,64,512]{2,1,0:T(8,128)(2,1)S(1)} %fusion.13.refs_2_, bf16[1,64,512]{2,1,0:T(8,128)(2,1)S(1)} %constant_dynamic-slice_fusion.1.refs_3_), custom_call_target="tpu_custom_call" | custom-call | flops 125829120 | bytes 65536 | tf_op jit(solution)/shard_map/pallas_call | solution.py:531
  73.0 1.4 %copy-done.6 = bf16[2,3,8,32,512]{4,3,2,1,0:T(8,128)(2,1)S(1)} copy-done((bf16[2,3,8,32,512]{4,3,2,1,0:T(8,128)(2,1)S(1)}, bf16[2,3,8,32,512]{4,3,2,1,0:T(8,128)(2,1)}, u32[]{:S(2)}) %copy-start.6) | copy-done | bytes 1572888
  74.4 41.5 %shard_map.251 = (bf16[8,32,512]{2,1,0:T(8,128)(2,1)S(1)}, f32[27,32,64]{2,1,0:T(8,128)S(1)}, f32[27,64,64]{2,1,0:T(8,128)S(1)}, f32[4,8,128]{2,1,0:T(8,128)S(1)}, bf16[2,16,128]{2,1,0:T(8,128)(2,1)S(1)}) custom-call(s32[8,27]{1,0:T(8,128)S(1)} %pad_add_fusion.refs_0_, s32[1]{0:T(128)} %copy.64.refs_1_, bf16[2,3,8,32,512]{4,3,2,1,0:T(8,128)(2,1)S(1)} %copy-done.6, ...), custom_call_target="tpu_custom_call" | custom-call | flops 1006632960 | bytes 1572864 | tf_op jit(solution)/shard_map/pallas_call | solution.py:531
  116.3 0.9 fusion.5
  117.2 0.7 reshape.223
  117.9 0.7 copy.65
  118.6 0.8 copy.66
  119.3 0.9 copy.67
  (119 shorter events, 8.3 us)
Async XLA Ops:
  0.6 7.7 %copy-start.10 = (bf16[8,32,512]{2,1,0:T(8,128)(2,1)S(1)}, bf16[8,32,512]{2,1,0:T(8,128)(2,1)}, u32[]{:S(2)}) copy-start(bf16[8,32,512]{2,1,0:T(8,128)(2,1)} %param.29) | copy-start | bytes 786436
  1.3 7.0 %copy-start.13 = (f32[8]{0:T(128)}, f32[8]{0:T(128)S(1)}, u32[]{:S(2)}) copy-start(f32[8]{0:T(128)S(1)} %compare_convert_fusion.2) | copy-start | bytes 100
  3.1 3.2 %copy-start.18 = (s32[8]{0:T(128)}, s32[8]{0:T(128)S(1)}, u32[]{:S(2)}) copy-start(s32[8]{0:T(128)S(1)} %get-tuple-element.48) | copy-start | bytes 100
  4.7 3.8 %copy-start = (bf16[27,32,64]{2,1,0:T(8,128)(2,1)S(1)}, bf16[27,32,64]{2,1,0:T(8,128)(2,1)}, u32[]{:S(2)}) copy-start(bf16[27,32,64]{2,1,0:T(8,128)(2,1)} %refs_4_.1) | copy-start | bytes 331780
  4.7 3.8 %copy-start.1 = (bf16[27,64,64]{2,1,0:T(8,128)(2,1)S(1)}, bf16[27,64,64]{2,1,0:T(8,128)(2,1)}, u32[]{:S(2)}) copy-start(bf16[27,64,64]{2,1,0:T(8,128)(2,1)} %refs_3_.1) | copy-start | bytes 663556
  4.7 3.8 %copy-start.2 = (bf16[64,64]{1,0:T(8,128)(2,1)S(1)}, bf16[64,64]{1,0:T(8,128)(2,1)}, u32[]{:S(2)}) copy-start(bf16[64,64]{1,0:T(8,128)(2,1)} %refs_5_.1) | copy-start | bytes 24580
  8.1 20.3 %copy-start.7 = (bf16[8,64,512]{2,1,0:T(8,128)(2,1)S(1)}, bf16[8,64,512]{2,1,0:T(8,128)(2,1)}, u32[]{:S(2)}) copy-start(bf16[8,64,512]{2,1,0:T(8,128)(2,1)} %constant.115) | copy-start | bytes 1572868
  26.5 1.2 copy-start.3
  27.9 0.9 copy-start.15
  27.9 5.1 %copy-start.11 = (bf16[64,64]{1,0:T(8,128)(2,1)}, bf16[64,64]{1,0:T(8,128)(2,1)S(1)}, u32[]{:S(2)}) copy-start(bf16[64,64]{1,0:T(8,128)(2,1)S(1)} %get-tuple-element.43) | copy-start | bytes 24580
  34.2 1.8 %copy-start.16 = (s32[10]{0:T(128)S(1)}, s32[10]{0:T(128)}, u32[]{:S(2)}) copy-start(s32[10]{0:T(128)} %copy-done.15) | copy-start | bytes 124
  35.8 13.2 %copy-start.19 = (s32[8]{0:T(128)S(1)}, s32[8]{0:T(128)}, u32[]{:S(2)}) copy-start(s32[8]{0:T(128)} %copy-done.18) | copy-start | bytes 100
  35.9 13.5 %copy-start.9 = (bf16[512,64,1]{0,1,2:T(8,128)(2,1)S(1)}, bf16[512,64,1]{0,1,2:T(8,128)(2,1)}, u32[]{:S(2)}) copy-start(bf16[512,64,1]{0,1,2:T(8,128)(2,1)} %constant.121) | copy-start | bytes 196612
  36.2 1.4 %copy-start.4 = (bf16[2,3,8,32,512]{4,3,2,1,0:T(8,128)(2,1)S(1)}, bf16[2,3,8,32,512]{4,3,2,1,0:T(8,128)(2,1)}, u32[]{:S(2)}) copy-start(bf16[2,3,8,32,512]{4,3,2,1,0:T(8,128)(2,1)} %copy-done.3) | copy-start | bytes 4718596
  49.6 1.2 %copy-start.8 = (bf16[8,32,512]{2,1,0:T(8,128)(2,1)S(1)}, bf16[8,32,512]{2,1,0:T(8,128)(2,1)}, u32[]{:S(2)}) copy-start(bf16[8,32,512]{2,1,0:T(8,128)(2,1)} %param.22) | copy-start | bytes 786436
  49.6 1.2 %copy-start.14 = (f32[8]{0:T(128)S(1)}, f32[8]{0:T(128)}, u32[]{:S(2)}) copy-start(f32[8]{0:T(128)} %copy-done.13) | copy-start | bytes 100
  50.1 17.1 %copy-start.17 = (s32[10]{0:T(128)S(1)}, s32[10]{0:T(128)}, u32[]{:S(2)}) copy-start(s32[10]{0:T(128)} %copy-done.15) | copy-start | bytes 124
  50.6 17.4 %copy-start.12 = (bf16[64,64]{1,0:T(8,128)(2,1)S(1)}, bf16[64,64]{1,0:T(8,128)(2,1)}, u32[]{:S(2)}) copy-start(bf16[64,64]{1,0:T(8,128)(2,1)} %copy-done.11) | copy-start | bytes 24580
  66.0 1.2 copy-start.5
  68.2 4.6 %copy-start.20 = (f32[128]{0:T(128)S(1)}, f32[128]{0:T(128)}, u32[]{:S(2)}) copy-start(f32[128]{0:T(128)} %pad.9.clone) | copy-start | bytes 1540
  73.0 1.4 %copy-start.6 = (bf16[2,3,8,32,512]{4,3,2,1,0:T(8,128)(2,1)S(1)}, bf16[2,3,8,32,512]{4,3,2,1,0:T(8,128)(2,1)}, u32[]{:S(2)}) copy-start(bf16[2,3,8,32,512]{4,3,2,1,0:T(8,128)(2,1)} %copy-done.5) | copy-start | bytes 4718596

commit v7 on v6

--- a/solution.py
+++ b/solution.py
@@ -328,7 +328,7 @@
     return pieces
 
 
-def brick_kernel(count, masked, scales, names, *refs):
+def brick_kernel(count, masked, scales, parts, names, *refs):
     refs = dict(zip(names, refs))
     field_ref, table, padded, columns = [
         refs[name] for name in ("field", "table", "padded", "columns")
@@ -413,10 +413,22 @@
             put(1, ahead[0], ahead[1])
     put(4, ahead[2], 0.0)
     if "weight" in refs:
+        weight, blocks = refs["weight"], refs["blocks"]
+
+        @pl.when(jnp.logical_or(brick == 0, parts > 1))
+        def order_taps():
+            zeros = jnp.zeros(weight.shape[2:], weight.dtype)
+            for tap_x in range(3):
+                taps = [weight[0, 9 * tap_x + int(tap)] for tap in TAP_ORDER] + [zeros]
+                for pair in range(WIDTH // 128):
+                    blocks[tap_x, :, 128 * pair : 128 * pair + 128] = jnp.concatenate(
+                        taps[2 * pair : 2 * pair + 2], axis=1
+                    )
+
         total = None
         for tap_x in range(3):
             part = lax.dot_general(
-                refs["weight"][0, tap_x],
+                blocks[tap_x],
                 columns[64 * tap_x : 64 * tap_x + 512, :],
                 (((1,), (1,)), ((), ())),
                 preferred_element_type=jnp.float32,
@@ -478,6 +490,7 @@
     slots = 3 * field_in.shape[2] if field_in.ndim == 5 else field_in.shape[0]
     rows = weight.shape[2] if weight is not None else grad_rows.shape[1]
     ins, outs, scratch = {}, {}, {}
+    parts = 1
 
     def whole(shape):
         return pl.BlockSpec(shape, lambda b: (0,) * len(shape))
@@ -499,10 +512,10 @@
     by_brick = pl.BlockSpec((1, rows, 512), lambda b: (b, 0, 0))
     if weight is not None:
         parts = weight.shape[0]
-        blocks = jnp.stack([weight_blocks(part) for part in weight])
         ins["weight"] = (
-            blocks, pl.BlockSpec((1, 3, rows, WIDTH), lambda b: (b % parts, 0, 0, 0))
+            weight, pl.BlockSpec((1, 27, rows, 64), lambda b: (b % parts, 0, 0, 0))
         )
+        scratch["blocks"] = pltpu.VMEM((3, rows, WIDTH), weight.dtype)
         result("out", (amount, rows, 512), out_dtype, by_brick)
     if grad_rows is not None:
         ins["grad"] = (grad_rows, by_brick)
@@ -529,7 +542,7 @@
     room = 12 if slots < 8 else 20 if wide is None else 30
     products = (weight is not None) + (grad_rows is not None)
     return pl.pallas_call(
-        lambda *refs: brick_kernel(count, masked, scales, names, *refs),
+        lambda *refs: brick_kernel(count, masked, scales, parts, names, *refs),
         grid=(amount,),
         in_specs=[spec for _, spec in ins.values()],
         out_specs=[spec for _, spec in outs.values()],
@@ -542,13 +555,6 @@
             transcendentals=0,
         ),
     )(*[value for value, _ in ins.values()])
-
-
-def weight_blocks(weight):
-    rows, channels = weight.shape[1:]
-    taps = weight.reshape(3, 9, rows, channels)[:, TAP_ORDER]
-    taps = jnp.concatenate([taps, jnp.zeros_like(taps[:, :1])], axis=1)
-    return jnp.transpose(taps, (0, 2, 1, 3)).reshape(3, rows, WIDTH)
 
 
 def unpack(total, out, scale):

time: 121 us -> 116 us (0.959)
  local copies, waits for them, and re-layouts: 18.5 us -> 13.1 us
    gather x5 -> x0, local copies, waits for them, and re-layouts: 3.93 us -> none  [weight_blocks(): taps = weight.reshape(3, 9, rows, channels)[:, TAP_ORDER]]
    another operation x11 -> x3, local copies, waits for them, and re-layouts: 2.64 us -> 0.41 us  [the longest x5 1.35 us: brick_pass(): blocks = jnp.stack([weight_blocks(part) for part in weight])]
    unnamed x51 -> x43, local copies, waits for them, and re-layouts: 7.66 us -> 9.28 us
where the time goes in v7:
time: 116 us; the launch traced here: 115 us
  Pallas kernels  91.1 us (79%)
  local copies, waits for them, and re-layouts  13.1 us (11%)
  matrix products  5.65 us (5%)
  other arithmetic  3.57 us (3%)
  between operations  1.87 us (2%)
    pallas_call x5, Pallas kernels, brick_pass(): pl.pallas_call(lambda *refs: brick_kernel(count, masked, scales, parts, n...  58.4 us
    pallas_call x2, Pallas kernels, trade(): pl.pallas_call(lambda *refs: trade_kernel(count, amount, *refs), in_specs...  32.7 us
    unnamed x43, local copies, waits for them, and re-layouts  9.28 us

profile of v7, /device:TPU:8, one launch (start us, length us, event | category | flops | bytes accessed | tf_op | source)
XLA Modules:
  0.0 115.3 jit_solution(2018994237977881292)
XLA Ops:
  1.4 0.6 pad.4.clone
  2.0 0.7 compare_select_fusion.1
  3.1 0.7 subtract_select_fusion
  4.0 1.2 %fusion.16 = bf16[8,32,64]{2,1,0:T(8,128)(2,1)S(1)} fusion(bf16[512,64,1]{0,1,2:T(8,128)(2,1)} %constant.94, bf16[8,32,512]{2,1,0:T(8,128)(2,1)} %param.16, f32[8]{0:T(128)S(1)} %compare_select_fusion.7), kind=kOutput, calls=%fused_computation.33 | convolution fusion | flops 16809984 | bytes 360480 | tf_op jit(solution)/shard_map/bcv,vu->bcu/dot_general | solution.py:45
  5.6 1.1 multiply_convert_fusion.refs_1_.refs_4_
  6.7 0.9 copy-done.1
  7.6 0.7 copy-done.3
  8.3 17.7 %shard_map.191 = (bf16[2,2,32,128]{3,2,1,0:T(8,128)(2,1)S(1)}, bf16[2,3,8,32,512]{4,3,2,1,0:T(8,128)(2,1)S(1)}, bf16[2,128,128]{2,1,0:T(8,128)(2,1)S(1)}, bf16[2...) custom-call(bf16[2,32,128]{2,1,0:T(8,128)(2,1)S(1)} %bitcast.161, ...), custom_call_target="tpu_custom_call" | custom-call | tf_op jit(solution)/shard_map/pallas_call | solution.py:192
  26.1 1.2 %copy-done.6 = bf16[2,3,8,32,512]{4,3,2,1,0:T(8,128)(2,1)} copy-done((bf16[2,3,8,32,512]{4,3,2,1,0:T(8,128)(2,1)}, bf16[2,3,8,32,512]{4,3,2,1,0:T(8,128)(2,1)S(1)}, u32[]{:S(2)}) %copy-start.6) | copy-done | bytes 1572888
  27.9 0.2 fusion.13.refs_2_
  28.2 1.5 %shard_map.192 = f32[1,128,512]{2,1,0:T(8,128)S(1)} custom-call(s32[1,27]{1,0:T(1,128)S(1)} %compare_select_fusion.refs_0_, s32[1]{0:T(128)} %copy.52.refs_1_, bf16[1,64,512]{2,1,0:T(8,128)(2,1)S(1)} %fusion.13.refs_2_, bf16[1,27,128,64]{3,2,1,0:T(8,128)(2,1)S(1)} %bitcast.156), custom_call_target="tpu_custom_call" | custom-call | flops 251658240 | bytes 65536 | tf_op jit(solution)/shard_map/pallas_call | solution.py:544
  29.8 0.5 fusion.14
  30.6 0.2 copy.23
  31.0 1.4 %copy-done.7 = bf16[2,3,8,32,512]{4,3,2,1,0:T(8,128)(2,1)S(1)} copy-done((bf16[2,3,8,32,512]{4,3,2,1,0:T(8,128)(2,1)S(1)}, bf16[2,3,8,32,512]{4,3,2,1,0:T(8,128)(2,1)}, u32[]{:S(2)}) %copy-start.7) | copy-done | bytes 1572888
  32.4 11.7 %shard_map.193 = (bf16[8,32,512]{2,1,0:T(8,128)(2,1)S(1)}, bf16[2,16,128]{2,1,0:T(8,128)(2,1)S(1)}) custom-call(s32[8,27]{1,0:T(8,128)S(1)} %pad_add_fusion.refs_0_, s32[1]{0:T(128)} %copy.52.refs_1_, bf16[2,3,8,32,512]{4,3,2,1,0:T(8,128)(2,1)S(1)} %copy-done.7, bf16[1,27,32,64]{3,2,1,0:T(8,128)(2,1)S(1)} %reverse_bitcast_fusion.1.refs_3_, ...), custom_call_target="tpu_custom_call" | custom-call | flops 503316480 | bytes 1572864 | tf_op jit(solution)/shard_map/pallas_call | solution.py:544
  44.5 0.2 convolution_convert_fusion.8
  45.3 0.3 copy.26
  45.9 14.9 %shard_map.194 = (bf16[2,2,16,128]{3,2,1,0:T(8,128)(2,1)S(1)}, bf16[2,3,8,32,512]{4,3,2,1,0:T(8,128)(2,1)S(1)}, bf16[2,128,128]{2,1,0:T(8,128)(2,1)S(1)}) custom-call(bf16[2,16,128]{2,1,0:T(8,128)(2,1)S(1)} %bitcast.162, bf16[8,32,512]{2,1,0:T(8,128)(2,1)S(1)} %fusion.6.refs_1_, bf16[128,128]{1,0:T(8,128)(2,1)S(1)} %reshape_reshape.16.refs_2_), custom_call_target="tpu_custom_call" | custom-call | tf_op jit(solution)/shard_map/pallas_call | solution.py:192
  60.9 1.2 %copy-done.4 = bf16[2,3,8,32,512]{4,3,2,1,0:T(8,128)(2,1)} copy-done((bf16[2,3,8,32,512]{4,3,2,1,0:T(8,128)(2,1)}, bf16[2,3,8,32,512]{4,3,2,1,0:T(8,128)(2,1)S(1)}, u32[]{:S(2)}) %copy-start.4) | copy-done | bytes 1572888
  62.5 0.2 fusion.12
  62.7 0.3 fusion.9
  63.3 2.3 %shard_map.196 = f32[2,32,512]{2,1,0:T(8,128)S(1)} custom-call(s32[2,27]{1,0:T(2,128)S(1)} %iota_select_fusion.refs_0_, s32[1]{0:T(128)} %copy.52.refs_1_, bf16[2,64,512]{2,1,0:T(8,128)(2,1)S(1)} %bitcast.159, bf16[2,27,32,64]{3,2,1,0:T(8,128)(2,1)S(1)} %pad_maximum_fusion.refs_3_), custom_call_target="tpu_custom_call" | custom-call | flops 125829120 | bytes 131072 | tf_op jit(solution)/shard_map/pallas_call | solution.py:544
  65.6 0.3 fusion.15
  66.1 0.2 convolution_convert_fusion.1
  66.4 1.2 %shard_map.195 = f32[3,64,640]{2,1,0:T(8,128)S(1)} custom-call(s32[1,27]{1,0:T(1,128)S(1)} %compare_select_fusion.refs_0_, s32[1]{0:T(128)} %copy.52.refs_1_, bf16[1,64,512]{2,1,0:T(8,128)(2,1)S(1)} %fusion.13.refs_2_, bf16[1,64,512]{2,1,0:T(8,128)(2,1)S(1)} %constant_dynamic-slice_fusion.1.refs_3_), custom_call_target="tpu_custom_call" | custom-call | flops 125829120 | bytes 65536 | tf_op jit(solution)/shard_map/pallas_call | solution.py:544
  67.8 1.4 %copy-done.5 = bf16[2,3,8,32,512]{4,3,2,1,0:T(8,128)(2,1)S(1)} copy-done((bf16[2,3,8,32,512]{4,3,2,1,0:T(8,128)(2,1)S(1)}, bf16[2,3,8,32,512]{4,3,2,1,0:T(8,128)(2,1)}, u32[]{:S(2)}) %copy-start.5) | copy-done | bytes 1572888
  69.2 41.7 %shard_map.197 = (bf16[8,32,512]{2,1,0:T(8,128)(2,1)S(1)}, f32[27,32,64]{2,1,0:T(8,128)S(1)}, f32[27,64,64]{2,1,0:T(8,128)S(1)}, f32[4,8,128]{2,1,0:T(8,128)S(1)}, bf16[2,16,128]{2,1,0:T(8,128)(2,1)S(1)}) custom-call(s32[8,27]{1,0:T(8,128)S(1)} %pad_add_fusion.refs_0_, s32[1]{0:T(128)} %copy.52.refs_1_, bf16[2,3,8,32,512]{4,3,2,1,0:T(8,128)(2,1)S(1)} %copy-done.5, ...), custom_call_target="tpu_custom_call" | custom-call | flops 1006632960 | bytes 1572864 | tf_op jit(solution)/shard_map/pallas_call | solution.py:544
  111.3 0.9 fusion.5
  112.2 0.7 reshape.223
  112.9 0.7 copy.53
  113.6 0.8 copy.54
  114.4 0.9 copy.55
  (88 shorter events, 4.8 us)
Async XLA Ops:
  0.6 6.0 %copy-start = (bf16[27,64,64]{2,1,0:T(8,128)(2,1)S(1)}, bf16[27,64,64]{2,1,0:T(8,128)(2,1)}, u32[]{:S(2)}) copy-start(bf16[27,64,64]{2,1,0:T(8,128)(2,1)} %refs_3_.1) | copy-start | bytes 663556
  3.0 24.9 %copy-start.13 = (s32[8]{0:T(128)}, s32[8]{0:T(128)S(1)}, u32[]{:S(2)}) copy-start(s32[8]{0:T(128)S(1)} %get-tuple-element.48) | copy-start | bytes 100
  3.8 24.2 %copy-start.8 = (bf16[8,64,512]{2,1,0:T(8,128)(2,1)S(1)}, bf16[8,64,512]{2,1,0:T(8,128)(2,1)}, u32[]{:S(2)}) copy-start(bf16[8,64,512]{2,1,0:T(8,128)(2,1)} %constant.93) | copy-start | bytes 1572868
  6.6 0.9 copy-start.1
  7.6 0.7 copy-start.3
  26.1 1.2 %copy-start.6 = (bf16[2,3,8,32,512]{4,3,2,1,0:T(8,128)(2,1)}, bf16[2,3,8,32,512]{4,3,2,1,0:T(8,128)(2,1)S(1)}, u32[]{:S(2)}) copy-start(bf16[2,3,8,32,512]{4,3,2,1,0:T(8,128)(2,1)S(1)} %get-tuple-element.21.refs_2_) | copy-start | bytes 4718596
  27.5 2.9 %copy-start.11 = (s32[10]{0:T(128)}, s32[10]{0:T(128)S(1)}, u32[]{:S(2)}) copy-start(s32[10]{0:T(128)S(1)} %pad_add_fusion.1) | copy-start | bytes 124
  30.9 13.2 %copy-start.14 = (s32[8]{0:T(128)S(1)}, s32[8]{0:T(128)}, u32[]{:S(2)}) copy-start(s32[8]{0:T(128)} %copy-done.13) | copy-start | bytes 100
  30.9 13.6 %copy-start.10 = (bf16[512,64,1]{0,1,2:T(8,128)(2,1)S(1)}, bf16[512,64,1]{0,1,2:T(8,128)(2,1)}, u32[]{:S(2)}) copy-start(bf16[512,64,1]{0,1,2:T(8,128)(2,1)} %constant.94) | copy-start | bytes 196612
  30.9 14.1 %copy-start.9 = (bf16[8,32,512]{2,1,0:T(8,128)(2,1)S(1)}, bf16[8,32,512]{2,1,0:T(8,128)(2,1)}, u32[]{:S(2)}) copy-start(bf16[8,32,512]{2,1,0:T(8,128)(2,1)} %param.16) | copy-start | bytes 786436
  31.0 1.4 %copy-start.7 = (bf16[2,3,8,32,512]{4,3,2,1,0:T(8,128)(2,1)S(1)}, bf16[2,3,8,32,512]{4,3,2,1,0:T(8,128)(2,1)}, u32[]{:S(2)}) copy-start(bf16[2,3,8,32,512]{4,3,2,1,0:T(8,128)(2,1)} %copy-done.6) | copy-start | bytes 4718596
  45.6 16.5 %copy-start.12 = (s32[10]{0:T(128)S(1)}, s32[10]{0:T(128)}, u32[]{:S(2)}) copy-start(s32[10]{0:T(128)} %copy-done.11) | copy-start | bytes 124
  60.9 1.2 %copy-start.4 = (bf16[2,3,8,32,512]{4,3,2,1,0:T(8,128)(2,1)}, bf16[2,3,8,32,512]{4,3,2,1,0:T(8,128)(2,1)S(1)}, u32[]{:S(2)}) copy-start(bf16[2,3,8,32,512]{4,3,2,1,0:T(8,128)(2,1)S(1)} %get-tuple-element.29.refs_2_) | copy-start | bytes 4718596
  63.0 4.5 %copy-start.16 = (f32[128]{0:T(128)S(1)}, f32[128]{0:T(128)}, u32[]{:S(2)}) copy-start(f32[128]{0:T(128)} %pad.4.clone) | copy-start | bytes 1540
  65.6 2.2 %copy-start.2 = (bf16[27,32,64]{2,1,0:T(8,128)(2,1)S(1)}, bf16[27,32,64]{2,1,0:T(8,128)(2,1)}, u32[]{:S(2)}) copy-start(bf16[27,32,64]{2,1,0:T(8,128)(2,1)} %refs_4_.1) | copy-start | bytes 331780
  67.8 1.4 %copy-start.5 = (bf16[2,3,8,32,512]{4,3,2,1,0:T(8,128)(2,1)S(1)}, bf16[2,3,8,32,512]{4,3,2,1,0:T(8,128)(2,1)}, u32[]{:S(2)}) copy-start(bf16[2,3,8,32,512]{4,3,2,1,0:T(8,128)(2,1)} %copy-done.4) | copy-start | bytes 4718596
  69.2 41.8 %copy-start.15 = (s32[8]{0:T(128)S(1)}, s32[8]{0:T(128)}, u32[]{:S(2)}) copy-start(s32[8]{0:T(128)} %copy-done.13) | copy-start | bytes 100

commit v8 on v7

--- a/solution.py
+++ b/solution.py
@@ -366,7 +366,14 @@
 
         if count:
             fetch.wait()
-        lax.fori_loop(0, slots, turn, 0)
+        stride = 3 if slots % 3 == 0 else 1
+
+        def turn_some(group, carry):
+            for offset in range(stride):
+                turn(group * stride + offset, carry)
+            return carry
+
+        lax.fori_loop(0, slots // stride, turn_some, 0)
         if "acc" in refs:
             refs["acc"][...] = jnp.zeros_like(refs["acc"])
 

time: 116 us -> 114 us (0.983)
  Pallas kernels: 91.1 us -> 89.6 us
    pallas_call x5, Pallas kernels: 58.4 us -> 56.9 us  [brick_pass(): pl.pallas_call(lambda *refs: brick_kernel(count, masked, scales, parts, n...]
where the time goes in v8:
time: 114 us
  Pallas kernels  89.6 us (79%)
  local copies, waits for them, and re-layouts  13.1 us (11%)
  matrix products  5.65 us (5%)
  other arithmetic  3.57 us (3%)
  between operations  1.87 us (2%)
    pallas_call x5, Pallas kernels, brick_pass(): pl.pallas_call(lambda *refs: brick_kernel(count, masked, scales, parts, n...  56.9 us
    pallas_call x2, Pallas kernels, trade(): pl.pallas_call(lambda *refs: trade_kernel(count, amount, *refs), in_specs...  32.7 us
    unnamed x43, local copies, waits for them, and re-layouts  9.28 us

profile of v8, /device:TPU:8, one launch (start us, length us, event | category | flops | bytes accessed | tf_op | source)
XLA Modules:
  0.0 113.8 jit_solution(15213059716187937912)
XLA Ops:
  1.4 0.6 pad.4.clone
  2.0 0.7 compare_select_fusion.1
  3.1 0.7 subtract_select_fusion
  4.0 1.2 %fusion.16 = bf16[8,32,64]{2,1,0:T(8,128)(2,1)S(1)} fusion(bf16[512,64,1]{0,1,2:T(8,128)(2,1)} %constant.94, bf16[8,32,512]{2,1,0:T(8,128)(2,1)} %param.16, f32[8]{0:T(128)S(1)} %compare_select_fusion.7), kind=kOutput, calls=%fused_computation.33 | convolution fusion | flops 16809984 | bytes 360480 | tf_op jit(solution)/shard_map/bcv,vu->bcu/dot_general | solution.py:45
  5.6 1.1 multiply_convert_fusion.refs_1_.refs_4_
  6.7 0.9 copy-done.1
  7.6 0.7 copy-done.3
  8.3 17.7 %shard_map.191 = (bf16[2,2,32,128]{3,2,1,0:T(8,128)(2,1)S(1)}, bf16[2,3,8,32,512]{4,3,2,1,0:T(8,128)(2,1)S(1)}, bf16[2,128,128]{2,1,0:T(8,128)(2,1)S(1)}, bf16[2...) custom-call(bf16[2,32,128]{2,1,0:T(8,128)(2,1)S(1)} %bitcast.161, ...), custom_call_target="tpu_custom_call" | custom-call | tf_op jit(solution)/shard_map/pallas_call | solution.py:192
  26.1 1.2 %copy-done.6 = bf16[2,3,8,32,512]{4,3,2,1,0:T(8,128)(2,1)} copy-done((bf16[2,3,8,32,512]{4,3,2,1,0:T(8,128)(2,1)}, bf16[2,3,8,32,512]{4,3,2,1,0:T(8,128)(2,1)S(1)}, u32[]{:S(2)}) %copy-start.6) | copy-done | bytes 1572888
  27.9 0.2 fusion.13.refs_2_
  28.2 1.5 %shard_map.192 = f32[1,128,512]{2,1,0:T(8,128)S(1)} custom-call(s32[1,27]{1,0:T(1,128)S(1)} %compare_select_fusion.refs_0_, s32[1]{0:T(128)} %copy.52.refs_1_, bf16[1,64,512]{2,1,0:T(8,128)(2,1)S(1)} %fusion.13.refs_2_, bf16[1,27,128,64]{3,2,1,0:T(8,128)(2,1)S(1)} %bitcast.156), custom_call_target="tpu_custom_call" | custom-call | flops 251658240 | bytes 65536 | tf_op jit(solution)/shard_map/pallas_call | solution.py:551
  29.8 0.5 fusion.14
  30.6 0.2 copy.23
  31.0 1.4 %copy-done.7 = bf16[2,3,8,32,512]{4,3,2,1,0:T(8,128)(2,1)S(1)} copy-done((bf16[2,3,8,32,512]{4,3,2,1,0:T(8,128)(2,1)S(1)}, bf16[2,3,8,32,512]{4,3,2,1,0:T(8,128)(2,1)}, u32[]{:S(2)}) %copy-start.7) | copy-done | bytes 1572888
  32.4 10.9 %shard_map.193 = (bf16[8,32,512]{2,1,0:T(8,128)(2,1)S(1)}, bf16[2,16,128]{2,1,0:T(8,128)(2,1)S(1)}) custom-call(s32[8,27]{1,0:T(8,128)S(1)} %pad_add_fusion.refs_0_, s32[1]{0:T(128)} %copy.52.refs_1_, bf16[2,3,8,32,512]{4,3,2,1,0:T(8,128)(2,1)S(1)} %copy-done.7, bf16[1,27,32,64]{3,2,1,0:T(8,128)(2,1)S(1)} %reverse_bitcast_fusion.1.refs_3_, ...), custom_call_target="tpu_custom_call" | custom-call | flops 503316480 | bytes 1572864 | tf_op jit(solution)/shard_map/pallas_call | solution.py:551
  43.6 0.2 convolution_convert_fusion.8
  44.5 0.3 copy.26
  45.1 14.9 %shard_map.194 = (bf16[2,2,16,128]{3,2,1,0:T(8,128)(2,1)S(1)}, bf16[2,3,8,32,512]{4,3,2,1,0:T(8,128)(2,1)S(1)}, bf16[2,128,128]{2,1,0:T(8,128)(2,1)S(1)}) custom-call(bf16[2,16,128]{2,1,0:T(8,128)(2,1)S(1)} %bitcast.162, bf16[8,32,512]{2,1,0:T(8,128)(2,1)S(1)} %fusion.6.refs_1_, bf16[128,128]{1,0:T(8,128)(2,1)S(1)} %reshape_reshape.16.refs_2_), custom_call_target="tpu_custom_call" | custom-call | tf_op jit(solution)/shard_map/pallas_call | solution.py:192
  60.1 1.2 %copy-done.4 = bf16[2,3,8,32,512]{4,3,2,1,0:T(8,128)(2,1)} copy-done((bf16[2,3,8,32,512]{4,3,2,1,0:T(8,128)(2,1)}, bf16[2,3,8,32,512]{4,3,2,1,0:T(8,128)(2,1)S(1)}, u32[]{:S(2)}) %copy-start.4) | copy-done | bytes 1572888
  61.7 0.2 fusion.12
  61.9 0.3 fusion.9
  62.5 2.3 %shard_map.196 = f32[2,32,512]{2,1,0:T(8,128)S(1)} custom-call(s32[2,27]{1,0:T(2,128)S(1)} %iota_select_fusion.refs_0_, s32[1]{0:T(128)} %copy.52.refs_1_, bf16[2,64,512]{2,1,0:T(8,128)(2,1)S(1)} %bitcast.159, bf16[2,27,32,64]{3,2,1,0:T(8,128)(2,1)S(1)} %pad_maximum_fusion.refs_3_), custom_call_target="tpu_custom_call" | custom-call | flops 125829120 | bytes 131072 | tf_op jit(solution)/shard_map/pallas_call | solution.py:551
  64.8 0.3 fusion.15
  65.3 0.2 convolution_convert_fusion.1
  65.6 1.2 %shard_map.195 = f32[3,64,640]{2,1,0:T(8,128)S(1)} custom-call(s32[1,27]{1,0:T(1,128)S(1)} %compare_select_fusion.refs_0_, s32[1]{0:T(128)} %copy.52.refs_1_, bf16[1,64,512]{2,1,0:T(8,128)(2,1)S(1)} %fusion.13.refs_2_, bf16[1,64,512]{2,1,0:T(8,128)(2,1)S(1)} %constant_dynamic-slice_fusion.1.refs_3_), custom_call_target="tpu_custom_call" | custom-call | flops 125829120 | bytes 65536 | tf_op jit(solution)/shard_map/pallas_call | solution.py:551
  67.0 1.4 %copy-done.5 = bf16[2,3,8,32,512]{4,3,2,1,0:T(8,128)(2,1)S(1)} copy-done((bf16[2,3,8,32,512]{4,3,2,1,0:T(8,128)(2,1)S(1)}, bf16[2,3,8,32,512]{4,3,2,1,0:T(8,128)(2,1)}, u32[]{:S(2)}) %copy-start.5) | copy-done | bytes 1572888
  68.4 41.1 %shard_map.197 = (bf16[8,32,512]{2,1,0:T(8,128)(2,1)S(1)}, f32[27,32,64]{2,1,0:T(8,128)S(1)}, f32[27,64,64]{2,1,0:T(8,128)S(1)}, f32[4,8,128]{2,1,0:T(8,128)S(1)}, bf16[2,16,128]{2,1,0:T(8,128)(2,1)S(1)}) custom-call(s32[8,27]{1,0:T(8,128)S(1)} %pad_add_fusion.refs_0_, s32[1]{0:T(128)} %copy.52.refs_1_, bf16[2,3,8,32,512]{4,3,2,1,0:T(8,128)(2,1)S(1)} %copy-done.5, ...), custom_call_target="tpu_custom_call" | custom-call | flops 1006632960 | bytes 1572864 | tf_op jit(solution)/shard_map/pallas_call | solution.py:551
  109.9 0.9 fusion.5
  110.8 0.7 reshape.223
  111.5 0.7 copy.53
  112.2 0.8 copy.54
  112.9 0.9 copy.55
  (88 shorter events, 4.8 us)
Async XLA Ops:
  0.6 6.0 %copy-start = (bf16[27,64,64]{2,1,0:T(8,128)(2,1)S(1)}, bf16[27,64,64]{2,1,0:T(8,128)(2,1)}, u32[]{:S(2)}) copy-start(bf16[27,64,64]{2,1,0:T(8,128)(2,1)} %refs_3_.1) | copy-start | bytes 663556
  3.0 24.9 %copy-start.13 = (s32[8]{0:T(128)}, s32[8]{0:T(128)S(1)}, u32[]{:S(2)}) copy-start(s32[8]{0:T(128)S(1)} %get-tuple-element.48) | copy-start | bytes 100
  3.8 24.2 %copy-start.8 = (bf16[8,64,512]{2,1,0:T(8,128)(2,1)S(1)}, bf16[8,64,512]{2,1,0:T(8,128)(2,1)}, u32[]{:S(2)}) copy-start(bf16[8,64,512]{2,1,0:T(8,128)(2,1)} %constant.93) | copy-start | bytes 1572868
  6.6 0.9 copy-start.1
  7.6 0.7 copy-start.3
  26.1 1.2 %copy-start.6 = (bf16[2,3,8,32,512]{4,3,2,1,0:T(8,128)(2,1)}, bf16[2,3,8,32,512]{4,3,2,1,0:T(8,128)(2,1)S(1)}, u32[]{:S(2)}) copy-start(bf16[2,3,8,32,512]{4,3,2,1,0:T(8,128)(2,1)S(1)} %get-tuple-element.21.refs_2_) | copy-start | bytes 4718596
  27.5 2.9 %copy-start.11 = (s32[10]{0:T(128)}, s32[10]{0:T(128)S(1)}, u32[]{:S(2)}) copy-start(s32[10]{0:T(128)S(1)} %pad_add_fusion.1) | copy-start | bytes 124
  30.9 12.4 %copy-start.14 = (s32[8]{0:T(128)S(1)}, s32[8]{0:T(128)}, u32[]{:S(2)}) copy-start(s32[8]{0:T(128)} %copy-done.13) | copy-start | bytes 100
  30.9 12.7 %copy-start.10 = (bf16[512,64,1]{0,1,2:T(8,128)(2,1)S(1)}, bf16[512,64,1]{0,1,2:T(8,128)(2,1)}, u32[]{:S(2)}) copy-start(bf16[512,64,1]{0,1,2:T(8,128)(2,1)} %constant.94) | copy-start | bytes 196612
  30.9 13.3 %copy-start.9 = (bf16[8,32,512]{2,1,0:T(8,128)(2,1)S(1)}, bf16[8,32,512]{2,1,0:T(8,128)(2,1)}, u32[]{:S(2)}) copy-start(bf16[8,32,512]{2,1,0:T(8,128)(2,1)} %param.16) | copy-start | bytes 786436
  31.0 1.4 %copy-start.7 = (bf16[2,3,8,32,512]{4,3,2,1,0:T(8,128)(2,1)S(1)}, bf16[2,3,8,32,512]{4,3,2,1,0:T(8,128)(2,1)}, u32[]{:S(2)}) copy-start(bf16[2,3,8,32,512]{4,3,2,1,0:T(8,128)(2,1)} %copy-done.6) | copy-start | bytes 4718596
  44.8 16.5 %copy-start.12 = (s32[10]{0:T(128)S(1)}, s32[10]{0:T(128)}, u32[]{:S(2)}) copy-start(s32[10]{0:T(128)} %copy-done.11) | copy-start | bytes 124
  60.1 1.2 %copy-start.4 = (bf16[2,3,8,32,512]{4,3,2,1,0:T(8,128)(2,1)}, bf16[2,3,8,32,512]{4,3,2,1,0:T(8,128)(2,1)S(1)}, u32[]{:S(2)}) copy-start(bf16[2,3,8,32,512]{4,3,2,1,0:T(8,128)(2,1)S(1)} %get-tuple-element.29.refs_2_) | copy-start | bytes 4718596
  62.2 4.5 %copy-start.16 = (f32[128]{0:T(128)S(1)}, f32[128]{0:T(128)}, u32[]{:S(2)}) copy-start(f32[128]{0:T(128)} %pad.4.clone) | copy-start | bytes 1540
  64.8 2.2 %copy-start.2 = (bf16[27,32,64]{2,1,0:T(8,128)(2,1)S(1)}, bf16[27,32,64]{2,1,0:T(8,128)(2,1)}, u32[]{:S(2)}) copy-start(bf16[27,32,64]{2,1,0:T(8,128)(2,1)} %refs_4_.1) | copy-start | bytes 331780
  67.0 1.4 %copy-start.5 = (bf16[2,3,8,32,512]{4,3,2,1,0:T(8,128)(2,1)S(1)}, bf16[2,3,8,32,512]{4,3,2,1,0:T(8,128)(2,1)}, u32[]{:S(2)}) copy-start(bf16[2,3,8,32,512]{4,3,2,1,0:T(8,128)(2,1)} %copy-done.4) | copy-start | bytes 4718596
  68.4 41.1 %copy-start.15 = (s32[8]{0:T(128)S(1)}, s32[8]{0:T(128)}, u32[]{:S(2)}) copy-start(s32[8]{0:T(128)} %copy-done.13) | copy-start | bytes 100
